TPU v7x, 32 devices: a whole 2x2x4 slice. The times are simulated.
32 devices in a mesh: gx: 8 (over y, x, core), gy: 4 (over z).
Axes of the slice: x: 2, y: 2, z: 4, core: 2. Of those that a mesh axis runs over, the one named last changes fastest.
Arguments:
- density: float32 [2, 32, 512], P(None, 'gx', 'gy'), may hold values from 0 to 1
- e_field: float32 [3, 32, 32, 512], P(None, 'gx', None, 'gy'), may hold values from -6 to 6
- h_field: float32 [3, 32, 32, 512], P(None, 'gx', None, 'gy'), may hold values from -6 to 6
- adj_e: float32 [3, 32, 32, 512], P(None, 'gx', None, 'gy'), may hold values from -6 to 6
- adj_h: float32 [3, 32, 32, 512], P(None, 'gx', None, 'gy'), may hold values from -6 to 6
- region: int32 [32, 512], P('gx', 'gy'), may hold values from 0 to 3
Outputs:
- density_grad: float32 [2, 32, 512], P(None, 'gx', 'gy')
- adj_e0: float32 [3, 32, 32, 512], P(None, 'gx', None, 'gy')
- adj_h0: float32 [3, 32, 32, 512], P(None, 'gx', None, 'gy')
Inputs may be any that keep to these rules, and one draw needn't show every extreme that they name: `region`: 0 open, 1 absorbing, 2 design, 3 source.
All inputs are finite; a program needn't handle non-finite values.
Results may differ from a plain program's by a relative error of at most 0.00002.
Values sent between devices are 32-bit elements; how exact they have to be, the bound alone decides.
No kernel may reach another device: no remote copies, remote signals or barrier semaphores. Data moves between devices by JAX's collectives and lax.ppermute only.
A program may use at most 64 MiB of HBM per device.

v0:
```python
import math

import jax
import jax.numpy as jnp
import numpy as np
from jax import lax
from jax.sharding import PartitionSpec as P

RAD = 2


COURANT = 0.5
SHARP = 4.0
LEVEL = 0.5
CONTRAST = 5.0
ABSORB = 0.3
OMEGA = 0.7


def from_behind(block, axis, distance):
    devices = range(lax.axis_size(axis))
    route = [(i - distance, i) for i in devices if i - distance in devices]
    return lax.ppermute(block, axis, route)


def with_halo(array, sides, width):
    for axis, dim in sides:
        count, length = (lax.axis_size(axis), array.shape[dim])
        up = [(i, (i + 1) % count) for i in range(count - 1)]
        down = [(j, i) for i, j in up]
        last = lax.slice_in_dim(array, length - width, length, axis=dim)
        first = lax.slice_in_dim(array, 0, width, axis=dim)
        before = lax.ppermute(last, axis, up)
        after = lax.ppermute(first, axis, down)
        array = jnp.concatenate([before, array, after], axis=dim)
    return array


def kernel_table(radius):
    offsets = np.arange(-radius, radius + 1)
    distance = np.sqrt(offsets[:, None] ** 2 + offsets[None, :] ** 2)
    table = np.maximum(0.0, radius + 1.0 - distance)
    return table / table.sum()


def conic_blur(padded, width_x, width_y, radius):
    table = kernel_table(radius)
    total = jnp.zeros((padded.shape[0], width_x, width_y), jnp.float32)
    for row_off in range(2 * radius + 1):
        for col_off in range(2 * radius + 1):
            total = (
                total
                + float(table[row_off, col_off])
                * padded[:, row_off : row_off + width_x, col_off : col_off + width_y]
            )
    return total


def coefficients(projected, region, slab_depth):
    depth_pos = jnp.arange(slab_depth).astype(jnp.float32)
    margin = float(slab_depth // 8)
    centre = slab_depth // 2
    ramp_z = jnp.maximum(
        jnp.maximum(
            (margin - depth_pos) / margin, (depth_pos - (slab_depth - 1 - margin)) / margin
        ),
        0.0,
    )
    design = (region == 2).astype(jnp.float32)
    absorbing = (region == 1).astype(jnp.float32)
    layer_zero = (jnp.arange(slab_depth) == centre).astype(jnp.float32)
    layer_one = (jnp.arange(slab_depth) == centre + 1).astype(jnp.float32)
    permit = 1.0 + CONTRAST * design[:, None, :] * (
        projected[0][:, None, :] * layer_zero[None, :, None]
        + projected[1][:, None, :] * layer_one[None, :, None]
    )
    damping = ABSORB * absorbing[:, None, :] + ABSORB * (ramp_z * ramp_z)[None, :, None]
    keep_e = (1.0 - damping) / (1.0 + damping)
    gain_e = COURANT / (permit * (1.0 + damping))
    return (keep_e, gain_e, permit)


def source(region, slab_depth, step):
    columns = (region == 3).astype(jnp.float32)
    source_plane = (jnp.arange(slab_depth) == slab_depth // 2 - 1).astype(jnp.float32)
    along_z = math.sin(OMEGA * (step + 1)) * columns[:, None, :] * source_plane[None, :, None]
    return jnp.stack([jnp.zeros_like(along_z), jnp.zeros_like(along_z), along_z])


def face_next(values, face, along):
    count = values.shape[along]
    extended = jnp.concatenate([lax.slice_in_dim(values, 1, count, axis=along), face], along)
    return extended - values


def face_prev(values, face, along):
    count = values.shape[along]
    extended = jnp.concatenate([face, lax.slice_in_dim(values, 0, count - 1, axis=along)], along)
    return values - extended


def curl_up(fields):
    next_rows = from_behind(fields[:, 1:3, :1], "gx", -1)
    side_rows = from_behind(fields[:, 0::2, :, :, :1], "gy", -1)
    zero_face = jnp.zeros_like(fields[:, 0, :, :1])
    part_x, part_y, part_z = (fields[:, 0], fields[:, 1], fields[:, 2])
    return jnp.stack(
        [
            face_next(part_z, side_rows[:, 1], 3) - face_next(part_y, zero_face, 2),
            face_next(part_x, zero_face, 2) - face_next(part_z, next_rows[:, 1], 1),
            face_next(part_y, next_rows[:, 0], 1) - face_next(part_x, side_rows[:, 0], 3),
        ],
        axis=1,
    )


def curl_down(fields):
    next_rows = from_behind(fields[:, 1:3, -1:], "gx", 1)
    side_rows = from_behind(fields[:, 0::2, :, :, -1:], "gy", 1)
    zero_face = jnp.zeros_like(fields[:, 0, :, :1])
    part_x, part_y, part_z = (fields[:, 0], fields[:, 1], fields[:, 2])
    return jnp.stack(
        [
            face_prev(part_z, side_rows[:, 1], 3) - face_prev(part_y, zero_face, 2),
            face_prev(part_x, zero_face, 2) - face_prev(part_z, next_rows[:, 1], 1),
            face_prev(part_y, next_rows[:, 0], 1) - face_prev(part_x, side_rows[:, 0], 3),
        ],
        axis=1,
    )


def smooth(values):
    padded = with_halo(values, (("gx", 1), ("gy", 2)), RAD)
    return conic_blur(padded, values.shape[1], values.shape[2], RAD)


def per_device(density, e_field, h_field, adj_e, adj_h, region):
    slab_depth = e_field.shape[2]
    filtered = smooth(density)
    crest = math.tanh(SHARP * LEVEL)
    scale_total = crest + math.tanh(SHARP * (1.0 - LEVEL))
    inner = jnp.tanh(SHARP * (filtered - LEVEL))
    projected = (crest + inner) / scale_total
    slope_proj = SHARP * (1.0 - inner * inner) / scale_total
    keep_e, gain_e, permit = coefficients(projected, region, slab_depth)
    source_one = source(region, slab_depth, 0)
    source_two = source(region, slab_depth, 1)
    e_zero = e_field[None]
    h_zero = h_field[None]
    back_e2 = adj_e[None]
    h_one = h_zero - COURANT * curl_up(e_zero)
    drive_one = curl_down(h_one) - source_one
    e_one = keep_e * e_zero + gain_e * drive_one
    h_two = h_one - COURANT * curl_up(e_one)
    drive_two = curl_down(h_two) - source_two
    back_h2 = adj_h[None] + curl_up(gain_e * back_e2)
    back_e1 = keep_e * back_e2 - COURANT * curl_down(back_h2)
    back_h1 = back_h2 + curl_up(gain_e * back_e1)
    back_e0 = keep_e * back_e1 - COURANT * curl_down(back_h1)
    sensitivity = -jnp.sum(back_e2 * drive_two + back_e1 * drive_one, axis=(0, 1)) * gain_e / permit
    centre = slab_depth // 2
    layers = jnp.moveaxis(sensitivity[:, centre : centre + 2, :], 1, 0)
    design = (region == 2).astype(jnp.float32)
    grad_filtered = CONTRAST * design[None] * layers * slope_proj
    density_grad = smooth(grad_filtered)
    return (density_grad, back_e0[0], h_zero[0] * 0.0 + back_h1[0])


def solution(mesh):
    return jax.shard_map(
        per_device,
        mesh=mesh,
        in_specs=(
            P(None, "gx", "gy"),
            P(None, "gx", None, "gy"),
            P(None, "gx", None, "gy"),
            P(None, "gx", None, "gy"),
            P(None, "gx", None, "gy"),
            P("gx", "gy"),
        ),
        out_specs=(P(None, "gx", "gy"), P(None, "gx", None, "gy"), P(None, "gx", None, "gy")),
        check_vma=False,
    )
```

profile of v0, /device:TPU:4, one launch (start us, length us, event | category | flops | bytes accessed | tf_op | source)
XLA Modules:
  0.0 100.2 jit_solution(8008946781131058952)
XLA Ops:
  3.3 4.5 %collective-permute-start.3 = (f32[2,2,128]{2,0,1:T(2,128)S(1)}, f32[2,2,128]{2,0,1:T(2,128)S(1)}, u32[]{:S(2)}, u32[]{:S(2)}) collective-permute-start(f32[2,2,128]{2,0,1:T(2,128)S(1)} %copy.49), channel_id=1, source_target_pairs={{4,0},{8,4},{12,8},{16,12},{20,16},{24,20},{28,24},{5,1},{9,5},{13... | collective-permute-start | bytes 6152 | tf_op jit(solution)/shard_map/ppermute | solution.py:34
  10.1 1.9 %collective-permute-start.1 = (f32[1,2,1,32,128]{4,3,2,1,0:T(8,128)S(1)}, f32[1,2,1,32,128]{4,3,2,1,0:T(8,128)S(1)}, u32[]{:S(2)}, u32[]{:S(2)}) collective-permute-start(f32[1,2,1,32,128]{4,3,2,1,0:T(8,128)S(1)} %slice.772), channel_id=1, source_target_pairs={{4,0},{8,4},{12,8},{16,12},{20,16},{24,20},{28,24},{5,1},{9,5},{13... | collective-permute-start | bytes 98312 | tf_op jit(solution)/shard_map/ppermute | solution.py:23
  15.1 5.2 %collective-permute-start.4 = (f32[2,8,2]{2,0,1:T(2,128)S(1)}, f32[2,8,2]{2,0,1:T(2,128)S(1)}, u32[]{:S(2)}, u32[]{:S(2)}) collective-permute-start(f32[2,8,2]{2,0,1:T(2,128)S(1)} %get-tuple-element.99), channel_id=1, source_target_pairs={{0,1},{1,2},{2,3},{4,5},{5,6},{6,7},{8,9},{9,10},{10,11},{12,13},{... | collective-permute-start | bytes 392 | tf_op jit(solution)/shard_map/ppermute | solution.py:33
  23.5 1.9 %collective-permute-start.13 = (f32[1,2,1,32,128]{4,3,2,1,0:T(8,128)S(1)}, f32[1,2,1,32,128]{4,3,2,1,0:T(8,128)S(1)}, u32[]{:S(2)}, u32[]{:S(2)}) collective-permute-start(f32[1,2,1,32,128]{4,3,2,1,0:T(8,128)S(1)} %slice.874), channel_id=1, source_target_pairs={{4,0},{8,4},{12,8},{16,12},{20,16},{24,20},{28,24},{5,1},{9,5},{13... | collective-permute-start | bytes 98312 | tf_op jit(solution)/shard_map/ppermute | solution.py:23
  25.4 3.8 %collective-permute-done.12 = f32[1,2,4,32,1]{4,3,2,1,0:T(8,128)S(1)} collective-permute-done((f32[1,2,4,32,1]{4,3,2,1,0:T(8,128)S(1)}, f32[1,2,4,32,1]{4,3,2,1,0:T(8,128)S(1)}, u32[]{:S(2)}, u32[]{:S(2)}) %collective-permute-start.12) | collective-permute-done | bytes 1056 | tf_op jit(solution)/shard_map/ppermute | solution.py:23
  30.9 3.9 %collective-permute-start.14 = (f32[1,2,4,32,1]{4,3,2,1,0:T(8,128)S(1)}, f32[1,2,4,32,1]{4,3,2,1,0:T(8,128)S(1)}, u32[]{:S(2)}, u32[]{:S(2)}) collective-permute-start(f32[1,2,4,32,1]{4,3,2,1,0:T(8,128)S(1)} %slice.691), channel_id=1, source_target_pairs={{0,1},{1,2},{2,3},{4,5},{5,6},{6,7},{8,9},{9,10},{10,11},{12,13},{... | collective-permute-start | bytes 3080 | tf_op jit(solution)/shard_map/ppermute | solution.py:23
  34.7 1.9 %collective-permute-start.15 = (f32[1,2,1,32,128]{4,3,2,1,0:T(8,128)S(1)}, f32[1,2,1,32,128]{4,3,2,1,0:T(8,128)S(1)}, u32[]{:S(2)}, u32[]{:S(2)}) collective-permute-start(f32[1,2,1,32,128]{4,3,2,1,0:T(8,128)S(1)} %slice.887), channel_id=1, source_target_pairs={{0,4},{4,8},{8,12},{12,16},{16,20},{20,24},{24,28},{1,5},{5,9},{9,... | collective-permute-start | bytes 98312 | tf_op jit(solution)/shard_map/ppermute | solution.py:23
  37.4 3.5 %collective-permute-done.15 = f32[1,2,1,32,128]{4,3,2,1,0:T(8,128)S(1)} collective-permute-done((f32[1,2,1,32,128]{4,3,2,1,0:T(8,128)S(1)}, f32[1,2,1,32,128]{4,3,2,1,0:T(8,128)S(1)}, u32[]{:S(2)}, u32[]{:S(2)}) %collective-permute-start.15) | collective-permute-done | bytes 32800 | tf_op jit(solution)/shard_map/ppermute | solution.py:23
  42.6 1.9 %collective-permute-start.21 = (f32[1,2,1,32,128]{4,3,2,1,0:T(8,128)S(1)}, f32[1,2,1,32,128]{4,3,2,1,0:T(8,128)S(1)}, u32[]{:S(2)}, u32[]{:S(2)}) collective-permute-start(f32[1,2,1,32,128]{4,3,2,1,0:T(8,128)S(1)} %slice.933), channel_id=1, source_target_pairs={{4,0},{8,4},{12,8},{16,12},{20,16},{24,20},{28,24},{5,1},{9,5},{13... | collective-permute-start | bytes 98312 | tf_op jit(solution)/shard_map/ppermute | solution.py:23
  44.5 3.5 %collective-permute-done.20 = f32[1,2,4,32,1]{4,3,2,1,0:T(8,128)S(1)} collective-permute-done((f32[1,2,4,32,1]{4,3,2,1,0:T(8,128)S(1)}, f32[1,2,4,32,1]{4,3,2,1,0:T(8,128)S(1)}, u32[]{:S(2)}, u32[]{:S(2)}) %collective-permute-start.20) | collective-permute-done | bytes 1056 | tf_op jit(solution)/shard_map/ppermute | solution.py:23
  50.2 3.9 %collective-permute-start.22 = (f32[1,2,4,32,1]{4,3,2,1,0:T(8,128)S(1)}, f32[1,2,4,32,1]{4,3,2,1,0:T(8,128)S(1)}, u32[]{:S(2)}, u32[]{:S(2)}) collective-permute-start(f32[1,2,4,32,1]{4,3,2,1,0:T(8,128)S(1)} %slice.750), channel_id=1, source_target_pairs={{0,1},{1,2},{2,3},{4,5},{5,6},{6,7},{8,9},{9,10},{10,11},{12,13},{... | collective-permute-start | bytes 3080 | tf_op jit(solution)/shard_map/ppermute | solution.py:23
  54.2 1.9 %collective-permute-start.23 = (f32[1,2,1,32,128]{4,3,2,1,0:T(8,128)S(1)}, f32[1,2,1,32,128]{4,3,2,1,0:T(8,128)S(1)}, u32[]{:S(2)}, u32[]{:S(2)}) collective-permute-start(f32[1,2,1,32,128]{4,3,2,1,0:T(8,128)S(1)} %slice.946), channel_id=1, source_target_pairs={{0,4},{4,8},{8,12},{12,16},{16,20},{20,24},{24,28},{1,5},{5,9},{9,... | collective-permute-start | bytes 98312 | tf_op jit(solution)/shard_map/ppermute | solution.py:23
  56.1 2.6 %collective-permute-start.6 = (f32[1,2,4,32,1]{4,3,2,1,0:T(8,128)S(1)}, f32[1,2,4,32,1]{4,3,2,1,0:T(8,128)S(1)}, u32[]{:S(2)}, u32[]{:S(2)}) collective-permute-start(f32[1,2,4,32,1]{4,3,2,1,0:T(8,128)S(1)} %slice.631), channel_id=1, source_target_pairs={{0,1},{1,2},{2,3},{4,5},{5,6},{6,7},{8,9},{9,10},{10,11},{12,13},{... | collective-permute-start | bytes 3080 | tf_op jit(solution)/shard_map/ppermute | solution.py:23
  58.7 1.9 %collective-permute-start.7 = (f32[1,2,1,32,128]{4,3,2,1,0:T(8,128)S(1)}, f32[1,2,1,32,128]{4,3,2,1,0:T(8,128)S(1)}, u32[]{:S(2)}, u32[]{:S(2)}) collective-permute-start(f32[1,2,1,32,128]{4,3,2,1,0:T(8,128)S(1)} %slice.831), channel_id=1, source_target_pairs={{0,4},{4,8},{8,12},{12,16},{16,20},{20,24},{24,28},{1,5},{5,9},{9,... | collective-permute-start | bytes 98312 | tf_op jit(solution)/shard_map/ppermute | solution.py:23
  61.4 3.5 %collective-permute-done.7 = f32[1,2,1,32,128]{4,3,2,1,0:T(8,128)S(1)} collective-permute-done((f32[1,2,1,32,128]{4,3,2,1,0:T(8,128)S(1)}, f32[1,2,1,32,128]{4,3,2,1,0:T(8,128)S(1)}, u32[]{:S(2)}, u32[]{:S(2)}) %collective-permute-start.7) | collective-permute-done | bytes 32800 | tf_op jit(solution)/shard_map/ppermute | solution.py:23
  66.8 1.9 %collective-permute-start.9 = (f32[1,2,1,32,128]{4,3,2,1,0:T(8,128)S(1)}, f32[1,2,1,32,128]{4,3,2,1,0:T(8,128)S(1)}, u32[]{:S(2)}, u32[]{:S(2)}) collective-permute-start(f32[1,2,1,32,128]{4,3,2,1,0:T(8,128)S(1)} %slice.846), channel_id=1, source_target_pairs={{4,0},{8,4},{12,8},{16,12},{20,16},{24,20},{28,24},{5,1},{9,5},{13... | collective-permute-start | bytes 98312 | tf_op jit(solution)/shard_map/ppermute | solution.py:23
  68.8 3.4 %collective-permute-done.8 = f32[1,2,4,32,1]{4,3,2,1,0:T(8,128)S(1)} collective-permute-done((f32[1,2,4,32,1]{4,3,2,1,0:T(8,128)S(1)}, f32[1,2,4,32,1]{4,3,2,1,0:T(8,128)S(1)}, u32[]{:S(2)}, u32[]{:S(2)}) %collective-permute-start.8) | collective-permute-done | bytes 1056 | tf_op jit(solution)/shard_map/ppermute | solution.py:23
  72.6 2.7 %collective-permute-start.10 = (f32[1,2,4,32,1]{4,3,2,1,0:T(8,128)S(1)}, f32[1,2,4,32,1]{4,3,2,1,0:T(8,128)S(1)}, u32[]{:S(2)}, u32[]{:S(2)}) collective-permute-start(f32[1,2,4,32,1]{4,3,2,1,0:T(8,128)S(1)} %slice.661), channel_id=1, source_target_pairs={{0,1},{1,2},{2,3},{4,5},{5,6},{6,7},{8,9},{9,10},{10,11},{12,13},{... | collective-permute-start | bytes 3080 | tf_op jit(solution)/shard_map/ppermute | solution.py:23
  75.4 1.9 %collective-permute-start.11 = (f32[1,2,1,32,128]{4,3,2,1,0:T(8,128)S(1)}, f32[1,2,1,32,128]{4,3,2,1,0:T(8,128)S(1)}, u32[]{:S(2)}, u32[]{:S(2)}) collective-permute-start(f32[1,2,1,32,128]{4,3,2,1,0:T(8,128)S(1)} %slice.859), channel_id=1, source_target_pairs={{0,4},{4,8},{8,12},{12,16},{16,20},{20,24},{24,28},{1,5},{5,9},{9,... | collective-permute-start | bytes 98312 | tf_op jit(solution)/shard_map/ppermute | solution.py:23
  78.0 3.5 %collective-permute-done.11 = f32[1,2,1,32,128]{4,3,2,1,0:T(8,128)S(1)} collective-permute-done((f32[1,2,1,32,128]{4,3,2,1,0:T(8,128)S(1)}, f32[1,2,1,32,128]{4,3,2,1,0:T(8,128)S(1)}, u32[]{:S(2)}, u32[]{:S(2)}) %collective-permute-start.11) | collective-permute-done | bytes 32800 | tf_op jit(solution)/shard_map/ppermute | solution.py:23
  84.5 2.4 %collective-permute-start.16 = (f32[2,2,128]{2,0,1:T(2,128)S(1)}, f32[2,2,128]{2,0,1:T(2,128)S(1)}, u32[]{:S(2)}, u32[]{:S(2)}) collective-permute-start(f32[2,2,128]{2,0,1:T(2,128)S(1)} %get-tuple-element.103), channel_id=1, source_target_pairs={{0,4},{4,8},{8,12},{12,16},{16,20},{20,24},{24,28},{1,5},{5,9},{9,... | collective-permute-start | bytes 6152 | tf_op jit(solution)/shard_map/ppermute | solution.py:33
  86.9 3.4 %collective-permute-done.16 = f32[2,2,128]{2,0,1:T(2,128)S(1)} collective-permute-done((f32[2,2,128]{2,0,1:T(2,128)S(1)}, f32[2,2,128]{2,0,1:T(2,128)S(1)}, u32[]{:S(2)}, u32[]{:S(2)}) %collective-permute-start.16) | collective-permute-done | bytes 2080 | tf_op jit(solution)/shard_map/ppermute | solution.py:33
  90.4 3.4 %collective-permute-start.18 = (f32[2,8,2]{2,0,1:T(2,128)S(1)}, f32[2,8,2]{2,0,1:T(2,128)S(1)}, u32[]{:S(2)}, u32[]{:S(2)}) collective-permute-start(f32[2,8,2]{2,0,1:T(2,128)S(1)} %get-tuple-element.97), channel_id=1, source_target_pairs={{0,1},{1,2},{2,3},{4,5},{5,6},{6,7},{8,9},{9,10},{10,11},{12,13},{... | collective-permute-start | bytes 392 | tf_op jit(solution)/shard_map/ppermute | solution.py:33
  95.2 4.2 %collective-permute-done.19 = f32[2,8,2]{2,0,1:T(2,128)S(1)} collective-permute-done((f32[2,8,2]{2,0,1:T(2,128)S(1)}, f32[2,8,2]{2,0,1:T(2,128)S(1)}, u32[]{:S(2)}, u32[]{:S(2)}) %collective-permute-start.19) | collective-permute-done | bytes 160 | tf_op jit(solution)/shard_map/ppermute | solution.py:34
  (158 shorter events, 25.8 us)
Async XLA Ops:
  1.4 11.6 %collective-permute-start.2 = (f32[2,2,128]{2,0,1:T(2,128)S(1)}, f32[2,2,128]{2,0,1:T(2,128)S(1)}, u32[]{:S(2)}, u32[]{:S(2)}) collective-permute-start(f32[2,2,128]{2,0,1:T(2,128)S(1)} %copy.48), channel_id=1, source_target_pairs={{0,4},{4,8},{8,12},{12,16},{16,20},{20,24},{24,28},{1,5},{5,9},{9,... | collective-permute-start | bytes 6152 | tf_op jit(solution)/shard_map/ppermute | solution.py:33
  3.3 10.4 %collective-permute-start.3 = (f32[2,2,128]{2,0,1:T(2,128)S(1)}, f32[2,2,128]{2,0,1:T(2,128)S(1)}, u32[]{:S(2)}, u32[]{:S(2)}) collective-permute-start(f32[2,2,128]{2,0,1:T(2,128)S(1)} %copy.49), channel_id=1, source_target_pairs={{4,0},{8,4},{12,8},{16,12},{20,16},{24,20},{28,24},{5,1},{9,5},{13... | collective-permute-start | bytes 6152 | tf_op jit(solution)/shard_map/ppermute | solution.py:34
  8.8 11.5 %collective-permute-start = (f32[1,2,4,32,1]{4,3,2,1,0:T(8,128)S(1)}, f32[1,2,4,32,1]{4,3,2,1,0:T(8,128)S(1)}, u32[]{:S(2)}, u32[]{:S(2)}) collective-permute-start(f32[1,2,4,32,1]{4,3,2,1,0:T(8,128)S(1)} %slice.587), channel_id=1, source_target_pairs={{1,0},{2,1},{3,2},{5,4},{6,5},{7,6},{9,8},{10,9},{11,10},{13,12},{... | collective-permute-start | bytes 3080 | tf_op jit(solution)/shard_map/ppermute | solution.py:23
  10.1 19.1 %collective-permute-start.1 = (f32[1,2,1,32,128]{4,3,2,1,0:T(8,128)S(1)}, f32[1,2,1,32,128]{4,3,2,1,0:T(8,128)S(1)}, u32[]{:S(2)}, u32[]{:S(2)}) collective-permute-start(f32[1,2,1,32,128]{4,3,2,1,0:T(8,128)S(1)} %slice.772), channel_id=1, source_target_pairs={{4,0},{8,4},{12,8},{16,12},{20,16},{24,20},{28,24},{5,1},{9,5},{13... | collective-permute-start | bytes 98312 | tf_op jit(solution)/shard_map/ppermute | solution.py:23
  13.8 6.5 %collective-permute-start.5 = (f32[2,8,2]{2,0,1:T(2,128)S(1)}, f32[2,8,2]{2,0,1:T(2,128)S(1)}, u32[]{:S(2)}, u32[]{:S(2)}) collective-permute-start(f32[2,8,2]{2,0,1:T(2,128)S(1)} %get-tuple-element.100), channel_id=1, source_target_pairs={{1,0},{2,1},{3,2},{5,4},{6,5},{7,6},{9,8},{10,9},{11,10},{13,12},{... | collective-permute-start | bytes 392 | tf_op jit(solution)/shard_map/ppermute | solution.py:34
  15.1 6.5 %collective-permute-start.4 = (f32[2,8,2]{2,0,1:T(2,128)S(1)}, f32[2,8,2]{2,0,1:T(2,128)S(1)}, u32[]{:S(2)}, u32[]{:S(2)}) collective-permute-start(f32[2,8,2]{2,0,1:T(2,128)S(1)} %get-tuple-element.99), channel_id=1, source_target_pairs={{0,1},{1,2},{2,3},{4,5},{5,6},{6,7},{8,9},{9,10},{10,11},{12,13},{... | collective-permute-start | bytes 392 | tf_op jit(solution)/shard_map/ppermute | solution.py:33
  22.0 7.2 %collective-permute-start.12 = (f32[1,2,4,32,1]{4,3,2,1,0:T(8,128)S(1)}, f32[1,2,4,32,1]{4,3,2,1,0:T(8,128)S(1)}, u32[]{:S(2)}, u32[]{:S(2)}) collective-permute-start(f32[1,2,4,32,1]{4,3,2,1,0:T(8,128)S(1)} %slice.677), channel_id=1, source_target_pairs={{1,0},{2,1},{3,2},{5,4},{6,5},{7,6},{9,8},{10,9},{11,10},{13,12},{... | collective-permute-start | bytes 3080 | tf_op jit(solution)/shard_map/ppermute | solution.py:23
  23.5 6.1 %collective-permute-start.13 = (f32[1,2,1,32,128]{4,3,2,1,0:T(8,128)S(1)}, f32[1,2,1,32,128]{4,3,2,1,0:T(8,128)S(1)}, u32[]{:S(2)}, u32[]{:S(2)}) collective-permute-start(f32[1,2,1,32,128]{4,3,2,1,0:T(8,128)S(1)} %slice.874), channel_id=1, source_target_pairs={{4,0},{8,4},{12,8},{16,12},{20,16},{24,20},{28,24},{5,1},{9,5},{13... | collective-permute-start | bytes 98312 | tf_op jit(solution)/shard_map/ppermute | solution.py:23
  30.9 6.5 %collective-permute-start.14 = (f32[1,2,4,32,1]{4,3,2,1,0:T(8,128)S(1)}, f32[1,2,4,32,1]{4,3,2,1,0:T(8,128)S(1)}, u32[]{:S(2)}, u32[]{:S(2)}) collective-permute-start(f32[1,2,4,32,1]{4,3,2,1,0:T(8,128)S(1)} %slice.691), channel_id=1, source_target_pairs={{0,1},{1,2},{2,3},{4,5},{5,6},{6,7},{8,9},{9,10},{10,11},{12,13},{... | collective-permute-start | bytes 3080 | tf_op jit(solution)/shard_map/ppermute | solution.py:23
  34.7 6.1 %collective-permute-start.15 = (f32[1,2,1,32,128]{4,3,2,1,0:T(8,128)S(1)}, f32[1,2,1,32,128]{4,3,2,1,0:T(8,128)S(1)}, u32[]{:S(2)}, u32[]{:S(2)}) collective-permute-start(f32[1,2,1,32,128]{4,3,2,1,0:T(8,128)S(1)} %slice.887), channel_id=1, source_target_pairs={{0,4},{4,8},{8,12},{12,16},{16,20},{20,24},{24,28},{1,5},{5,9},{9,... | collective-permute-start | bytes 98312 | tf_op jit(solution)/shard_map/ppermute | solution.py:23
  41.2 6.9 %collective-permute-start.20 = (f32[1,2,4,32,1]{4,3,2,1,0:T(8,128)S(1)}, f32[1,2,4,32,1]{4,3,2,1,0:T(8,128)S(1)}, u32[]{:S(2)}, u32[]{:S(2)}) collective-permute-start(f32[1,2,4,32,1]{4,3,2,1,0:T(8,128)S(1)} %slice.736), channel_id=1, source_target_pairs={{1,0},{2,1},{3,2},{5,4},{6,5},{7,6},{9,8},{10,9},{11,10},{13,12},{... | collective-permute-start | bytes 3080 | tf_op jit(solution)/shard_map/ppermute | solution.py:23
  42.6 5.4 %collective-permute-start.21 = (f32[1,2,1,32,128]{4,3,2,1,0:T(8,128)S(1)}, f32[1,2,1,32,128]{4,3,2,1,0:T(8,128)S(1)}, u32[]{:S(2)}, u32[]{:S(2)}) collective-permute-start(f32[1,2,1,32,128]{4,3,2,1,0:T(8,128)S(1)} %slice.933), channel_id=1, source_target_pairs={{4,0},{8,4},{12,8},{16,12},{20,16},{24,20},{28,24},{5,1},{9,5},{13... | collective-permute-start | bytes 98312 | tf_op jit(solution)/shard_map/ppermute | solution.py:23
  50.2 10.4 %collective-permute-start.22 = (f32[1,2,4,32,1]{4,3,2,1,0:T(8,128)S(1)}, f32[1,2,4,32,1]{4,3,2,1,0:T(8,128)S(1)}, u32[]{:S(2)}, u32[]{:S(2)}) collective-permute-start(f32[1,2,4,32,1]{4,3,2,1,0:T(8,128)S(1)} %slice.750), channel_id=1, source_target_pairs={{0,1},{1,2},{2,3},{4,5},{5,6},{6,7},{8,9},{9,10},{10,11},{12,13},{... | collective-permute-start | bytes 3080 | tf_op jit(solution)/shard_map/ppermute | solution.py:23
  54.2 11.0 %collective-permute-start.23 = (f32[1,2,1,32,128]{4,3,2,1,0:T(8,128)S(1)}, f32[1,2,1,32,128]{4,3,2,1,0:T(8,128)S(1)}, u32[]{:S(2)}, u32[]{:S(2)}) collective-permute-start(f32[1,2,1,32,128]{4,3,2,1,0:T(8,128)S(1)} %slice.946), channel_id=1, source_target_pairs={{0,4},{4,8},{8,12},{12,16},{16,20},{20,24},{24,28},{1,5},{5,9},{9,... | collective-permute-start | bytes 98312 | tf_op jit(solution)/shard_map/ppermute | solution.py:23
  56.1 5.3 %collective-permute-start.6 = (f32[1,2,4,32,1]{4,3,2,1,0:T(8,128)S(1)}, f32[1,2,4,32,1]{4,3,2,1,0:T(8,128)S(1)}, u32[]{:S(2)}, u32[]{:S(2)}) collective-permute-start(f32[1,2,4,32,1]{4,3,2,1,0:T(8,128)S(1)} %slice.631), channel_id=1, source_target_pairs={{0,1},{1,2},{2,3},{4,5},{5,6},{6,7},{8,9},{9,10},{10,11},{12,13},{... | collective-permute-start | bytes 3080 | tf_op jit(solution)/shard_map/ppermute | solution.py:23
  58.7 6.1 %collective-permute-start.7 = (f32[1,2,1,32,128]{4,3,2,1,0:T(8,128)S(1)}, f32[1,2,1,32,128]{4,3,2,1,0:T(8,128)S(1)}, u32[]{:S(2)}, u32[]{:S(2)}) collective-permute-start(f32[1,2,1,32,128]{4,3,2,1,0:T(8,128)S(1)} %slice.831), channel_id=1, source_target_pairs={{0,4},{4,8},{8,12},{12,16},{16,20},{20,24},{24,28},{1,5},{5,9},{9,... | collective-permute-start | bytes 98312 | tf_op jit(solution)/shard_map/ppermute | solution.py:23
  65.3 6.9 %collective-permute-start.8 = (f32[1,2,4,32,1]{4,3,2,1,0:T(8,128)S(1)}, f32[1,2,4,32,1]{4,3,2,1,0:T(8,128)S(1)}, u32[]{:S(2)}, u32[]{:S(2)}) collective-permute-start(f32[1,2,4,32,1]{4,3,2,1,0:T(8,128)S(1)} %slice.647), channel_id=1, source_target_pairs={{1,0},{2,1},{3,2},{5,4},{6,5},{7,6},{9,8},{10,9},{11,10},{13,12},{... | collective-permute-start | bytes 3080 | tf_op jit(solution)/shard_map/ppermute | solution.py:23
  66.8 5.3 %collective-permute-start.9 = (f32[1,2,1,32,128]{4,3,2,1,0:T(8,128)S(1)}, f32[1,2,1,32,128]{4,3,2,1,0:T(8,128)S(1)}, u32[]{:S(2)}, u32[]{:S(2)}) collective-permute-start(f32[1,2,1,32,128]{4,3,2,1,0:T(8,128)S(1)} %slice.846), channel_id=1, source_target_pairs={{4,0},{8,4},{12,8},{16,12},{20,16},{24,20},{28,24},{5,1},{9,5},{13... | collective-permute-start | bytes 98312 | tf_op jit(solution)/shard_map/ppermute | solution.py:23
  72.6 5.4 %collective-permute-start.10 = (f32[1,2,4,32,1]{4,3,2,1,0:T(8,128)S(1)}, f32[1,2,4,32,1]{4,3,2,1,0:T(8,128)S(1)}, u32[]{:S(2)}, u32[]{:S(2)}) collective-permute-start(f32[1,2,4,32,1]{4,3,2,1,0:T(8,128)S(1)} %slice.661), channel_id=1, source_target_pairs={{0,1},{1,2},{2,3},{4,5},{5,6},{6,7},{8,9},{9,10},{10,11},{12,13},{... | collective-permute-start | bytes 3080 | tf_op jit(solution)/shard_map/ppermute | solution.py:23
  75.4 6.1 %collective-permute-start.11 = (f32[1,2,1,32,128]{4,3,2,1,0:T(8,128)S(1)}, f32[1,2,1,32,128]{4,3,2,1,0:T(8,128)S(1)}, u32[]{:S(2)}, u32[]{:S(2)}) collective-permute-start(f32[1,2,1,32,128]{4,3,2,1,0:T(8,128)S(1)} %slice.859), channel_id=1, source_target_pairs={{0,4},{4,8},{8,12},{12,16},{16,20},{20,24},{24,28},{1,5},{5,9},{9,... | collective-permute-start | bytes 98312 | tf_op jit(solution)/shard_map/ppermute | solution.py:23
  82.6 4.3 %collective-permute-start.17 = (f32[2,2,128]{2,0,1:T(2,128)S(1)}, f32[2,2,128]{2,0,1:T(2,128)S(1)}, u32[]{:S(2)}, u32[]{:S(2)}) collective-permute-start(f32[2,2,128]{2,0,1:T(2,128)S(1)} %get-tuple-element.104), channel_id=1, source_target_pairs={{4,0},{8,4},{12,8},{16,12},{20,16},{24,20},{28,24},{5,1},{9,5},{13... | collective-permute-start | bytes 6152 | tf_op jit(solution)/shard_map/ppermute | solution.py:34
  84.5 5.8 %collective-permute-start.16 = (f32[2,2,128]{2,0,1:T(2,128)S(1)}, f32[2,2,128]{2,0,1:T(2,128)S(1)}, u32[]{:S(2)}, u32[]{:S(2)}) collective-permute-start(f32[2,2,128]{2,0,1:T(2,128)S(1)} %get-tuple-element.103), channel_id=1, source_target_pairs={{0,4},{4,8},{8,12},{12,16},{16,20},{20,24},{24,28},{1,5},{5,9},{9,... | collective-permute-start | bytes 6152 | tf_op jit(solution)/shard_map/ppermute | solution.py:33
  90.4 4.8 %collective-permute-start.18 = (f32[2,8,2]{2,0,1:T(2,128)S(1)}, f32[2,8,2]{2,0,1:T(2,128)S(1)}, u32[]{:S(2)}, u32[]{:S(2)}) collective-permute-start(f32[2,8,2]{2,0,1:T(2,128)S(1)} %get-tuple-element.97), channel_id=1, source_target_pairs={{0,1},{1,2},{2,3},{4,5},{5,6},{6,7},{8,9},{9,10},{10,11},{12,13},{... | collective-permute-start | bytes 392 | tf_op jit(solution)/shard_map/ppermute | solution.py:33
  93.8 5.5 %collective-permute-start.19 = (f32[2,8,2]{2,0,1:T(2,128)S(1)}, f32[2,8,2]{2,0,1:T(2,128)S(1)}, u32[]{:S(2)}, u32[]{:S(2)}) collective-permute-start(f32[2,8,2]{2,0,1:T(2,128)S(1)} %get-tuple-element.98), channel_id=1, source_target_pairs={{1,0},{2,1},{3,2},{5,4},{6,5},{7,6},{9,8},{10,9},{11,10},{13,12},{... | collective-permute-start | bytes 392 | tf_op jit(solution)/shard_map/ppermute | solution.py:34
  (6 other events, 14.4 us)
where the time goes:
time: 101 us; the launch traced here: 100 us
  starting transfers between devices  55.6 us (55%)
  waiting for transfers between devices  32.2 us (32%)
  local copies, waits for them, and re-layouts  6.85 us (7%)
  other arithmetic  3.93 us (4%)
  between operations  1.61 us (2%)
    ppermute x16, starting transfers between devices, from_behind(): return lax.ppermute(block, axis, route)  33.6 us
    ppermute x16, waiting for transfers between devices, from_behind(): return lax.ppermute(block, axis, route)  23.3 us
    ppermute x4, starting transfers between devices, with_halo(): before = lax.ppermute(last, axis, up)  12.9 us
    ppermute x4, starting transfers between devices, with_halo(): after = lax.ppermute(first, axis, down)  9.04 us
    ppermute x4, waiting for transfers between devices, with_halo(): before = lax.ppermute(last, axis, up)  4.73 us
    ppermute x4, waiting for transfers between devices, with_halo(): after = lax.ppermute(first, axis, down)  4.2 us
    unnamed x16, local copies, waits for them, and re-layouts  3.57 us
  transfers between devices with their start and end apart: 24, of which 12 were waited for; matrix products, arithmetic and copies ran while one was open for 3% of the time, Pallas kernels for 0%

commit v1 on v0

v1 whole, which is shorter than its diff:
```python
import functools
import math

import jax
import jax.numpy as jnp
import numpy as np
from jax import lax
from jax.experimental import pallas as pl
from jax.experimental.pallas import tpu as pltpu
from jax.sharding import PartitionSpec as P

RAD = 2
COURANT = 0.5
SHARP = 4.0
LEVEL = 0.5
CONTRAST = 5.0
ABSORB = 0.3
OMEGA = 0.7
CREST = math.tanh(SHARP * LEVEL)
SCALE = CREST + math.tanh(SHARP * (1.0 - LEVEL))

LANES = 128
TILE = 8
FULL_K = 2
WIN_K = 4
DEN_K = 8
FIRST, LAST = -4, 8
DEN_BASE = 6


def kernel_table(radius):
    offsets = np.arange(-radius, radius + 1)
    distance = np.sqrt(offsets[:, None] ** 2 + offsets[None, :] ** 2)
    table = np.maximum(0.0, radius + 1.0 - distance)
    return table / table.sum()


def odd_swap(index):
    return ((index + 1) ^ 1) - 1


def pair_permute(block, partner):
    count_x, count_y = lax.axis_size("gx"), lax.axis_size("gy")
    route = []
    for i in range(count_x):
        for j in range(count_y):
            a, b = partner(i, j, count_x, count_y)
            route.append((i * count_y + j, a * count_y + b))
    return lax.ppermute(block, ("gx", "gy"), route)


def x_even(i, j, nx, ny):
    return i ^ 1, j


def x_odd(i, j, nx, ny):
    return (odd_swap(i), j) if 0 < i < nx - 1 else (i, j ^ 1)


def y_even(i, j, nx, ny):
    return i, j ^ 1


def y_odd(i, j, nx, ny):
    return (i, odd_swap(j)) if 0 < j < ny - 1 else (i ^ 1, j)


def x_far_low(i, j, nx, ny):
    return (i + 2 if i % 4 < 2 else i - 2), j


def x_far_high(i, j, nx, ny):
    a = i + 2 if i % 4 >= 2 else i - 2
    return (a, j) if 0 <= a < nx else (i ^ 1, j)


class Sent:
    def __init__(self, depth):
        self.depth = depth
        self.full = {}
        at = 0
        for name in ("ae", "ah"):
            for c in range(3):
                for near in range(2):
                    self.full[name, c, near] = at
                    at += depth
        self.third = {}
        for name in ("ae", "ah"):
            for c in range(3):
                self.third[name, c] = at
                at += TILE
        self.window = {}
        for name in ("e", "h"):
            for c in range(3):
                for row in range(4):
                    self.window[name, c, row] = at
                    at += TILE
        self.density = at
        at += TILE
        self.region = at
        at += TILE
        self.rows = at


class Packed:
    def __init__(self, depth):
        self.full = {}
        slots = LANES // (2 * FULL_K)
        count = 0
        for name in ("ae", "ah"):
            for c in range(3):
                for row in range(-2, 6):
                    self.full[name, c, row] = (count // slots * depth, count % slots)
                    count += 1
        at = -(-count // slots) * depth
        self.full_rows = at
        self.window = {}
        slots = LANES // (2 * WIN_K)
        count = 0
        for name, low, high in (("e", FIRST, LAST), ("h", FIRST, LAST), ("ae", -3, 7), ("ah", -3, 7)):
            for c in range(3):
                for row in range(low, high):
                    self.window[name, c, row] = (at + count // slots * TILE, count % slots)
                    count += 1
        at += -(-count // slots) * TILE
        self.window_rows = at
        self.density = at
        self.rows = at + TILE


def lane_index(rows, lanes=LANES):
    return lax.broadcasted_iota(jnp.int32, (rows, lanes), 1)


def pack_x_kernel(depth, den, e, h, ae, ah, reg, to_even, to_odd):
    odd = lax.rem(lax.axis_index("gx"), 2)
    sent = Sent(depth)
    rows = den.shape[1]
    low = depth // 2 - 4
    for ref, right in ((to_even, 1 - odd), (to_odd, odd)):
        start = right * (rows - 2)
        third = 2 + right * (rows - 5)
        for name, field in (("ae", ae), ("ah", ah)):
            for c in range(3):
                for near in range(2):
                    at = sent.full[name, c, near]
                    ref[at : at + depth, :] = field[c, start + near]
                at = sent.third[name, c]
                ref[at : at + TILE, :] = field[c, third, low : low + TILE, :]
        for name, field in (("e", e), ("h", h)):
            for c in range(3):
                for row in range(4):
                    at = sent.window[name, c, row]
                    ref[at : at + TILE, :] = field[c, row, low : low + TILE, :]
        at = sent.density
        ref[at : at + 4, :] = den[0]
        ref[at + 4 : at + 8, :] = den[1]
        at = sent.region
        ref[at : at + 4, :] = reg[...].astype(jnp.float32)
        ref[at + 4 : at + 8, :] = jnp.zeros((4, LANES), jnp.float32)


class Rows:
    def __init__(self, depth, own, from_even, from_odd):
        index = lax.axis_index("gx")
        last = lax.axis_size("gx") - 1
        odd = lax.rem(index, 2)
        even = 1 - odd
        as_float = lambda flag: flag.astype(jnp.float32)
        self.left = as_float(odd), as_float(even * (index > 0).astype(jnp.int32))
        self.right = as_float(even), as_float(odd * (index < last).astype(jnp.int32))
        self.sent = Sent(depth)
        self.depth = depth
        self.low = depth // 2 - 4
        self.own = own
        self.even, self.odd = from_even, from_odd

    def of(self, side, at, count):
        return side[0] * self.even[at : at + count, :] + side[1] * self.odd[at : at + count, :]

    def full(self, name, c, row):
        if 0 <= row < 4:
            return self.own[name][c, row]
        if row < 0:
            return self.of(self.left, self.sent.full[name, c, row + 2], self.depth)
        return self.of(self.right, self.sent.full[name, c, row - 4], self.depth)

    def window(self, name, c, row):
        low, sent = self.low, self.sent
        if 0 <= row < 4:
            return self.own[name][c, row, low : low + TILE, :]
        side = self.left if row < 0 else self.right
        if name in ("e", "h"):
            return self.of(side, sent.window[name, c, row + 4 if row < 0 else row - 4], TILE)
        if row in (-3, 6):
            return self.of(side, sent.third[name, c], TILE)
        return self.of(side, sent.full[name, c, row + 2 if row < 0 else row - 4] + low, TILE)


def pack_y_kernel(depth, den, e, h, ae, ah, reg, from_even, from_odd, far_low, far_high, packed, columns):
    rows = Rows(depth, {"e": e, "h": h, "ae": ae, "ah": ah}, from_even, from_odd)
    plan = Packed(depth)
    index = lax.axis_index("gx")
    last = lax.axis_size("gx") - 1
    high = lax.rem(index, 4) // 2
    as_float = lambda flag: flag.astype(jnp.float32)
    left_far = as_float(high), as_float((1 - high) * (index > 1).astype(jnp.int32))
    right_far = as_float(1 - high), as_float(high * (index < last - 1).astype(jnp.int32))
    zero_row = jnp.zeros((1, LANES), jnp.float32)
    left = rows.of(rows.left, rows.sent.density, TILE)
    right = rows.of(rows.right, rows.sent.density, TILE)
    for layer in range(2):
        at = layer * 16
        columns[at : at + 1, :] = zero_row
        columns[at + 1 : at + 2, :] = left_far[0] * far_low[layer, 3:4, :] + left_far[1] * far_high[layer, 3:4, :]
        columns[at + 2 : at + 6, :] = left[4 * layer : 4 * layer + 4]
        columns[at + 6 : at + 10, :] = den[layer]
        columns[at + 10 : at + 14, :] = right[4 * layer : 4 * layer + 4]
        columns[at + 14 : at + 15, :] = right_far[0] * far_low[layer, 0:1, :] + right_far[1] * far_high[layer, 0:1, :]
        columns[at + 15 : at + 16, :] = zero_row
    at = 32
    columns[at : at + 2, :] = jnp.zeros((2, LANES), jnp.float32)
    columns[at + 2 : at + 6, :] = rows.of(rows.left, rows.sent.region, TILE)[:4]
    columns[at + 6 : at + 10, :] = reg[...].astype(jnp.float32)
    columns[at + 10 : at + 14, :] = rows.of(rows.right, rows.sent.region, TILE)[:4]
    columns[at + 14 : at + 16, :] = jnp.zeros((2, LANES), jnp.float32)

    def pack(planes, width, count):
        slots = LANES // (2 * width)
        owner = lax.rem((lane_index(count) + width) // (2 * width), slots)
        total = None
        for slot, plane in enumerate(planes):
            moved = pltpu.roll(plane, slot * 2 * width, 1) if slot else plane
            total = moved if total is None else jnp.where(owner == slot, moved, total)
        return total

    groups = {}
    for key, (at, slot) in plan.full.items():
        groups.setdefault(at, []).append(key)
    for at, keys in groups.items():
        packed[at : at + depth, :] = pack([rows.full(*key) for key in keys], FULL_K, depth)
    groups = {}
    for key, (at, slot) in plan.window.items():
        groups.setdefault(at, []).append(key)
    for at, keys in groups.items():
        packed[at : at + TILE, :] = pack([rows.window(*key) for key in keys], WIN_K, TILE)
    at = plan.density
    packed[at : at + TILE, :] = pack([columns[8 * n : 8 * n + 8, :] for n in range(6)], DEN_K, TILE)


def up_z(block):
    depth = block.shape[0]
    moved = pltpu.roll(block, depth - 1, 0)
    if depth == TILE:
        return moved - block
    edge = lax.broadcasted_iota(jnp.int32, block.shape, 0) == depth - 1
    return jnp.where(edge, 0.0, moved) - block


def down_z(block):
    moved = pltpu.roll(block, 1, 0)
    if block.shape[0] == TILE:
        return block - moved
    edge = lax.broadcasted_iota(jnp.int32, block.shape, 0) == 0
    return block - jnp.where(edge, 0.0, moved)


def up_y(block):
    return pltpu.roll(block, block.shape[1] - 1, 1) - block


def down_y(block):
    return block - pltpu.roll(block, 1, 1)


def curl_up(here, after):
    x, y, z = here
    return (up_y(z) - up_z(y), up_z(x) - (after[2] - z), (after[1] - y) - up_y(x))


def curl_down(here, before):
    x, y, z = here
    return (down_y(z) - down_z(y), down_z(x) - (z - before[2]), (y - before[1]) - down_y(x))


def blur(block):
    table = kernel_table(RAD)
    lanes, count = block.shape[1], block.shape[0]
    sums = [block]
    for b in range(1, RAD + 1):
        sums.append(pltpu.roll(block, b, 1) + pltpu.roll(block, lanes - b, 1))
    total = None
    for a in range(RAD + 1):
        part = sum(float(table[RAD + a, RAD + b]) * sums[b] for b in range(RAD + 1))
        if a:
            part = pltpu.roll(part, a, 0) + pltpu.roll(part, count - a, 0)
        total = part if total is None else total + part
    return total


def main_kernel(
    depth, den, e, h, ae, ah, reg, from_even, from_odd, columns, packed_even, packed_odd,
    grad, out_e, out_h,
    halo, ga, bh, be, gb, ratio_rows,
):
    rows = Rows(depth, {"e": e, "h": h, "ae": ae, "ah": ah}, from_even, from_odd)
    plan = Packed(depth)
    wide = 2 * LANES
    centre = depth // 2
    low = rows.low
    j = lax.axis_index("gy")
    last_y = lax.axis_size("gy") - 1
    odd_y = lax.rem(j, 2)
    even_y = 1 - odd_y
    as_float = lambda flag: flag.astype(jnp.float32)
    has_left = as_float((j > 0).astype(jnp.int32))
    has_right = as_float((j < last_y).astype(jnp.int32))
    left = as_float(odd_y), as_float(even_y * (j > 0).astype(jnp.int32))
    right = as_float(even_y), as_float(odd_y * (j < last_y).astype(jnp.int32))

    def combine(at, count, width):
        from_left = lax.rem(lane_index(count), 2 * width) >= width
        even, odd = packed_even[at : at + count, :], packed_odd[at : at + count, :]
        halo[at : at + count, :] = jnp.where(from_left, left[0] * even + left[1] * odd, right[0] * even + right[1] * odd)

    combine(0, plan.full_rows, FULL_K)
    combine(plan.full_rows, plan.window_rows - plan.full_rows, WIN_K)
    combine(plan.density, TILE, DEN_K)

    def unroll(at, count, shift):
        block = halo[at : at + count, :]
        return pltpu.roll(block, LANES - shift, 1) if shift else block

    def full(name, c, row):
        at, slot = plan.full[name, c, row]
        return jnp.concatenate([rows.full(name, c, row), unroll(at, depth, slot * 2 * FULL_K)], 1)

    def window(name, c, row):
        at, slot = plan.window[name, c, row]
        return jnp.concatenate([rows.window(name, c, row), unroll(at, TILE, slot * 2 * WIN_K)], 1)

    def column_block(n):
        parts = []
        for half in range(2):
            at = 8 * (2 * n + half)
            parts.append(
                jnp.concatenate(
                    [columns[at : at + 8, :], unroll(plan.density, TILE, (2 * n + half) * 2 * DEN_K)], 1
                )
            )
        return jnp.concatenate(parts, 0)

    region = column_block(2)
    design = (region == 2.0).astype(jnp.float32)
    absorbing = (region == 1.0).astype(jnp.float32)
    source = (region == 3.0).astype(jnp.float32)
    inverse, slope = [], []
    for layer in range(2):
        inner = jnp.tanh(SHARP * (blur(column_block(layer)) - LEVEL))
        projected = (CREST + inner) / SCALE
        slope.append(SHARP * (1.0 - inner * inner) / SCALE)
        inverse.append(1.0 / (1.0 + CONTRAST * design * projected))
    damp = ABSORB * absorbing
    keep_col = (1.0 - damp) / (1.0 + damp)
    gain_col = COURANT / (1.0 + damp)

    lane = lane_index(TILE, wide)
    inside = jnp.where(lane < LANES, 1.0, jnp.where(lane < LANES + LANES // 2, has_right, has_left))
    has_below = rows.left[0] + rows.left[1]
    has_above = rows.right[0] + rows.right[1]
    masks = {"own": inside, "below": inside * has_below, "above": inside * has_above}
    steps = {key: COURANT * value for key, value in masks.items()}
    where_row = lambda row: "own" if 0 <= row < 4 else ("below" if row < 0 else "above")

    def spread(block, row, count=TILE):
        at = row + DEN_BASE
        return jnp.broadcast_to(block[at : at + 1, :], (count, block.shape[1]))

    sub = lax.broadcasted_iota(jnp.int32, (TILE, wide), 0) + low

    def layered(row):
        first, second = spread(inverse[0], row), spread(inverse[1], row)
        return jnp.where(sub == centre, first, jnp.where(sub == centre + 1, second, 1.0))

    keep_win = {row: spread(keep_col, row) for row in range(-3, 7)}
    layer_win = {row: layered(row) for row in range(-3, 7)}
    gain_win = {row: spread(gain_col, row) * layer_win[row] * masks[where_row(row)] for row in range(-3, 7)}
    source_plane = (sub == centre - 1).astype(jnp.float32)
    amounts = [math.sin(OMEGA * (step + 1)) for step in range(2)]
    e0 = {row: [window("e", c, row) for c in range(3)] for row in range(-4, 8)}
    h0 = {row: [window("h", c, row) for c in range(3)] for row in range(-4, 7)}
    h1, e1, h2, drive1, drive2 = {}, {}, {}, {}, {}

    def minus_step(base, curl, row):
        step = steps[where_row(row)]
        return [b - step * c for b, c in zip(base, curl)]

    for row in range(-4, 7):
        h1[row] = minus_step(h0[row], curl_up(e0[row], e0[row + 1]), row)
    for row in range(-3, 7):
        drive = list(curl_down(h1[row], h1[row - 1]))
        at_source = source_plane * spread(source, row)
        drive[2] = drive[2] - amounts[0] * at_source
        drive1[row] = drive
        e1[row] = [keep_win[row] * b + gain_win[row] * d for b, d in zip(e0[row], drive)]
    for row in range(-3, 6):
        h2[row] = minus_step(h1[row], curl_up(e1[row], e1[row + 1]), row)
    for row in range(-2, 6):
        drive2[row] = list(curl_down(h2[row], h2[row - 1]))
        drive2[row][2] = drive2[row][2] - amounts[1] * source_plane * spread(source, row)
    a2 = {row: [window("ae", c, row) for c in range(3)] for row in range(-3, 7)}
    ga_win = {row: [gain_win[row] * v for v in a2[row]] for row in range(-3, 7)}
    bh_win = {}
    for row in range(-3, 6):
        mask = masks[where_row(row)]
        curl = curl_up(ga_win[row], ga_win[row + 1])
        bh_win[row] = [window("ah", c, row) + mask * curl[c] for c in range(3)]
    ratio_rows[...] = jnp.zeros(ratio_rows.shape, jnp.float32)
    for row in range(-2, 6):
        a1 = minus_step(
            [keep_win[row] * v for v in a2[row]], curl_down(bh_win[row], bh_win[row - 1]), row
        )
        total = sum(a2[row][c] * drive2[row][c] + a1[c] * drive1[row][c] for c in range(3))
        for layer in range(2):
            at = centre + layer - low
            ratio_rows[layer, row + DEN_BASE : row + DEN_BASE + 1, :] = total[at : at + 1, :]
    for layer in range(2):
        sensitivity = -ratio_rows[layer] * gain_col * inverse[layer] * inverse[layer]
        smoothed = blur(CONTRAST * design * sensitivity * slope[layer])
        grad[layer] = smoothed[DEN_BASE : DEN_BASE + 4, :LANES]

    z = lax.broadcasted_iota(jnp.int32, (depth, wide), 0)
    zf = z.astype(jnp.float32)
    margin = float(depth // 8)
    ramp = jnp.maximum(jnp.maximum((margin - zf) / margin, (zf - (depth - 1 - margin)) / margin), 0.0)
    open_damp = ABSORB * ramp * ramp
    full_damp = open_damp + ABSORB
    gain_open, gain_abs = COURANT / (1.0 + open_damp), COURANT / (1.0 + full_damp)
    keep_open, keep_abs = (1.0 - open_damp) / (1.0 + open_damp), (1.0 - full_damp) / (1.0 + full_damp)

    def coefficient(row):
        flag = spread(absorbing, row, depth) > 0.5
        layers = jnp.where(
            z == centre,
            spread(inverse[0], row, depth),
            jnp.where(z == centre + 1, spread(inverse[1], row, depth), 1.0),
        )
        return jnp.where(flag, keep_abs, keep_open), jnp.where(flag, gain_abs, gain_open) * layers

    def stretch(block):
        return jnp.broadcast_to(block[:1, :], (depth, wide))

    masks = {key: stretch(value) for key, value in masks.items()}
    steps = {key: stretch(value) for key, value in steps.items()}

    for row in range(-2, 6):
        keep, gain = coefficient(row)
        for c in range(3):
            value = full("ae", c, row)
            ga[c, row + 2] = gain * value
            if -1 <= row <= 4:
                be[c, row + 1] = keep * value
    for row in range(-2, 5):
        curl = curl_up([ga[c, row + 2] for c in range(3)], [ga[c, row + 3] for c in range(3)])
        for c in range(3):
            bh[c, row + 2] = full("ah", c, row) + masks[where_row(row)] * curl[c]
    for row in range(-1, 5):
        keep, gain = coefficient(row)
        curl = curl_down([bh[c, row + 2] for c in range(3)], [bh[c, row + 1] for c in range(3)])
        for c in range(3):
            value = be[c, row + 1] - steps[where_row(row)] * curl[c]
            be[c, row + 1] = keep * value
            gb[c, row + 1] = gain * value
    for row in range(-1, 4):
        curl = curl_up([gb[c, row + 1] for c in range(3)], [gb[c, row + 2] for c in range(3)])
        for c in range(3):
            value = bh[c, row + 2] + masks[where_row(row)] * curl[c]
            bh[c, row + 2] = value
            if row >= 0:
                out_h[c, row] = value[:, :LANES]
    for row in range(4):
        curl = curl_down([bh[c, row + 2] for c in range(3)], [bh[c, row + 1] for c in range(3)])
        for c in range(3):
            out_e[c, row] = be[c, row + 1][:, :LANES] - COURANT * curl[c][:, :LANES]


def per_device(density, e_field, h_field, adj_e, adj_h, region):
    depth = e_field.shape[2]
    sent, plan = Sent(depth), Packed(depth)
    f32 = jnp.float32
    own = (density, e_field, h_field, adj_e, adj_h, region)
    params = pltpu.CompilerParams(vmem_limit_bytes=32 * 1024 * 1024)
    shape = jax.ShapeDtypeStruct
    to_even, to_odd = pl.pallas_call(
        functools.partial(pack_x_kernel, depth),
        out_shape=(shape((sent.rows, LANES), f32),) * 2,
        compiler_params=params,
        name="pack_x",
    )(*own)
    from_odd = pair_permute(to_odd, x_odd)
    from_even = pair_permute(to_even, x_even)
    far_low = pair_permute(density, x_far_low)
    far_high = pair_permute(density, x_far_high)
    packed, columns = pl.pallas_call(
        functools.partial(pack_y_kernel, depth),
        out_shape=(shape((plan.rows, LANES), f32), shape((48, LANES), f32)),
        compiler_params=params,
        name="pack_y",
    )(*own, from_even, from_odd, far_low, far_high)
    packed_odd = pair_permute(packed, y_odd)
    packed_even = pair_permute(packed, y_even)
    wide = 2 * LANES
    return pl.pallas_call(
        functools.partial(main_kernel, depth),
        out_shape=(
            shape(density.shape, f32),
            shape(e_field.shape, f32),
            shape(e_field.shape, f32),
        ),
        scratch_shapes=[
            pltpu.VMEM((plan.rows, LANES), f32),
            pltpu.VMEM((3, 8, depth, wide), f32),
            pltpu.VMEM((3, 7, depth, wide), f32),
            pltpu.VMEM((3, 6, depth, wide), f32),
            pltpu.VMEM((3, 6, depth, wide), f32),
            pltpu.VMEM((2, 16, wide), f32),
        ],
        compiler_params=params,
        name="adjoint",
    )(*own, from_even, from_odd, columns, packed_even, packed_odd)


def solution(mesh):
    field = P(None, "gx", None, "gy")
    design = P(None, "gx", "gy")
    return jax.shard_map(
        per_device,
        mesh=mesh,
        in_specs=(design, field, field, field, field, P("gx", "gy")),
        out_specs=(design, field, field),
        check_vma=False,
    )
```

time: 101 us -> 26.3 us (0.26)
  the two profiles are of different devices: /device:TPU:4 before, /device:TPU:0 now
where the time goes in v1:
time: 26.3 us; the launch traced here: 26 us
  starting transfers between devices  10.4 us (40%)
  waiting for transfers between devices  7.22 us (27%)
  local copies, waits for them, and re-layouts  5.07 us (19%)
  Pallas kernels  2.71 us (10%)
  between operations  0.66 us (3%)
    ppermute x6, starting transfers between devices, pair_permute(): return lax.ppermute(block, ('gx', 'gy'), route)  10.4 us
    ppermute x6, waiting for transfers between devices, pair_permute(): return lax.ppermute(block, ('gx', 'gy'), route)  7.22 us
    unnamed x12, local copies, waits for them, and re-layouts  5.07 us
    pallas_call x1, Pallas kernels, per_device(): pl.pallas_call(functools.partial(main_kernel, depth), out_shape=(shape(de...  2.26 us
  transfers between devices with their start and end apart: 6, of which 2 were waited for; matrix products, arithmetic and copies ran while one was open for 0% of the time, Pallas kernels for 0%

profile of v1, /device:TPU:0, one launch (start us, length us, event | category | flops | bytes accessed | tf_op | source)
XLA Modules:
  0.0 26.0 jit_solution(11285578037023492663)
XLA Ops:
  0.6 0.0 copy-start
  0.6 0.9 %copy-done = f32[3,4,32,128]{3,2,1,0:T(8,128)S(1)} copy-done((f32[3,4,32,128]{3,2,1,0:T(8,128)S(1)}, f32[3,4,32,128]{3,2,1,0:T(8,128)}, u32[]{:S(2)}) %copy-start) | copy-done | bytes 196632
  1.6 0.0 copy-start.1
  1.6 0.9 %copy-done.1 = f32[3,4,32,128]{3,2,1,0:T(8,128)S(1)} copy-done((f32[3,4,32,128]{3,2,1,0:T(8,128)S(1)}, f32[3,4,32,128]{3,2,1,0:T(8,128)}, u32[]{:S(2)}) %copy-start.1) | copy-done | bytes 196632
  2.5 0.0 copy-start.2
  2.5 0.9 %copy-done.2 = f32[3,4,32,128]{3,2,1,0:T(8,128)S(1)} copy-done((f32[3,4,32,128]{3,2,1,0:T(8,128)S(1)}, f32[3,4,32,128]{3,2,1,0:T(8,128)}, u32[]{:S(2)}) %copy-start.2) | copy-done | bytes 196632
  3.4 0.0 copy-start.3
  3.4 0.9 %copy-done.3 = f32[3,4,32,128]{3,2,1,0:T(8,128)S(1)} copy-done((f32[3,4,32,128]{3,2,1,0:T(8,128)S(1)}, f32[3,4,32,128]{3,2,1,0:T(8,128)}, u32[]{:S(2)}) %copy-start.3) | copy-done | bytes 196632
  4.3 0.7 %copy-done.4 = f32[2,4,128]{2,1,0:T(4,128)S(1)} copy-done((f32[2,4,128]{2,1,0:T(4,128)S(1)}, f32[2,4,128]{2,1,0:T(4,128)}, u32[]{:S(2)}) %copy-start.4) | copy-done | bytes 4120
  5.0 0.7 %copy-done.5 = s32[4,128]{1,0:T(4,128)S(1)} copy-done((s32[4,128]{1,0:T(4,128)S(1)}, s32[4,128]{1,0:T(4,128)}, u32[]{:S(2)}) %copy-start.5) | copy-done | bytes 2072
  5.8 0.5 %collective-permute-start = (f32[640,128]{1,0:T(8,128)S(1)}, f32[640,128]{1,0:T(8,128)S(1)}, u32[]{:S(2)}, u32[]{:S(2)}) collective-permute-start(f32[640,128]{1,0:T(8,128)S(1)} %get-tuple-element.7), channel_id=1, source_target_pairs={{0,4},{1,5},{2,6},{3,7},{4,0},{5,1},{6,2},{7,3},{8,12},{9,13},{10,... | collective-permute-start | bytes 983048 | tf_op jit(solution)/shard_map/ppermute | solution.py:49
  6.3 2.6 %collective-permute-start.1 = (f32[640,128]{1,0:T(8,128)S(1)}, f32[640,128]{1,0:T(8,128)S(1)}, u32[]{:S(2)}, u32[]{:S(2)}) collective-permute-start(f32[640,128]{1,0:T(8,128)S(1)} %get-tuple-element.8), channel_id=1, source_target_pairs={{0,1},{1,0},{2,3},{3,2},{4,8},{5,9},{6,10},{7,11},{8,4},{9,5},{10,... | collective-permute-start | bytes 983048 | tf_op jit(solution)/shard_map/ppermute | solution.py:49
  8.9 0.0 collective-permute-start.3
  9.0 2.8 %collective-permute-start.2 = (f32[2,4,128]{2,1,0:T(4,128)S(1)}, f32[2,4,128]{2,1,0:T(4,128)S(1)}, u32[]{:S(2)}, u32[]{:S(2)}) collective-permute-start(f32[2,4,128]{2,1,0:T(4,128)S(1)} %copy-done.4), channel_id=1, source_target_pairs={{0,8},{1,9},{2,10},{3,11},{4,12},{5,13},{6,14},{7,15},{8,0},{9,1},... | collective-permute-start | bytes 12296 | tf_op jit(solution)/shard_map/ppermute | solution.py:49
  11.8 0.0 collective-permute-done.3.far_high
  11.8 4.9 %collective-permute-done.2.far_low = f32[2,4,128]{2,1,0:T(4,128)S(1)} collective-permute-done((f32[2,4,128]{2,1,0:T(4,128)S(1)}, f32[2,4,128]{2,1,0:T(4,128)S(1)}, u32[]{:S(2)}, u32[]{:S(2)}) %collective-permute-start.2) | collective-permute-done | bytes 4128 | tf_op jit(solution)/shard_map/ppermute | solution.py:49
  16.7 0.0 collective-permute-done.from_even
  16.7 0.0 collective-permute-done.1.from_odd
  16.7 0.4 %pack_y.1 = (f32[144,128]{1,0:T(8,128)S(1)}, f32[48,128]{1,0:T(8,128)S(1)}) custom-call(f32[2,4,128]{2,1,0:T(4,128)S(1)} %copy-done.4, f32[3,4,32,128]{3,2,1,0:T(8,128)S(1)} %copy-done, f32[3,4,32,128]{3,2,1,0:T(8,128)S(1)} %copy-done.1, f32[3,4,32,128]{3,2,1,0:T(8,128)S(1)} %copy-done.2, f32[3,4,32,128]{3,2,1,0:T(8,128)S(1)} %copy-done.3, ...), custom_call_target="tpu_custom_call" | custom-call | tf_op jit(solution)/shard_map/pack_y/pallas_call | solution.py:504
  17.1 0.8 %collective-permute-start.5 = (f32[144,128]{1,0:T(8,128)S(1)}, f32[144,128]{1,0:T(8,128)S(1)}, u32[]{:S(2)}, u32[]{:S(2)}) collective-permute-start(f32[144,128]{1,0:T(8,128)S(1)} %get-tuple-element.10), channel_id=1, source_target_pairs={{0,4},{1,2},{2,1},{3,7},{4,0},{5,6},{6,5},{7,3},{8,12},{9,10},{10,... | collective-permute-start | bytes 221192 | tf_op jit(solution)/shard_map/ppermute | solution.py:49
  17.9 3.6 %collective-permute-start.4 = (f32[144,128]{1,0:T(8,128)S(1)}, f32[144,128]{1,0:T(8,128)S(1)}, u32[]{:S(2)}, u32[]{:S(2)}) collective-permute-start(f32[144,128]{1,0:T(8,128)S(1)} %get-tuple-element.10), channel_id=1, source_target_pairs={{0,1},{1,0},{2,3},{3,2},{4,5},{5,4},{6,7},{7,6},{8,9},{9,8},{10,11... | collective-permute-start | bytes 221192 | tf_op jit(solution)/shard_map/ppermute | solution.py:49
  21.4 0.0 collective-permute-done.5.packed_odd
  21.4 2.3 %collective-permute-done.4.packed_even = f32[144,128]{1,0:T(8,128)S(1)} collective-permute-done((f32[144,128]{1,0:T(8,128)S(1)}, f32[144,128]{1,0:T(8,128)S(1)}, u32[]{:S(2)}, u32[]{:S(2)}) %collective-permute-start.4) | collective-permute-done | bytes 73760 | tf_op jit(solution)/shard_map/ppermute | solution.py:49
  23.8 2.3 %adjoint.1 = (f32[2,4,128]{2,1,0:T(4,128)}, f32[3,4,32,128]{3,2,1,0:T(8,128)}, f32[3,4,32,128]{3,2,1,0:T(8,128)}) custom-call(f32[2,4,128]{2,1,0:T(4,128)S(1)} %copy-done.4, f32[3,4,32,128]{3,2,1,0:T(8,128)S(1)} %copy-done, f32[3,4,32,128]{3,2,1,0:T(8,128)S(1)} %copy-done.1, f32[3,4,32,128]{3,2,1,0:T(8,128)S(1)} %copy-done.2, ...), custom_call_target="tpu_custom_call" | custom-call | tf_op jit(solution)/shard_map/adjoint/pallas_call | solution.py:513
  (3 shorter events, 0.0 us)
Async XLA Ops:
  0.6 0.9 %copy-start = (f32[3,4,32,128]{3,2,1,0:T(8,128)S(1)}, f32[3,4,32,128]{3,2,1,0:T(8,128)}, u32[]{:S(2)}) copy-start(f32[3,4,32,128]{3,2,1,0:T(8,128)} %e.5) | copy-start | bytes 589828
  1.6 0.9 %copy-start.1 = (f32[3,4,32,128]{3,2,1,0:T(8,128)S(1)}, f32[3,4,32,128]{3,2,1,0:T(8,128)}, u32[]{:S(2)}) copy-start(f32[3,4,32,128]{3,2,1,0:T(8,128)} %h.5) | copy-start | bytes 589828
  2.5 0.9 %copy-start.2 = (f32[3,4,32,128]{3,2,1,0:T(8,128)S(1)}, f32[3,4,32,128]{3,2,1,0:T(8,128)}, u32[]{:S(2)}) copy-start(f32[3,4,32,128]{3,2,1,0:T(8,128)} %ae.5) | copy-start | bytes 589828
  3.4 0.9 %copy-start.3 = (f32[3,4,32,128]{3,2,1,0:T(8,128)S(1)}, f32[3,4,32,128]{3,2,1,0:T(8,128)}, u32[]{:S(2)}) copy-start(f32[3,4,32,128]{3,2,1,0:T(8,128)} %ah.5) | copy-start | bytes 589828
  4.3 0.7 %copy-start.4 = (f32[2,4,128]{2,1,0:T(4,128)S(1)}, f32[2,4,128]{2,1,0:T(4,128)}, u32[]{:S(2)}) copy-start(f32[2,4,128]{2,1,0:T(4,128)} %den.5) | copy-start | bytes 12292
  5.0 0.7 %copy-start.5 = (s32[4,128]{1,0:T(4,128)S(1)}, s32[4,128]{1,0:T(4,128)}, u32[]{:S(2)}) copy-start(s32[4,128]{1,0:T(4,128)} %reg.5) | copy-start | bytes 6148
  5.8 10.9 %collective-permute-start = (f32[640,128]{1,0:T(8,128)S(1)}, f32[640,128]{1,0:T(8,128)S(1)}, u32[]{:S(2)}, u32[]{:S(2)}) collective-permute-start(f32[640,128]{1,0:T(8,128)S(1)} %get-tuple-element.7), channel_id=1, source_target_pairs={{0,4},{1,5},{2,6},{3,7},{4,0},{5,1},{6,2},{7,3},{8,12},{9,13},{10,... | collective-permute-start | bytes 983048 | tf_op jit(solution)/shard_map/ppermute | solution.py:49
  6.3 10.4 %collective-permute-start.1 = (f32[640,128]{1,0:T(8,128)S(1)}, f32[640,128]{1,0:T(8,128)S(1)}, u32[]{:S(2)}, u32[]{:S(2)}) collective-permute-start(f32[640,128]{1,0:T(8,128)S(1)} %get-tuple-element.8), channel_id=1, source_target_pairs={{0,1},{1,0},{2,3},{3,2},{4,8},{5,9},{6,10},{7,11},{8,4},{9,5},{10,... | collective-permute-start | bytes 983048 | tf_op jit(solution)/shard_map/ppermute | solution.py:49
  8.9 2.9 %collective-permute-start.3 = (f32[2,4,128]{2,1,0:T(4,128)S(1)}, f32[2,4,128]{2,1,0:T(4,128)S(1)}, u32[]{:S(2)}, u32[]{:S(2)}) collective-permute-start(f32[2,4,128]{2,1,0:T(4,128)S(1)} %copy-done.4), channel_id=1, source_target_pairs={{0,4},{1,5},{2,6},{3,7},{4,0},{5,1},{6,2},{7,3},{8,16},{9,17},{10,... | collective-permute-start | bytes 12296 | tf_op jit(solution)/shard_map/ppermute | solution.py:49
  9.0 7.7 %collective-permute-start.2 = (f32[2,4,128]{2,1,0:T(4,128)S(1)}, f32[2,4,128]{2,1,0:T(4,128)S(1)}, u32[]{:S(2)}, u32[]{:S(2)}) collective-permute-start(f32[2,4,128]{2,1,0:T(4,128)S(1)} %copy-done.4), channel_id=1, source_target_pairs={{0,8},{1,9},{2,10},{3,11},{4,12},{5,13},{6,14},{7,15},{8,0},{9,1},... | collective-permute-start | bytes 12296 | tf_op jit(solution)/shard_map/ppermute | solution.py:49
  17.1 4.3 %collective-permute-start.5 = (f32[144,128]{1,0:T(8,128)S(1)}, f32[144,128]{1,0:T(8,128)S(1)}, u32[]{:S(2)}, u32[]{:S(2)}) collective-permute-start(f32[144,128]{1,0:T(8,128)S(1)} %get-tuple-element.10), channel_id=1, source_target_pairs={{0,4},{1,2},{2,1},{3,7},{4,0},{5,6},{6,5},{7,3},{8,12},{9,10},{10,... | collective-permute-start | bytes 221192 | tf_op jit(solution)/shard_map/ppermute | solution.py:49
  17.9 5.9 %collective-permute-start.4 = (f32[144,128]{1,0:T(8,128)S(1)}, f32[144,128]{1,0:T(8,128)S(1)}, u32[]{:S(2)}, u32[]{:S(2)}) collective-permute-start(f32[144,128]{1,0:T(8,128)S(1)} %get-tuple-element.10), channel_id=1, source_target_pairs={{0,1},{1,0},{2,3},{3,2},{4,5},{5,4},{6,7},{7,6},{8,9},{9,8},{10,11... | collective-permute-start | bytes 221192 | tf_op jit(solution)/shard_map/ppermute | solution.py:49

commit v2 on v1

v2 whole, which is shorter than its diff:
```python
import functools
import math

import jax
import jax.numpy as jnp
import numpy as np
from jax import lax
from jax.experimental import pallas as pl
from jax.experimental.pallas import tpu as pltpu
from jax.sharding import PartitionSpec as P

RAD = 2
COURANT = 0.5
SHARP = 4.0
LEVEL = 0.5
CONTRAST = 5.0
ABSORB = 0.3
OMEGA = 0.7
CREST = math.tanh(SHARP * LEVEL)
SCALE = CREST + math.tanh(SHARP * (1.0 - LEVEL))

LANES = 128
LOAD_VMEM = 56 * 1024 * 1024
TILE = 8
FULL_K = 2
WIN_K = 4
FIRST, LAST = -4, 8
DEN_BASE = 6


def kernel_table(radius):
    offsets = np.arange(-radius, radius + 1)
    distance = np.sqrt(offsets[:, None] ** 2 + offsets[None, :] ** 2)
    table = np.maximum(0.0, radius + 1.0 - distance)
    return table / table.sum()


def odd_swap(index):
    return ((index + 1) ^ 1) - 1


def pair_permute(block, partner):
    count_x, count_y = lax.axis_size("gx"), lax.axis_size("gy")
    route = []
    for i in range(count_x):
        for j in range(count_y):
            a, b = partner(i, j, count_x, count_y)
            route.append((i * count_y + j, a * count_y + b))
    return lax.ppermute(block, ("gx", "gy"), route)


def x_even(i, j, nx, ny):
    return i ^ 1, j


def x_odd(i, j, nx, ny):
    return (odd_swap(i), j) if 0 < i < nx - 1 else (i, j ^ 1)


def x_ring(i, j, nx, ny):
    return odd_swap(i) % nx, j


def y_even(i, j, nx, ny):
    return i, j ^ 1


def y_odd(i, j, nx, ny):
    return (i, odd_swap(j)) if 0 < j < ny - 1 else (i ^ 1, j)


class Sent:
    def __init__(self, depth):
        self.full = {}
        at = 0
        for name in ("ae", "ah"):
            for c in range(3):
                for near in range(2):
                    self.full[name, c, near] = at
                    at += depth
        self.third = {}
        for name in ("ae", "ah"):
            for c in range(3):
                self.third[name, c] = at
                at += TILE
        self.window = {}
        for name in ("e", "h"):
            for c in range(3):
                for row in range(4):
                    self.window[name, c, row] = at
                    at += TILE
        self.density = at
        self.region = at + TILE
        self.mate = at + 2 * TILE
        self.rows = at + 3 * TILE


FIELDS = ("ae", "ah", "e", "h")


class Edges:
    def __init__(self, depth):
        self.window_at = depth
        self.columns_at = depth + 3 * TILE
        self.mate_at = self.columns_at + 2 * TILE
        self.rows = self.mate_at + TILE

    def full_slot(self, name, c, row):
        return row % 4 * 6 + FIELDS.index(name) * 3 + c

    def window_slot(self, name, c, row):
        place = (FIELDS.index(name) * 3 + c) * 4 + row % 4
        return place // 16 * TILE, place % 16


def lane_index(rows, lanes=LANES):
    return lax.broadcasted_iota(jnp.int32, (rows, lanes), 1)


def pack(planes, width):
    slots = LANES // (2 * width)
    owner = lax.rem((lane_index(planes[0].shape[0]) + width) // (2 * width), slots)
    total = None
    for slot, plane in enumerate(planes):
        moved = pltpu.roll(plane, slot * 2 * width, 1) if slot else plane
        total = moved if total is None else jnp.where(owner == slot, moved, total)
    return total


def near_layers(depth):
    low = depth // 2 - 4
    return low, low // TILE * TILE


def load_kernel(depth, den, e, h, ae, ah, reg, own_den, own_e, own_h, own_ae, own_ah, own_reg, sems):
    near = pl.ds(near_layers(depth)[1], 2 * TILE)
    pairs = (
        (ae, own_ae),
        (ah, own_ah),
        (e.at[:, :, near, :], own_e),
        (h.at[:, :, near, :], own_h),
        (den, own_den),
        (reg, own_reg),
    )
    copies = [pltpu.make_async_copy(source, target, sems.at[n]) for n, (source, target) in enumerate(pairs)]
    for copy in copies:
        copy.start()
    for copy in copies:
        copy.wait()


def near_windows(depth, e, h, ae, ah):
    low, base = near_layers(depth)
    windows = []
    for field, start in ((ae, low), (ah, low), (e, low - base), (h, low - base)):
        for c in range(3):
            for row in range(4):
                windows.append(field[c, row, start : start + TILE, :])
    return windows


def first_kernel(depth, den, e, h, ae, ah, reg, mate_den, edges, to_even, to_odd):
    plan, sent = Edges(depth), Sent(depth)
    low = near_layers(depth)[0]
    odd = lax.rem(lax.axis_index("gx"), 2)
    own = {"ae": ae, "ah": ah}
    windows = near_windows(depth, e, h, ae, ah)
    for ref, right in ((to_even, 1 - odd), (to_odd, odd)):
        start = right * (ae.shape[1] - 2)
        third = 2 + right * (ae.shape[1] - 5)
        for name in ("ae", "ah"):
            for c in range(3):
                for near in range(2):
                    at = sent.full[name, c, near]
                    ref[at : at + depth, :] = own[name][c, start + near]
                at = sent.third[name, c]
                ref[at : at + TILE, :] = own[name][c, third, low : low + TILE, :]
        for n, name in ((2, "e"), (3, "h")):
            for c in range(3):
                for row in range(4):
                    at = sent.window[name, c, row]
                    ref[at : at + TILE, :] = windows[(3 * n + c) * 4 + row]
    planes = [own[name][c, row] for row in range(4) for name in ("ae", "ah") for c in range(3)]
    edges[0:depth, :] = pack(planes, FULL_K)
    for n in range(3):
        at = plan.window_at + n * TILE
        edges[at : at + TILE, :] = pack(windows[16 * n : 16 * n + 16], WIN_K)
    for ref, at, mate in (
        (edges, plan.columns_at, plan.mate_at),
        (to_even, sent.density, sent.mate),
        (to_odd, sent.density, sent.mate),
    ):
        ref[at : at + 4, :] = den[0]
        ref[at + 4 : at + 8, :] = den[1]
        ref[at + 8 : at + 12, :] = reg[...].astype(jnp.float32)
        ref[at + 12 : at + 16, :] = jnp.zeros((4, LANES), jnp.float32)
        ref[mate : mate + 4, :] = mate_den[0]
        ref[mate + 4 : mate + 8, :] = mate_den[1]


def as_float(flag):
    return flag.astype(jnp.float32)


class Sides:
    def __init__(self, axis):
        index = lax.axis_index(axis)
        last = lax.axis_size(axis) - 1
        odd = lax.rem(index, 2)
        even = 1 - odd
        self.left = as_float(odd), as_float(even * (index > 0).astype(jnp.int32))
        self.right = as_float(even), as_float(odd * (index < last).astype(jnp.int32))

    @staticmethod
    def of(side, even, odd, at, count):
        return side[0] * even[at : at + count, :] + side[1] * odd[at : at + count, :]


class Rows:
    def __init__(self, depth, own, from_even, from_odd):
        self.sides = Sides("gx")
        self.sent = Sent(depth)
        self.depth = depth
        self.low, self.base = near_layers(depth)
        self.own = own
        self.even, self.odd = from_even, from_odd

    def of(self, row, at, count):
        side = self.sides.left if row < 0 else self.sides.right
        return self.sides.of(side, self.even, self.odd, at, count)

    def full(self, name, c, row):
        if 0 <= row < 4:
            return self.own[name][c, row]
        return self.of(row, self.sent.full[name, c, row + 2 if row < 0 else row - 4], self.depth)

    def window(self, name, c, row):
        sent = self.sent
        if 0 <= row < 4:
            low = self.low - self.base if name in ("e", "h") else self.low
            return self.own[name][c, row, low : low + TILE, :]
        if name in ("e", "h"):
            return self.of(row, sent.window[name, c, row % 4], TILE)
        if row in (-3, 6):
            return self.of(row, sent.third[name, c], TILE)
        return self.of(row, sent.full[name, c, row + 2 if row < 0 else row - 4] + self.low, TILE)


def combine_kernel(depth, even, odd, halo):
    plan = Edges(depth)
    sides = Sides("gy")
    for at, end, width in (
        (0, plan.window_at, FULL_K),
        (plan.window_at, plan.columns_at, WIN_K),
        (plan.columns_at, plan.rows, LANES // 2),
    ):
        from_left = lax.rem(lane_index(end - at), 2 * width) >= width
        left = sides.of(sides.left, even, odd, at, end - at)
        right = sides.of(sides.right, even, odd, at, end - at)
        halo[at:end, :] = jnp.where(from_left, left, right)


def columns_kernel(depth, den, reg, from_even, from_odd, halo, halo_even, halo_odd, columns, far):
    plan, sent = Edges(depth), Sent(depth)
    sides = Sides("gx")
    odd = as_float(lax.rem(lax.axis_index("gx"), 2))
    for lane, (own, even, away, at, mate) in enumerate(
        (
            (None, from_even, from_odd, sent.density, sent.mate),
            (halo, halo_even, halo_odd, plan.columns_at, plan.mate_at),
        )
    ):
        lanes = pl.ds(lane * LANES, LANES)
        below = sides.of(sides.left, even, away, at, 2 * TILE)
        above = sides.of(sides.right, even, away, at, 2 * TILE)
        zero_row = jnp.zeros((1, LANES), jnp.float32)
        for n in range(3):
            if own is None:
                here = den[n] if n < 2 else reg[...].astype(jnp.float32)
            else:
                here = own[at + 4 * n : at + 4 * n + 4, :]
            to = 16 * n
            columns[to : to + 1, lanes] = zero_row
            columns[to + 15 : to + 16, lanes] = zero_row
            first = last = zero_row
            if n < 2:
                first = sides.left[1] * away[mate + 4 * n + 3 : mate + 4 * n + 4, :]
                last = sides.right[1] * away[mate + 4 * n : mate + 4 * n + 1, :]
                far[2 * n + lane : 2 * n + lane + 1, :] = (1.0 - odd) * below[4 * n + 3 : 4 * n + 4] + odd * above[4 * n : 4 * n + 1]
            columns[to + 1 : to + 2, lanes] = first
            columns[to + 2 : to + 6, lanes] = below[4 * n : 4 * n + 4]
            columns[to + 6 : to + 10, lanes] = here
            columns[to + 10 : to + 14, lanes] = above[4 * n : 4 * n + 4]
            columns[to + 14 : to + 15, lanes] = last
    far[4:8, :] = jnp.zeros((4, LANES), jnp.float32)


def up_z(block):
    depth = block.shape[0]
    moved = pltpu.roll(block, depth - 1, 0)
    if depth == TILE:
        return moved - block
    edge = lax.broadcasted_iota(jnp.int32, block.shape, 0) == depth - 1
    return jnp.where(edge, 0.0, moved) - block


def down_z(block):
    moved = pltpu.roll(block, 1, 0)
    if block.shape[0] == TILE:
        return block - moved
    edge = lax.broadcasted_iota(jnp.int32, block.shape, 0) == 0
    return block - jnp.where(edge, 0.0, moved)


def up_y(block):
    return pltpu.roll(block, block.shape[1] - 1, 1) - block


def down_y(block):
    return block - pltpu.roll(block, 1, 1)


def curl_up(here, after):
    x, y, z = here
    return (up_y(z) - up_z(y), up_z(x) - (after[2] - z), (after[1] - y) - up_y(x))


def curl_down(here, before):
    x, y, z = here
    return (down_y(z) - down_z(y), down_z(x) - (z - before[2]), (y - before[1]) - down_y(x))


def blur(block):
    table = kernel_table(RAD)
    lanes, count = block.shape[1], block.shape[0]
    sums = [block]
    for b in range(1, RAD + 1):
        sums.append(pltpu.roll(block, b, 1) + pltpu.roll(block, lanes - b, 1))
    total = None
    for a in range(RAD + 1):
        part = sum(float(table[RAD + a, RAD + b]) * sums[b] for b in range(RAD + 1))
        if a:
            part = pltpu.roll(part, a, 0) + pltpu.roll(part, count - a, 0)
        total = part if total is None else total + part
    return total


class Halos:
    def __init__(self, depth, x_sides, own, even, odd):
        self.depth = depth
        self.plan = Edges(depth)
        self.x_sides = x_sides
        self.own, self.even, self.odd = own, even, odd

    def of(self, row, at, count):
        if 0 <= row < 4:
            return self.own[at : at + count, :]
        side = self.x_sides.left if row < 0 else self.x_sides.right
        return self.x_sides.of(side, self.even, self.odd, at, count)

    def full(self, name, c, row):
        return unroll(self.of(row, 0, self.depth), self.plan.full_slot(name, c, row) * 2 * FULL_K)

    def window(self, name, c, row):
        at, slot = self.plan.window_slot(name, c, row)
        return unroll(self.of(row, self.plan.window_at + at, TILE), slot * 2 * WIN_K)


def unroll(block, shift):
    return pltpu.roll(block, LANES - shift, 1) if shift else block


class Coefficients:
    def __init__(self, region, densities):
        self.design = (region == 2.0).astype(jnp.float32)
        self.absorbing = (region == 1.0).astype(jnp.float32)
        self.source = (region == 3.0).astype(jnp.float32)
        self.inverse, self.slope = [], []
        for density in densities:
            inner = jnp.tanh(SHARP * (blur(density) - LEVEL))
            projected = (CREST + inner) / SCALE
            self.slope.append(SHARP * (1.0 - inner * inner) / SCALE)
            self.inverse.append(1.0 / (1.0 + CONTRAST * self.design * projected))
        damp = ABSORB * self.absorbing
        self.keep = (1.0 - damp) / (1.0 + damp)
        self.gain = COURANT / (1.0 + damp)


def inside_masks(x_sides, y_sides):
    lane = lane_index(TILE, 2 * LANES)
    inside = jnp.where(lane < LANES, 1.0, jnp.where(lane < LANES + LANES // 2, sum(y_sides.right), sum(y_sides.left)))
    return {"own": inside, "below": inside * sum(x_sides.left), "above": inside * sum(x_sides.right)}


def where_row(row):
    return "own" if 0 <= row < 4 else ("below" if row < 0 else "above")


def spread(block, row, count=TILE):
    at = row + DEN_BASE
    return jnp.broadcast_to(block[at : at + 1, :], (count, block.shape[1]))


def near_kernel(
    depth, e, h, ae, ah, from_even, from_odd, halo, halo_even, halo_odd, columns, far,
    grad,
    ratio_rows,
):
    rows = Rows(depth, {"e": e, "h": h, "ae": ae, "ah": ah}, from_even, from_odd)
    halos = Halos(depth, rows.sides, halo, halo_even, halo_odd)
    wide = 2 * LANES
    centre = depth // 2
    low = rows.low

    def window(name, c, row):
        return jnp.concatenate([rows.window(name, c, row), halos.window(name, c, row)], 1)

    odd = lax.rem(lax.axis_index("gx"), 2)
    far_at = jnp.where(odd == 1, DEN_BASE - 5, DEN_BASE + 8)
    at_far = lax.broadcasted_iota(jnp.int32, (16, wide), 0) == far_at
    densities = []
    for layer in range(2):
        row = jnp.concatenate([far[2 * layer : 2 * layer + 1, :], far[2 * layer + 1 : 2 * layer + 2, :]], 1)
        densities.append(jnp.where(at_far, jnp.broadcast_to(row, (16, wide)), columns[16 * layer : 16 * layer + 16, :]))
    known = Coefficients(columns[32:48, :], densities)
    inverse, slope, design, source = known.inverse, known.slope, known.design, known.source
    keep_col, gain_col = known.keep, known.gain
    masks = inside_masks(rows.sides, Sides("gy"))
    steps = {key: COURANT * value for key, value in masks.items()}

    sub = lax.broadcasted_iota(jnp.int32, (TILE, wide), 0) + low

    def layered(row):
        first, second = spread(inverse[0], row), spread(inverse[1], row)
        return jnp.where(sub == centre, first, jnp.where(sub == centre + 1, second, 1.0))

    keep_win = {row: spread(keep_col, row) for row in range(-3, 7)}
    layer_win = {row: layered(row) for row in range(-3, 7)}
    gain_win = {row: spread(gain_col, row) * layer_win[row] * masks[where_row(row)] for row in range(-3, 7)}
    source_plane = (sub == centre - 1).astype(jnp.float32)
    amounts = [math.sin(OMEGA * (step + 1)) for step in range(2)]
    e0 = {row: [window("e", c, row) for c in range(3)] for row in range(-4, 8)}
    h0 = {row: [window("h", c, row) for c in range(3)] for row in range(-4, 7)}
    h1, e1, h2, drive1, drive2 = {}, {}, {}, {}, {}

    def minus_step(base, curl, row):
        step = steps[where_row(row)]
        return [b - step * c for b, c in zip(base, curl)]

    for row in range(-4, 7):
        h1[row] = minus_step(h0[row], curl_up(e0[row], e0[row + 1]), row)
    for row in range(-3, 7):
        drive = list(curl_down(h1[row], h1[row - 1]))
        at_source = source_plane * spread(source, row)
        drive[2] = drive[2] - amounts[0] * at_source
        drive1[row] = drive
        e1[row] = [keep_win[row] * b + gain_win[row] * d for b, d in zip(e0[row], drive)]
    for row in range(-3, 6):
        h2[row] = minus_step(h1[row], curl_up(e1[row], e1[row + 1]), row)
    for row in range(-2, 6):
        drive2[row] = list(curl_down(h2[row], h2[row - 1]))
        drive2[row][2] = drive2[row][2] - amounts[1] * source_plane * spread(source, row)
    a2 = {row: [window("ae", c, row) for c in range(3)] for row in range(-3, 7)}
    ga_win = {row: [gain_win[row] * v for v in a2[row]] for row in range(-3, 7)}
    bh_win = {}
    for row in range(-3, 6):
        mask = masks[where_row(row)]
        curl = curl_up(ga_win[row], ga_win[row + 1])
        bh_win[row] = [window("ah", c, row) + mask * curl[c] for c in range(3)]
    ratio_rows[...] = jnp.zeros(ratio_rows.shape, jnp.float32)
    for row in range(-2, 6):
        a1 = minus_step(
            [keep_win[row] * v for v in a2[row]], curl_down(bh_win[row], bh_win[row - 1]), row
        )
        total = sum(a2[row][c] * drive2[row][c] + a1[c] * drive1[row][c] for c in range(3))
        for layer in range(2):
            at = centre + layer - low
            ratio_rows[layer, row + DEN_BASE : row + DEN_BASE + 1, :] = total[at : at + 1, :]
    for layer in range(2):
        sensitivity = -ratio_rows[layer] * gain_col * inverse[layer] * inverse[layer]
        smoothed = blur(CONTRAST * design * sensitivity * slope[layer])
        grad[layer] = smoothed[DEN_BASE : DEN_BASE + 4, :LANES]


def full_kernel(
    depth, ae, ah, from_even, from_odd, halo, halo_even, halo_odd, columns,
    out_e, out_h,
    ga, bh, be, gb,
):
    rows = Rows(depth, {"ae": ae, "ah": ah}, from_even, from_odd)
    halos = Halos(depth, rows.sides, halo, halo_even, halo_odd)
    wide = 2 * LANES
    centre = depth // 2

    def full(name, c, row):
        return jnp.concatenate([rows.full(name, c, row), halos.full(name, c, row)], 1)

    known = Coefficients(columns[32:48, :], [columns[16 * layer : 16 * layer + 16, :] for layer in range(2)])
    inverse, absorbing = known.inverse, known.absorbing
    masks = inside_masks(rows.sides, Sides("gy"))
    steps = {key: COURANT * value for key, value in masks.items()}

    z = lax.broadcasted_iota(jnp.int32, (depth, wide), 0)
    zf = z.astype(jnp.float32)
    margin = float(depth // 8)
    ramp = jnp.maximum(jnp.maximum((margin - zf) / margin, (zf - (depth - 1 - margin)) / margin), 0.0)
    open_damp = ABSORB * ramp * ramp
    full_damp = open_damp + ABSORB
    gain_open, gain_abs = COURANT / (1.0 + open_damp), COURANT / (1.0 + full_damp)
    keep_open, keep_abs = (1.0 - open_damp) / (1.0 + open_damp), (1.0 - full_damp) / (1.0 + full_damp)

    def coefficient(row):
        flag = spread(absorbing, row, depth) > 0.5
        layers = jnp.where(
            z == centre,
            spread(inverse[0], row, depth),
            jnp.where(z == centre + 1, spread(inverse[1], row, depth), 1.0),
        )
        return jnp.where(flag, keep_abs, keep_open), jnp.where(flag, gain_abs, gain_open) * layers

    def stretch(block):
        return jnp.broadcast_to(block[:1, :], (depth, wide))

    masks = {key: stretch(value) for key, value in masks.items()}
    steps = {key: stretch(value) for key, value in steps.items()}

    for row in range(-2, 6):
        keep, gain = coefficient(row)
        for c in range(3):
            value = full("ae", c, row)
            ga[c, row + 2] = gain * value
            if -1 <= row <= 4:
                be[c, row + 1] = keep * value
    for row in range(-2, 5):
        curl = curl_up([ga[c, row + 2] for c in range(3)], [ga[c, row + 3] for c in range(3)])
        for c in range(3):
            bh[c, row + 2] = full("ah", c, row) + masks[where_row(row)] * curl[c]
    for row in range(-1, 5):
        keep, gain = coefficient(row)
        curl = curl_down([bh[c, row + 2] for c in range(3)], [bh[c, row + 1] for c in range(3)])
        for c in range(3):
            value = be[c, row + 1] - steps[where_row(row)] * curl[c]
            be[c, row + 1] = keep * value
            gb[c, row + 1] = gain * value
    for row in range(-1, 4):
        curl = curl_up([gb[c, row + 1] for c in range(3)], [gb[c, row + 2] for c in range(3)])
        for c in range(3):
            value = bh[c, row + 2] + masks[where_row(row)] * curl[c]
            bh[c, row + 2] = value
            if row >= 0:
                out_h[c, row] = value[:, :LANES]
    for row in range(4):
        curl = curl_down([bh[c, row + 2] for c in range(3)], [bh[c, row + 1] for c in range(3)])
        for c in range(3):
            out_e[c, row] = be[c, row + 1][:, :LANES] - COURANT * curl[c][:, :LANES]


def per_device(density, e_field, h_field, adj_e, adj_h, region):
    depth = e_field.shape[2]
    sent, plan = Sent(depth), Edges(depth)
    f32 = jnp.float32
    params = pltpu.CompilerParams(vmem_limit_bytes=32 * 1024 * 1024)
    shape = jax.ShapeDtypeStruct
    near = e_field.shape[:2] + (2 * TILE, LANES)
    mate_den = pair_permute(density, x_even)
    own = pl.pallas_call(
        functools.partial(load_kernel, depth),
        out_shape=(
            pltpu.VMEM(density.shape, f32),
            pltpu.VMEM(near, f32),
            pltpu.VMEM(near, f32),
            pltpu.VMEM(adj_e.shape, f32),
            pltpu.VMEM(adj_h.shape, f32),
            pltpu.VMEM(region.shape, region.dtype),
        ),
        in_specs=[pl.BlockSpec(memory_space=pltpu.HBM)] * 6,
        scratch_shapes=[pltpu.SemaphoreType.DMA((6,))],
        compiler_params=pltpu.CompilerParams(vmem_limit_bytes=LOAD_VMEM),
        name="load",
    )(density, e_field, h_field, adj_e, adj_h, region)
    fields = own[1:5]
    edges, to_even, to_odd = pl.pallas_call(
        functools.partial(first_kernel, depth),
        out_shape=(
            shape((plan.rows, LANES), f32),
            shape((sent.rows, LANES), f32),
            shape((sent.rows, LANES), f32),
        ),
        compiler_params=params,
        name="first",
    )(*own, mate_den)
    edges_odd = pair_permute(edges, y_odd)
    edges_even = pair_permute(edges, y_even)
    from_odd = pair_permute(to_odd, x_ring)
    from_even = pair_permute(to_even, x_even)
    halo = pl.pallas_call(
        functools.partial(combine_kernel, depth),
        out_shape=shape((plan.rows, LANES), f32),
        compiler_params=params,
        name="combine",
    )(edges_even, edges_odd)
    halo_odd = pair_permute(halo, x_odd)
    halo_even = pair_permute(halo, x_even)
    wide = 2 * LANES
    columns, far = pl.pallas_call(
        functools.partial(columns_kernel, depth),
        out_shape=(shape((48, wide), f32), shape((TILE, LANES), f32)),
        compiler_params=params,
        name="columns",
    )(own[0], own[5], from_even, from_odd, halo, halo_even, halo_odd)
    far = pair_permute(far, x_even)
    adj_e0, adj_h0 = pl.pallas_call(
        functools.partial(full_kernel, depth),
        out_shape=(shape(e_field.shape, f32), shape(e_field.shape, f32)),
        scratch_shapes=[
            pltpu.VMEM((3, 8, depth, wide), f32),
            pltpu.VMEM((3, 7, depth, wide), f32),
            pltpu.VMEM((3, 6, depth, wide), f32),
            pltpu.VMEM((3, 6, depth, wide), f32),
        ],
        compiler_params=params,
        name="full",
    )(*fields[2:], from_even, from_odd, halo, halo_even, halo_odd, columns)
    grad = pl.pallas_call(
        functools.partial(near_kernel, depth),
        out_shape=shape(density.shape, f32),
        scratch_shapes=[pltpu.VMEM((2, 16, wide), f32)],
        compiler_params=params,
        name="near",
    )(*fields, from_even, from_odd, halo, halo_even, halo_odd, columns, far)
    return grad, adj_e0, adj_h0


def solution(mesh):
    field = P(None, "gx", None, "gy")
    design = P(None, "gx", "gy")
    return jax.shard_map(
        per_device,
        mesh=mesh,
        in_specs=(design, field, field, field, field, P("gx", "gy")),
        out_specs=(design, field, field),
        check_vma=False,
    )
```

time: 26.3 us -> 18.5 us (0.70)
  local copies, waits for them, and re-layouts: 5.07 us -> 0 us
  waiting for transfers between devices: 7.22 us -> 4.42 us
  Pallas kernels: 2.71 us -> 4.32 us
  starting transfers between devices: 10.4 us -> 8.8 us
    unnamed x12 -> x0, local copies, waits for them, and re-layouts: 5.07 us -> none
    ppermute x6 -> x8, waiting for transfers between devices: 7.22 us -> 4.42 us  [pair_permute(): return lax.ppermute(block, ('gx', 'gy'), route)]
    pallas_call x3 -> x6, Pallas kernels: 2.71 us -> 4.32 us  [the longest x1 1.47 us: per_device(): pl.pallas_call(functools.partial(full_kernel, depth), out_shape=(shape(e_...]
    ppermute x6 -> x8, starting transfers between devices: 10.4 us -> 8.8 us  [pair_permute(): return lax.ppermute(block, ('gx', 'gy'), route)]
  transfers between devices with their start and end apart: 6 -> 8, of which waited for: 2 -> 2; matrix products, arithmetic and copies ran while one was open for 0% -> 0% of each run, Pallas kernels for 0% -> 15%
where the time goes in v2:
time: 18.5 us; the launch traced here: 18.2 us
  starting transfers between devices  8.8 us (48%)
  waiting for transfers between devices  4.42 us (24%)
  Pallas kernels  4.32 us (23%)
  between operations  0.69 us (4%)
    ppermute x8, starting transfers between devices, pair_permute(): return lax.ppermute(block, ('gx', 'gy'), route)  8.8 us
    ppermute x8, waiting for transfers between devices, pair_permute(): return lax.ppermute(block, ('gx', 'gy'), route)  4.42 us
    pallas_call x1, Pallas kernels, per_device(): pl.pallas_call(functools.partial(full_kernel, depth), out_shape=(shape(e_...  1.47 us
    pallas_call x1, Pallas kernels, per_device(): pl.pallas_call(functools.partial(near_kernel, depth), out_shape=shape(den...  1.41 us
    pallas_call x1, Pallas kernels, per_device(): pl.pallas_call(functools.partial(load_kernel, depth), out_shape=(pltpu.VM...  1.19 us
  transfers between devices with their start and end apart: 8, of which 2 were waited for; matrix products, arithmetic and copies ran while one was open for 0% of the time, Pallas kernels for 15%

profile of v2, /device:TPU:0, one launch (start us, length us, event | category | flops | bytes accessed | tf_op | source)
XLA Modules:
  0.0 18.2 jit_solution(7959729515398208959)
XLA Ops:
  0.6 0.5 %collective-permute-start = (f32[2,4,128]{2,1,0:T(4,128)}, f32[2,4,128]{2,1,0:T(4,128)S(1)}, u32[]{:S(2)}, u32[]{:S(2)}) collective-permute-start(f32[2,4,128]{2,1,0:T(4,128)} %den.1), channel_id=1, source_target_pairs={{0,4},{1,5},{2,6},{3,7},{4,0},{5,1},{6,2},{7,3},{8,12},{9,13},{10,... | collective-permute-start | bytes 12296 | tf_op jit(solution)/shard_map/ppermute | solution.py:49
  1.1 1.2 %load.1 = (f32[2,4,128]{2,1,0:T(4,128)S(1)}, f32[3,4,16,128]{3,2,1,0:T(8,128)S(1)}, f32[3,4,16,128]{3,2,1,0:T(8,128)S(1)}, f32[3,4,32,128]{3,2,1,0:T(8,128)S(1)}...) custom-call(f32[2,4,128]{2,1,0:T(4,128)} %den.1, f32[3,4,32,128]{3,2,1,0:T(8,128)} %e.1, f32[3,4,32,128]{3,2,1,0:T(8,128)} %h.1, ...), custom_call_target="tpu_custom_call" | custom-call | tf_op jit(solution)/shard_map/load/pallas_call | solution.py:566
  2.3 0.0 collective-permute-done.mate_den
  2.4 0.2 %first.1 = (f32[80,128]{1,0:T(8,128)S(1)}, f32[648,128]{1,0:T(8,128)S(1)}, f32[648,128]{1,0:T(8,128)S(1)}) custom-call(f32[2,4,128]{2,1,0:T(4,128)S(1)} %get-tuple-element.20.den, f32[3,4,16,128]{3,2,1,0:T(8,128)S(1)} %get-tuple-element.16.e, f32[3,4,16,128]{3,2,1,0:T(8,128)S(1)} %get-tuple-element.17.h, f32[3,4,32,128]{3,2,1,0:T(8,128)S(1)} %get-tuple-element.18.ae, ...), custom_call_target="tpu_custom_call" | custom-call | tf_op jit(solution)/shard_map/first/pallas_call | solution.py:582
  2.6 0.2 %collective-permute-start.1 = (f32[648,128]{1,0:T(8,128)S(1)}, f32[648,128]{1,0:T(8,128)S(1)}, u32[]{:S(2)}, u32[]{:S(2)}) collective-permute-start(f32[648,128]{1,0:T(8,128)S(1)} %get-tuple-element.22), channel_id=1, source_target_pairs={{0,4},{1,5},{2,6},{3,7},{4,0},{5,1},{6,2},{7,3},{8,12},{9,13},{10,... | collective-permute-start | bytes 995336 | tf_op jit(solution)/shard_map/ppermute | solution.py:49
  2.8 3.6 %collective-permute-start.2 = (f32[648,128]{1,0:T(8,128)S(1)}, f32[648,128]{1,0:T(8,128)S(1)}, u32[]{:S(2)}, u32[]{:S(2)}) collective-permute-start(f32[648,128]{1,0:T(8,128)S(1)} %get-tuple-element.23), channel_id=1, source_target_pairs={{0,28},{1,29},{2,30},{3,31},{4,8},{5,9},{6,10},{7,11},{8,4},{9,5},... | collective-permute-start | bytes 995336 | tf_op jit(solution)/shard_map/ppermute | solution.py:49
  6.4 1.6 %collective-permute-start.3 = (f32[80,128]{1,0:T(8,128)S(1)}, f32[80,128]{1,0:T(8,128)S(1)}, u32[]{:S(2)}, u32[]{:S(2)}) collective-permute-start(f32[80,128]{1,0:T(8,128)S(1)} %get-tuple-element.24), channel_id=1, source_target_pairs={{0,1},{1,0},{2,3},{3,2},{4,5},{5,4},{6,7},{7,6},{8,9},{9,8},{10,11... | collective-permute-start | bytes 122888 | tf_op jit(solution)/shard_map/ppermute | solution.py:49
  7.9 0.0 collective-permute-start.4
  7.9 2.4 %collective-permute-done.3.even = f32[80,128]{1,0:T(8,128)S(1)} collective-permute-done((f32[80,128]{1,0:T(8,128)S(1)}, f32[80,128]{1,0:T(8,128)S(1)}, u32[]{:S(2)}, u32[]{:S(2)}) %collective-permute-start.3) | collective-permute-done | bytes 40992 | tf_op jit(solution)/shard_map/ppermute | solution.py:49
  10.4 0.0 collective-permute-done.4.odd
  10.4 0.1 collective-permute-start.5
  10.5 2.8 %collective-permute-start.6 = (f32[80,128]{1,0:T(8,128)S(1)}, f32[80,128]{1,0:T(8,128)S(1)}, u32[]{:S(2)}, u32[]{:S(2)}) collective-permute-start(f32[80,128]{1,0:T(8,128)S(1)} %combine.1.halo), channel_id=1, source_target_pairs={{0,1},{1,0},{2,3},{3,2},{4,8},{5,9},{6,10},{7,11},{8,4},{9,5},{10,... | collective-permute-start | bytes 122888 | tf_op jit(solution)/shard_map/ppermute | solution.py:49
  13.2 0.0 collective-permute-done.5.halo_even
  13.2 2.0 %collective-permute-done.6.halo_odd = f32[80,128]{1,0:T(8,128)S(1)} collective-permute-done((f32[80,128]{1,0:T(8,128)S(1)}, f32[80,128]{1,0:T(8,128)S(1)}, u32[]{:S(2)}, u32[]{:S(2)}) %collective-permute-start.6) | collective-permute-done | bytes 40992 | tf_op jit(solution)/shard_map/ppermute | solution.py:49
  15.2 0.0 collective-permute-done.1.from_even
  15.2 0.0 collective-permute-done.2.from_odd
  15.3 0.1 collective-permute-start.7
  15.3 1.5 %full.1 = (f32[3,4,32,128]{3,2,1,0:T(8,128)}, f32[3,4,32,128]{3,2,1,0:T(8,128)}) custom-call(f32[3,4,32,128]{3,2,1,0:T(8,128)S(1)} %get-tuple-element.18.ae, f32[3,4,32,128]{3,2,1,0:T(8,128)S(1)} %get-tuple-element.19.ah, f32[648,128]{1,0:T(8,128)S(1)} %collective-permute-done.1.from_even, f32[648,128]{1,0:T(8,128)S(1)} %collective-permute-done.2.from_odd, ...), custom_call_target="tpu_custom_call" | custom-call | tf_op jit(solution)/shard_map/full/pallas_call | solution.py:612
  16.8 0.0 collective-permute-done.7.far
  16.8 1.4 %near.1 = f32[2,4,128]{2,1,0:T(4,128)} custom-call(f32[3,4,16,128]{3,2,1,0:T(8,128)S(1)} %get-tuple-element.16.e, f32[3,4,16,128]{3,2,1,0:T(8,128)S(1)} %get-tuple-element.17.h, f32[3,4,32,128]{3,2,1,0:T(8,128)S(1)} %get-tuple-element.18.ae, f32[3,4,32,128]{3,2,1,0:T(8,128)S(1)} %get-tuple-element.19.ah, f32[648,128]{1,0:T(8,128)S(1)} %collective-permute-done.1.from_even, ...), custom_call_target="tpu_custom_call" | custom-call | tf_op jit(solution)/shard_map/near/pallas_call | solution.py:624
  (2 shorter events, 0.0 us)
Async XLA Ops:
  0.6 1.7 %collective-permute-start = (f32[2,4,128]{2,1,0:T(4,128)}, f32[2,4,128]{2,1,0:T(4,128)S(1)}, u32[]{:S(2)}, u32[]{:S(2)}) collective-permute-start(f32[2,4,128]{2,1,0:T(4,128)} %den.1), channel_id=1, source_target_pairs={{0,4},{1,5},{2,6},{3,7},{4,0},{5,1},{6,2},{7,3},{8,12},{9,13},{10,... | collective-permute-start | bytes 12296 | tf_op jit(solution)/shard_map/ppermute | solution.py:49
  2.6 12.7 %collective-permute-start.1 = (f32[648,128]{1,0:T(8,128)S(1)}, f32[648,128]{1,0:T(8,128)S(1)}, u32[]{:S(2)}, u32[]{:S(2)}) collective-permute-start(f32[648,128]{1,0:T(8,128)S(1)} %get-tuple-element.22), channel_id=1, source_target_pairs={{0,4},{1,5},{2,6},{3,7},{4,0},{5,1},{6,2},{7,3},{8,12},{9,13},{10,... | collective-permute-start | bytes 995336 | tf_op jit(solution)/shard_map/ppermute | solution.py:49
  2.8 12.4 %collective-permute-start.2 = (f32[648,128]{1,0:T(8,128)S(1)}, f32[648,128]{1,0:T(8,128)S(1)}, u32[]{:S(2)}, u32[]{:S(2)}) collective-permute-start(f32[648,128]{1,0:T(8,128)S(1)} %get-tuple-element.23), channel_id=1, source_target_pairs={{0,28},{1,29},{2,30},{3,31},{4,8},{5,9},{6,10},{7,11},{8,4},{9,5},... | collective-permute-start | bytes 995336 | tf_op jit(solution)/shard_map/ppermute | solution.py:49
  6.4 4.0 %collective-permute-start.3 = (f32[80,128]{1,0:T(8,128)S(1)}, f32[80,128]{1,0:T(8,128)S(1)}, u32[]{:S(2)}, u32[]{:S(2)}) collective-permute-start(f32[80,128]{1,0:T(8,128)S(1)} %get-tuple-element.24), channel_id=1, source_target_pairs={{0,1},{1,0},{2,3},{3,2},{4,5},{5,4},{6,7},{7,6},{8,9},{9,8},{10,11... | collective-permute-start | bytes 122888 | tf_op jit(solution)/shard_map/ppermute | solution.py:49
  7.9 2.4 %collective-permute-start.4 = (f32[80,128]{1,0:T(8,128)S(1)}, f32[80,128]{1,0:T(8,128)S(1)}, u32[]{:S(2)}, u32[]{:S(2)}) collective-permute-start(f32[80,128]{1,0:T(8,128)S(1)} %get-tuple-element.24), channel_id=1, source_target_pairs={{0,4},{1,2},{2,1},{3,7},{4,0},{5,6},{6,5},{7,3},{8,12},{9,10},{10,... | collective-permute-start | bytes 122888 | tf_op jit(solution)/shard_map/ppermute | solution.py:49
  10.4 2.8 %collective-permute-start.5 = (f32[80,128]{1,0:T(8,128)S(1)}, f32[80,128]{1,0:T(8,128)S(1)}, u32[]{:S(2)}, u32[]{:S(2)}) collective-permute-start(f32[80,128]{1,0:T(8,128)S(1)} %combine.1.halo), channel_id=1, source_target_pairs={{0,4},{1,5},{2,6},{3,7},{4,0},{5,1},{6,2},{7,3},{8,12},{9,13},{10,... | collective-permute-start | bytes 122888 | tf_op jit(solution)/shard_map/ppermute | solution.py:49
  10.5 4.7 %collective-permute-start.6 = (f32[80,128]{1,0:T(8,128)S(1)}, f32[80,128]{1,0:T(8,128)S(1)}, u32[]{:S(2)}, u32[]{:S(2)}) collective-permute-start(f32[80,128]{1,0:T(8,128)S(1)} %combine.1.halo), channel_id=1, source_target_pairs={{0,1},{1,0},{2,3},{3,2},{4,8},{5,9},{6,10},{7,11},{8,4},{9,5},{10,... | collective-permute-start | bytes 122888 | tf_op jit(solution)/shard_map/ppermute | solution.py:49
  15.3 1.6 %collective-permute-start.7 = (f32[8,128]{1,0:T(8,128)S(1)}, f32[8,128]{1,0:T(8,128)S(1)}, u32[]{:S(2)}, u32[]{:S(2)}) collective-permute-start(f32[8,128]{1,0:T(8,128)S(1)} %get-tuple-element.26), channel_id=1, source_target_pairs={{0,4},{1,5},{2,6},{3,7},{4,0},{5,1},{6,2},{7,3},{8,12},{9,13},{10,... | collective-permute-start | bytes 12296 | tf_op jit(solution)/shard_map/ppermute | solution.py:49

commit v3 on v2

--- a/solution.py
+++ b/solution.py
@@ -69,26 +69,36 @@
     return (i, odd_swap(j)) if 0 < j < ny - 1 else (i ^ 1, j)
 
 
+PIECES = (
+    ("e", 1, (0, 1, 2), 6, -2, -2),
+    ("e", 2, (0, 1, 2), 6, -2, -2),
+    ("e", 3, (0, 1, 2), 5, -1, -2),
+    ("e", 4, (0, 1, 2), 4, 0, -2),
+    ("h", 1, (0, 1, 2), 5, -2, -2),
+    ("h", 2, (0, 1, 2), 5, -2, -2),
+    ("h", 3, (0, 1, 2), 4, -1, -2),
+    ("h", 4, (1, 2), 3, 0, 0),
+    ("ae", 3, (0, 1, 2), 3, 0, -1),
+    ("ah", 3, (1, 2), 2, 0, 0),
+    ("ah", 2, (0,), 3, -1, -1),
+)
+
+
 class Sent:
     def __init__(self, depth):
         self.full = {}
         at = 0
-        for name in ("ae", "ah"):
-            for c in range(3):
-                for near in range(2):
-                    self.full[name, c, near] = at
+        for name, far in (("ae", (0, 1, 2)), ("ah", (1, 2))):
+            for distance in (1, 2):
+                for c in (0, 1, 2) if distance == 1 else far:
+                    self.full[name, c, distance] = at
                     at += depth
-        self.third = {}
-        for name in ("ae", "ah"):
-            for c in range(3):
-                self.third[name, c] = at
-                at += TILE
-        self.window = {}
-        for name in ("e", "h"):
-            for c in range(3):
-                for row in range(4):
-                    self.window[name, c, row] = at
-                    at += TILE
+        self.pieces = {}
+        for name, distance, components, count, left, right in PIECES:
+            for c in components:
+                self.pieces[name, c, distance] = at, count, left, right
+                at += count
+        at = -(-at // TILE) * TILE
         self.density = at
         self.region = at + TILE
         self.mate = at + 2 * TILE
@@ -98,12 +108,15 @@
 FIELDS = ("ae", "ah", "e", "h")
 
 
+COLUMN_K = 8
+COLUMN_LANE = 104
+
+
 class Edges:
     def __init__(self, depth):
         self.window_at = depth
-        self.columns_at = depth + 3 * TILE
-        self.mate_at = self.columns_at + 2 * TILE
-        self.rows = self.mate_at + TILE
+        self.rows = depth + 3 * TILE
+        self.density, self.region, self.mate = 0, TILE, 2 * TILE
 
     def full_slot(self, name, c, row):
         return row % 4 * 6 + FIELDS.index(name) * 3 + c
@@ -165,37 +178,37 @@
     odd = lax.rem(lax.axis_index("gx"), 2)
     own = {"ae": ae, "ah": ah}
     windows = near_windows(depth, e, h, ae, ah)
+    centre = depth // 2
+    base = near_layers(depth)[1]
+    fields = {"ae": (ae, centre), "ah": (ah, centre), "e": (e, centre - base), "h": (h, centre - base)}
     for ref, right in ((to_even, 1 - odd), (to_odd, odd)):
-        start = right * (ae.shape[1] - 2)
-        third = 2 + right * (ae.shape[1] - 5)
-        for name in ("ae", "ah"):
-            for c in range(3):
-                for near in range(2):
-                    at = sent.full[name, c, near]
-                    ref[at : at + depth, :] = own[name][c, start + near]
-                at = sent.third[name, c]
-                ref[at : at + TILE, :] = own[name][c, third, low : low + TILE, :]
-        for n, name in ((2, "e"), (3, "h")):
-            for c in range(3):
-                for row in range(4):
-                    at = sent.window[name, c, row]
-                    ref[at : at + TILE, :] = windows[(3 * n + c) * 4 + row]
+        row_of = lambda distance: right * (ae.shape[1] + 1 - 2 * distance) + distance - 1
+        for (name, c, distance), at in sent.full.items():
+            ref[at : at + depth, :] = own[name][c, row_of(distance)]
+        for (name, c, distance), (at, count, from_left, from_right) in sent.pieces.items():
+            field, middle = fields[name]
+            row = row_of(distance)
+            value = field[c, row, middle + from_left : middle + from_left + count, :]
+            if from_left != from_right:
+                other = field[c, row, middle + from_right : middle + from_right + count, :]
+                value = jnp.where(jnp.full(value.shape, right, jnp.int32) == 1, value, other)
+            ref[at : at + count, :] = value
     planes = [own[name][c, row] for row in range(4) for name in ("ae", "ah") for c in range(3)]
-    edges[0:depth, :] = pack(planes, FULL_K)
+    blank = jnp.zeros((4, LANES), jnp.float32)
+    column = jnp.concatenate(
+        [den[0], den[1], reg[...].astype(jnp.float32), blank, mate_den[0], mate_den[1]]
+        + [blank] * ((depth - 3 * TILE) // 4),
+        0,
+    )
+    lane = lane_index(depth)
+    mine = (lane >= COLUMN_LANE - COLUMN_K) & (lane < COLUMN_LANE + COLUMN_K)
+    edges[0:depth, :] = jnp.where(mine, pltpu.roll(column, COLUMN_LANE, 1), pack(planes, FULL_K))
     for n in range(3):
         at = plan.window_at + n * TILE
         edges[at : at + TILE, :] = pack(windows[16 * n : 16 * n + 16], WIN_K)
-    for ref, at, mate in (
-        (edges, plan.columns_at, plan.mate_at),
-        (to_even, sent.density, sent.mate),
-        (to_odd, sent.density, sent.mate),
-    ):
-        ref[at : at + 4, :] = den[0]
-        ref[at + 4 : at + 8, :] = den[1]
-        ref[at + 8 : at + 12, :] = reg[...].astype(jnp.float32)
-        ref[at + 12 : at + 16, :] = jnp.zeros((4, LANES), jnp.float32)
-        ref[mate : mate + 4, :] = mate_den[0]
-        ref[mate + 4 : mate + 8, :] = mate_den[1]
+    for ref in (to_even, to_odd):
+        at = sent.density
+        ref[at : at + 3 * TILE, :] = column[: 3 * TILE]
 
 
 def as_float(flag):
@@ -232,60 +245,72 @@
     def full(self, name, c, row):
         if 0 <= row < 4:
             return self.own[name][c, row]
-        return self.of(row, self.sent.full[name, c, row + 2 if row < 0 else row - 4], self.depth)
+        distance = -row if row < 0 else row - 3
+        if (name, c, distance) not in self.sent.full:
+            return jnp.zeros((self.depth, LANES), jnp.float32)
+        return self.of(row, self.sent.full[name, c, distance], self.depth)
 
     def window(self, name, c, row):
         sent = self.sent
         if 0 <= row < 4:
             low = self.low - self.base if name in ("e", "h") else self.low
             return self.own[name][c, row, low : low + TILE, :]
-        if name in ("e", "h"):
-            return self.of(row, sent.window[name, c, row % 4], TILE)
-        if row in (-3, 6):
-            return self.of(row, sent.third[name, c], TILE)
-        return self.of(row, sent.full[name, c, row + 2 if row < 0 else row - 4] + self.low, TILE)
+        distance = -row if row < 0 else row - 3
+        if (name, c, distance) in sent.full:
+            return self.of(row, sent.full[name, c, distance] + self.low, TILE)
+        if (name, c, distance) not in sent.pieces:
+            return jnp.zeros((TILE, LANES), jnp.float32)
+        at, count, from_left, from_right = sent.pieces[name, c, distance]
+        at -= self.depth // 2 - self.low + (from_left if row < 0 else from_right)
+        return self.of(row, at, TILE)
 
 
 def combine_kernel(depth, even, odd, halo):
     plan = Edges(depth)
     sides = Sides("gy")
-    for at, end, width in (
-        (0, plan.window_at, FULL_K),
-        (plan.window_at, plan.columns_at, WIN_K),
-        (plan.columns_at, plan.rows, LANES // 2),
-    ):
-        from_left = lax.rem(lane_index(end - at), 2 * width) >= width
+    for at, end, width in ((0, plan.window_at, FULL_K), (plan.window_at, plan.rows, WIN_K)):
+        lane = lane_index(end - at)
+        from_left = lax.rem(lane, 2 * width) >= width
+        if at == 0:
+            beside = (lane >= COLUMN_LANE - COLUMN_K) & (lane < COLUMN_LANE + COLUMN_K)
+            from_left = jnp.where(beside, (lane < COLUMN_LANE).astype(jnp.int32), from_left.astype(jnp.int32)) == 1
         left = sides.of(sides.left, even, odd, at, end - at)
         right = sides.of(sides.right, even, odd, at, end - at)
         halo[at:end, :] = jnp.where(from_left, left, right)
 
 
 def columns_kernel(depth, den, reg, from_even, from_odd, halo, halo_even, halo_odd, columns, far):
-    plan, sent = Edges(depth), Sent(depth)
+    sent = Sent(depth)
     sides = Sides("gx")
     odd = as_float(lax.rem(lax.axis_index("gx"), 2))
-    for lane, (own, even, away, at, mate) in enumerate(
-        (
-            (None, from_even, from_odd, sent.density, sent.mate),
-            (halo, halo_even, halo_odd, plan.columns_at, plan.mate_at),
-        )
+    count = 3 * TILE
+
+    def beside(ref):
+        return pltpu.roll(ref[0:count, :], LANES - COLUMN_LANE, 1)
+
+    def within(ref):
+        return ref[sent.density : sent.density + count, :]
+
+    for lane, (own, even, away) in enumerate(
+        ((None, within(from_even), within(from_odd)), (beside(halo), beside(halo_even), beside(halo_odd)))
     ):
         lanes = pl.ds(lane * LANES, LANES)
-        below = sides.of(sides.left, even, away, at, 2 * TILE)
-        above = sides.of(sides.right, even, away, at, 2 * TILE)
+        below = sides.left[0] * even + sides.left[1] * away
+        above = sides.right[0] * even + sides.right[1] * away
         zero_row = jnp.zeros((1, LANES), jnp.float32)
+        mate = 2 * TILE
         for n in range(3):
             if own is None:
                 here = den[n] if n < 2 else reg[...].astype(jnp.float32)
             else:
-                here = own[at + 4 * n : at + 4 * n + 4, :]
+                here = own[4 * n : 4 * n + 4]
             to = 16 * n
             columns[to : to + 1, lanes] = zero_row
             columns[to + 15 : to + 16, lanes] = zero_row
             first = last = zero_row
             if n < 2:
-                first = sides.left[1] * away[mate + 4 * n + 3 : mate + 4 * n + 4, :]
-                last = sides.right[1] * away[mate + 4 * n : mate + 4 * n + 1, :]
+                first = sides.left[1] * away[mate + 4 * n + 3 : mate + 4 * n + 4]
+                last = sides.right[1] * away[mate + 4 * n : mate + 4 * n + 1]
                 far[2 * n + lane : 2 * n + lane + 1, :] = (1.0 - odd) * below[4 * n + 3 : 4 * n + 4] + odd * above[4 * n : 4 * n + 1]
             columns[to + 1 : to + 2, lanes] = first
             columns[to + 2 : to + 6, lanes] = below[4 * n : 4 * n + 4]
@@ -402,18 +427,23 @@
 
 
 def near_kernel(
-    depth, e, h, ae, ah, from_even, from_odd, halo, halo_even, halo_odd, columns, far,
-    grad,
-    ratio_rows,
+    depth, columns, far, done_e, done_h, near,
+    out_grad, out_e, out_h,
+    grad, ratio_rows, sems,
 ):
-    rows = Rows(depth, {"e": e, "h": h, "ae": ae, "ah": ah}, from_even, from_odd)
-    halos = Halos(depth, rows.sides, halo, halo_even, halo_odd)
+    copies = [
+        pltpu.make_async_copy(done_e, out_e, sems.at[0]),
+        pltpu.make_async_copy(done_h, out_h, sems.at[1]),
+        pltpu.make_async_copy(grad, out_grad, sems.at[2]),
+    ]
+    copies[0].start()
+    copies[1].start()
     wide = 2 * LANES
     centre = depth // 2
-    low = rows.low
-
-    def window(name, c, row):
-        return jnp.concatenate([rows.window(name, c, row), halos.window(name, c, row)], 1)
+    low = near_layers(depth)[0]
+
+    def given(n, row):
+        return [near[n, c, row + 3] for c in range(3)]
 
     odd = lax.rem(lax.axis_index("gx"), 2)
     far_at = jnp.where(odd == 1, DEN_BASE - 5, DEN_BASE + 8)
@@ -425,7 +455,7 @@
     known = Coefficients(columns[32:48, :], densities)
     inverse, slope, design, source = known.inverse, known.slope, known.design, known.source
     keep_col, gain_col = known.keep, known.gain
-    masks = inside_masks(rows.sides, Sides("gy"))
+    masks = inside_masks(Sides("gx"), Sides("gy"))
     steps = {key: COURANT * value for key, value in masks.items()}
 
     sub = lax.broadcasted_iota(jnp.int32, (TILE, wide), 0) + low
@@ -438,35 +468,27 @@
     layer_win = {row: layered(row) for row in range(-3, 7)}
     gain_win = {row: spread(gain_col, row) * layer_win[row] * masks[where_row(row)] for row in range(-3, 7)}
     source_plane = (sub == centre - 1).astype(jnp.float32)
-    amounts = [math.sin(OMEGA * (step + 1)) for step in range(2)]
-    e0 = {row: [window("e", c, row) for c in range(3)] for row in range(-4, 8)}
-    h0 = {row: [window("h", c, row) for c in range(3)] for row in range(-4, 7)}
     h1, e1, h2, drive1, drive2 = {}, {}, {}, {}, {}
 
     def minus_step(base, curl, row):
         step = steps[where_row(row)]
         return [b - step * c for b, c in zip(base, curl)]
 
-    for row in range(-4, 7):
-        h1[row] = minus_step(h0[row], curl_up(e0[row], e0[row + 1]), row)
     for row in range(-3, 7):
-        drive = list(curl_down(h1[row], h1[row - 1]))
-        at_source = source_plane * spread(source, row)
-        drive[2] = drive[2] - amounts[0] * at_source
-        drive1[row] = drive
-        e1[row] = [keep_win[row] * b + gain_win[row] * d for b, d in zip(e0[row], drive)]
+        h1[row], drive1[row] = given(0, row), given(1, row)
+        e1[row] = [kept + gain_win[row] * d for kept, d in zip(given(2, row), drive1[row])]
     for row in range(-3, 6):
         h2[row] = minus_step(h1[row], curl_up(e1[row], e1[row + 1]), row)
     for row in range(-2, 6):
         drive2[row] = list(curl_down(h2[row], h2[row - 1]))
-        drive2[row][2] = drive2[row][2] - amounts[1] * source_plane * spread(source, row)
-    a2 = {row: [window("ae", c, row) for c in range(3)] for row in range(-3, 7)}
+        drive2[row][2] = drive2[row][2] - math.sin(OMEGA * 2.0) * source_plane * spread(source, row)
+    a2 = {row: given(3, row) for row in range(-3, 7)}
     ga_win = {row: [gain_win[row] * v for v in a2[row]] for row in range(-3, 7)}
     bh_win = {}
     for row in range(-3, 6):
         mask = masks[where_row(row)]
         curl = curl_up(ga_win[row], ga_win[row + 1])
-        bh_win[row] = [window("ah", c, row) + mask * curl[c] for c in range(3)]
+        bh_win[row] = [v + mask * d for v, d in zip(given(4, row), curl)]
     ratio_rows[...] = jnp.zeros(ratio_rows.shape, jnp.float32)
     for row in range(-2, 6):
         a1 = minus_step(
@@ -480,14 +502,17 @@
         sensitivity = -ratio_rows[layer] * gain_col * inverse[layer] * inverse[layer]
         smoothed = blur(CONTRAST * design * sensitivity * slope[layer])
         grad[layer] = smoothed[DEN_BASE : DEN_BASE + 4, :LANES]
+    copies[2].start()
+    for copy in copies:
+        copy.wait()
 
 
 def full_kernel(
-    depth, ae, ah, from_even, from_odd, halo, halo_even, halo_odd, columns,
-    out_e, out_h,
+    depth, e, h, ae, ah, from_even, from_odd, halo, halo_even, halo_odd, columns,
+    out_e, out_h, near,
     ga, bh, be, gb,
 ):
-    rows = Rows(depth, {"ae": ae, "ah": ah}, from_even, from_odd)
+    rows = Rows(depth, {"e": e, "h": h, "ae": ae, "ah": ah}, from_even, from_odd)
     halos = Halos(depth, rows.sides, halo, halo_even, halo_odd)
     wide = 2 * LANES
     centre = depth // 2
@@ -499,6 +524,29 @@
     inverse, absorbing = known.inverse, known.absorbing
     masks = inside_masks(rows.sides, Sides("gy"))
     steps = {key: COURANT * value for key, value in masks.items()}
+
+    def window(name, c, row):
+        return jnp.concatenate([rows.window(name, c, row), halos.window(name, c, row)], 1)
+
+    sub = lax.broadcasted_iota(jnp.int32, (TILE, wide), 0) + rows.low
+    at_source = (sub == centre - 1).astype(jnp.float32) * math.sin(OMEGA)
+    fields, magnetic = {}, {}
+    for row in range(-4, 8):
+        fields[row] = [window("e", c, row) for c in range(3)]
+    for row in range(-4, 7):
+        curl = curl_up(fields[row], fields[row + 1])
+        magnetic[row] = [window("h", c, row) - steps[where_row(row)] * curl[c] for c in range(3)]
+    for row in range(-3, 7):
+        drive = list(curl_down(magnetic[row], magnetic[row - 1]))
+        drive[2] = drive[2] - at_source * spread(known.source, row)
+        keep = spread(known.keep, row)
+        for c in range(3):
+            near[0, c, row + 3] = magnetic[row][c]
+            near[1, c, row + 3] = drive[c]
+            near[2, c, row + 3] = keep * fields[row][c]
+            near[3, c, row + 3] = window("ae", c, row)
+            if row < 6:
+                near[4, c, row + 3] = window("ah", c, row)
 
     z = lax.broadcasted_iota(jnp.int32, (depth, wide), 0)
     zf = z.astype(jnp.float32)
@@ -591,7 +639,7 @@
     )(*own, mate_den)
     edges_odd = pair_permute(edges, y_odd)
     edges_even = pair_permute(edges, y_even)
-    from_odd = pair_permute(to_odd, x_ring)
+    from_odd = pair_permute(to_odd, x_odd)
     from_even = pair_permute(to_even, x_even)
     halo = pl.pallas_call(
         functools.partial(combine_kernel, depth),
@@ -609,9 +657,13 @@
         name="columns",
     )(own[0], own[5], from_even, from_odd, halo, halo_even, halo_odd)
     far = pair_permute(far, x_even)
-    adj_e0, adj_h0 = pl.pallas_call(
+    done = pl.pallas_call(
         functools.partial(full_kernel, depth),
-        out_shape=(shape(e_field.shape, f32), shape(e_field.shape, f32)),
+        out_shape=(
+            pltpu.VMEM(e_field.shape, f32),
+            pltpu.VMEM(e_field.shape, f32),
+            pltpu.VMEM((5, 3, 10, TILE, wide), f32),
+        ),
         scratch_shapes=[
             pltpu.VMEM((3, 8, depth, wide), f32),
             pltpu.VMEM((3, 7, depth, wide), f32),
@@ -620,15 +672,19 @@
         ],
         compiler_params=params,
         name="full",
-    )(*fields[2:], from_even, from_odd, halo, halo_even, halo_odd, columns)
-    grad = pl.pallas_call(
+    )(*fields, from_even, from_odd, halo, halo_even, halo_odd, columns)
+    return pl.pallas_call(
         functools.partial(near_kernel, depth),
-        out_shape=shape(density.shape, f32),
-        scratch_shapes=[pltpu.VMEM((2, 16, wide), f32)],
+        out_shape=(shape(density.shape, f32), shape(e_field.shape, f32), shape(e_field.shape, f32)),
+        out_specs=[pl.BlockSpec(memory_space=pltpu.HBM)] * 3,
+        scratch_shapes=[
+            pltpu.VMEM(density.shape, f32),
+            pltpu.VMEM((2, 16, wide), f32),
+            pltpu.SemaphoreType.DMA((3,)),
+        ],
         compiler_params=params,
         name="near",
-    )(*fields, from_even, from_odd, halo, halo_even, halo_odd, columns, far)
-    return grad, adj_e0, adj_h0
+    )(columns, far, *done)
 
 
 def solution(mesh):

time: 18.5 us -> 17.4 us (0.941)
  waiting for transfers between devices: 4.42 us -> 3.82 us
  Pallas kernels: 4.32 us -> 3.76 us
    pallas_call x2, Pallas kernels: 2.88 us -> 2.24 us  [the longest x1 1.21 us: per_device(): pl.pallas_call(functools.partial(near_kernel, depth), out_shape=(shape(de...]
    ppermute x8, waiting for transfers between devices: 4.42 us -> 3.82 us  [pair_permute(): return lax.ppermute(block, ('gx', 'gy'), route)]
  transfers between devices with their start and end apart: 8 -> 8, of which waited for: 2 -> 3; matrix products, arithmetic and copies ran while one was open for 0% -> 0% of each run, Pallas kernels for 15% -> 13%
where the time goes in v3:
time: 17.4 us; the launch traced here: 17.2 us
  starting transfers between devices  8.96 us (51%)
  waiting for transfers between devices  3.82 us (22%)
  Pallas kernels  3.76 us (22%)
  between operations  0.68 us (4%)
    ppermute x8, starting transfers between devices, pair_permute(): return lax.ppermute(block, ('gx', 'gy'), route)  8.96 us
    ppermute x8, waiting for transfers between devices, pair_permute(): return lax.ppermute(block, ('gx', 'gy'), route)  3.82 us
    pallas_call x1, Pallas kernels, per_device(): pl.pallas_call(functools.partial(near_kernel, depth), out_shape=(shape(de...  1.21 us
    pallas_call x1, Pallas kernels, per_device(): pl.pallas_call(functools.partial(load_kernel, depth), out_shape=(pltpu.VM...  1.19 us
    pallas_call x1, Pallas kernels, per_device(): pl.pallas_call(functools.partial(full_kernel, depth), out_shape=(pltpu.VM...  1.03 us
  transfers between devices with their start and end apart: 8, of which 3 were waited for; matrix products, arithmetic and copies ran while one was open for 0% of the time, Pallas kernels for 13%

profile of v3, /device:TPU:0, one launch (start us, length us, event | category | flops | bytes accessed | tf_op | source)
XLA Modules:
  0.0 17.2 jit_solution(13246149729188840693)
XLA Ops:
  0.6 0.5 %collective-permute-start = (f32[2,4,128]{2,1,0:T(4,128)}, f32[2,4,128]{2,1,0:T(4,128)S(1)}, u32[]{:S(2)}, u32[]{:S(2)}) collective-permute-start(f32[2,4,128]{2,1,0:T(4,128)} %den.1), channel_id=1, source_target_pairs={{0,4},{1,5},{2,6},{3,7},{4,0},{5,1},{6,2},{7,3},{8,12},{9,13},{10,... | collective-permute-start | bytes 12296 | tf_op jit(solution)/shard_map/ppermute | solution.py:49
  1.1 1.2 %load.1 = (f32[2,4,128]{2,1,0:T(4,128)S(1)}, f32[3,4,16,128]{3,2,1,0:T(8,128)S(1)}, f32[3,4,16,128]{3,2,1,0:T(8,128)S(1)}, f32[3,4,32,128]{3,2,1,0:T(8,128)S(1)}...) custom-call(f32[2,4,128]{2,1,0:T(4,128)} %den.1, f32[3,4,32,128]{3,2,1,0:T(8,128)} %e.1, f32[3,4,32,128]{3,2,1,0:T(8,128)} %h.1, ...), custom_call_target="tpu_custom_call" | custom-call | tf_op jit(solution)/shard_map/load/pallas_call | solution.py:614
  2.3 0.0 collective-permute-done.mate_den
  2.4 0.2 %first.1 = (f32[56,128]{1,0:T(8,128)S(1)}, f32[504,128]{1,0:T(8,128)S(1)}, f32[504,128]{1,0:T(8,128)S(1)}) custom-call(f32[2,4,128]{2,1,0:T(4,128)S(1)} %get-tuple-element.17.den, f32[3,4,16,128]{3,2,1,0:T(8,128)S(1)} %get-tuple-element.19.e, f32[3,4,16,128]{3,2,1,0:T(8,128)S(1)} %get-tuple-element.20.h, f32[3,4,32,128]{3,2,1,0:T(8,128)S(1)} %get-tuple-element.21.ae, ...), custom_call_target="tpu_custom_call" | custom-call | tf_op jit(solution)/shard_map/first/pallas_call | solution.py:630
  2.6 0.2 %collective-permute-start.1 = (f32[504,128]{1,0:T(8,128)S(1)}, f32[504,128]{1,0:T(8,128)S(1)}, u32[]{:S(2)}, u32[]{:S(2)}) collective-permute-start(f32[504,128]{1,0:T(8,128)S(1)} %get-tuple-element.23), channel_id=1, source_target_pairs={{0,4},{1,5},{2,6},{3,7},{4,0},{5,1},{6,2},{7,3},{8,12},{9,13},{10,... | collective-permute-start | bytes 774152 | tf_op jit(solution)/shard_map/ppermute | solution.py:49
  2.8 2.9 %collective-permute-start.2 = (f32[504,128]{1,0:T(8,128)S(1)}, f32[504,128]{1,0:T(8,128)S(1)}, u32[]{:S(2)}, u32[]{:S(2)}) collective-permute-start(f32[504,128]{1,0:T(8,128)S(1)} %get-tuple-element.24), channel_id=1, source_target_pairs={{0,1},{1,0},{2,3},{3,2},{4,8},{5,9},{6,10},{7,11},{8,4},{9,5},{10,... | collective-permute-start | bytes 774152 | tf_op jit(solution)/shard_map/ppermute | solution.py:49
  5.7 0.0 collective-permute-start.4
  5.8 3.1 %collective-permute-start.3 = (f32[56,128]{1,0:T(8,128)S(1)}, f32[56,128]{1,0:T(8,128)S(1)}, u32[]{:S(2)}, u32[]{:S(2)}) collective-permute-start(f32[56,128]{1,0:T(8,128)S(1)} %get-tuple-element.25), channel_id=1, source_target_pairs={{0,1},{1,0},{2,3},{3,2},{4,5},{5,4},{6,7},{7,6},{8,9},{9,8},{10,11... | collective-permute-start | bytes 86024 | tf_op jit(solution)/shard_map/ppermute | solution.py:49
  8.9 0.0 collective-permute-done.4.odd
  8.9 1.8 %collective-permute-done.3.even = f32[56,128]{1,0:T(8,128)S(1)} collective-permute-done((f32[56,128]{1,0:T(8,128)S(1)}, f32[56,128]{1,0:T(8,128)S(1)}, u32[]{:S(2)}, u32[]{:S(2)}) %collective-permute-start.3) | collective-permute-done | bytes 28704 | tf_op jit(solution)/shard_map/ppermute | solution.py:49
  10.8 2.1 %collective-permute-start.6 = (f32[56,128]{1,0:T(8,128)S(1)}, f32[56,128]{1,0:T(8,128)S(1)}, u32[]{:S(2)}, u32[]{:S(2)}) collective-permute-start(f32[56,128]{1,0:T(8,128)S(1)} %combine.1.halo), channel_id=1, source_target_pairs={{0,1},{1,0},{2,3},{3,2},{4,8},{5,9},{6,10},{7,11},{8,4},{9,5},{10,... | collective-permute-start | bytes 86024 | tf_op jit(solution)/shard_map/ppermute | solution.py:49
  12.9 0.0 collective-permute-start.5
  12.9 1.8 %collective-permute-done.6.halo_odd = f32[56,128]{1,0:T(8,128)S(1)} collective-permute-done((f32[56,128]{1,0:T(8,128)S(1)}, f32[56,128]{1,0:T(8,128)S(1)}, u32[]{:S(2)}, u32[]{:S(2)}) %collective-permute-start.6) | collective-permute-done | bytes 28704 | tf_op jit(solution)/shard_map/ppermute | solution.py:49
  14.7 0.0 collective-permute-done.5.halo_even
  14.7 0.0 collective-permute-done.1.from_even
  14.7 0.0 collective-permute-done.2.from_odd
  14.7 0.1 columns.1
  14.8 0.0 collective-permute-start.7
  14.9 1.0 %full.1 = (f32[3,4,32,128]{3,2,1,0:T(8,128)S(1)}, f32[3,4,32,128]{3,2,1,0:T(8,128)S(1)}, f32[5,3,10,8,256]{4,3,2,1,0:T(8,128)S(1)}) custom-call(f32[3,4,16,128]{3,2,1,0:T(8,128)S(1)} %get-tuple-element.19.e, f32[3,4,16,128]{3,2,1,0:T(8,128)S(1)} %get-tuple-element.20.h, f32[3,4,32,128]{3,2,1,0:T(8,128)S(1)} %get-tuple-element.21.ae, ...), custom_call_target="tpu_custom_call" | custom-call | tf_op jit(solution)/shard_map/full/pallas_call | solution.py:660
  15.9 0.1 collective-permute-done.7.far
  16.0 1.2 %near.1 = (f32[2,4,128]{2,1,0:T(4,128)}, f32[3,4,32,128]{3,2,1,0:T(8,128)}, f32[3,4,32,128]{3,2,1,0:T(8,128)}) custom-call(f32[48,256]{1,0:T(8,128)S(1)} %get-tuple-element.26.columns, f32[8,128]{1,0:T(8,128)S(1)} %collective-permute-done.7.far, f32[3,4,32,128]{3,2,1,0:T(8,128)S(1)} %get-tuple-element.28.done_e, ...), custom_call_target="tpu_custom_call" | custom-call | tf_op jit(solution)/shard_map/near/pallas_call | solution.py:676
  (1 shorter events, 0.0 us)
Async XLA Ops:
  0.6 1.7 %collective-permute-start = (f32[2,4,128]{2,1,0:T(4,128)}, f32[2,4,128]{2,1,0:T(4,128)S(1)}, u32[]{:S(2)}, u32[]{:S(2)}) collective-permute-start(f32[2,4,128]{2,1,0:T(4,128)} %den.1), channel_id=1, source_target_pairs={{0,4},{1,5},{2,6},{3,7},{4,0},{5,1},{6,2},{7,3},{8,12},{9,13},{10,... | collective-permute-start | bytes 12296 | tf_op jit(solution)/shard_map/ppermute | solution.py:49
  2.6 12.1 %collective-permute-start.1 = (f32[504,128]{1,0:T(8,128)S(1)}, f32[504,128]{1,0:T(8,128)S(1)}, u32[]{:S(2)}, u32[]{:S(2)}) collective-permute-start(f32[504,128]{1,0:T(8,128)S(1)} %get-tuple-element.23), channel_id=1, source_target_pairs={{0,4},{1,5},{2,6},{3,7},{4,0},{5,1},{6,2},{7,3},{8,12},{9,13},{10,... | collective-permute-start | bytes 774152 | tf_op jit(solution)/shard_map/ppermute | solution.py:49
  2.8 11.9 %collective-permute-start.2 = (f32[504,128]{1,0:T(8,128)S(1)}, f32[504,128]{1,0:T(8,128)S(1)}, u32[]{:S(2)}, u32[]{:S(2)}) collective-permute-start(f32[504,128]{1,0:T(8,128)S(1)} %get-tuple-element.24), channel_id=1, source_target_pairs={{0,1},{1,0},{2,3},{3,2},{4,8},{5,9},{6,10},{7,11},{8,4},{9,5},{10,... | collective-permute-start | bytes 774152 | tf_op jit(solution)/shard_map/ppermute | solution.py:49
  5.7 3.2 %collective-permute-start.4 = (f32[56,128]{1,0:T(8,128)S(1)}, f32[56,128]{1,0:T(8,128)S(1)}, u32[]{:S(2)}, u32[]{:S(2)}) collective-permute-start(f32[56,128]{1,0:T(8,128)S(1)} %get-tuple-element.25), channel_id=1, source_target_pairs={{0,4},{1,2},{2,1},{3,7},{4,0},{5,6},{6,5},{7,3},{8,12},{9,10},{10,... | collective-permute-start | bytes 86024 | tf_op jit(solution)/shard_map/ppermute | solution.py:49
  5.8 5.0 %collective-permute-start.3 = (f32[56,128]{1,0:T(8,128)S(1)}, f32[56,128]{1,0:T(8,128)S(1)}, u32[]{:S(2)}, u32[]{:S(2)}) collective-permute-start(f32[56,128]{1,0:T(8,128)S(1)} %get-tuple-element.25), channel_id=1, source_target_pairs={{0,1},{1,0},{2,3},{3,2},{4,5},{5,4},{6,7},{7,6},{8,9},{9,8},{10,11... | collective-permute-start | bytes 86024 | tf_op jit(solution)/shard_map/ppermute | solution.py:49
  10.8 3.9 %collective-permute-start.6 = (f32[56,128]{1,0:T(8,128)S(1)}, f32[56,128]{1,0:T(8,128)S(1)}, u32[]{:S(2)}, u32[]{:S(2)}) collective-permute-start(f32[56,128]{1,0:T(8,128)S(1)} %combine.1.halo), channel_id=1, source_target_pairs={{0,1},{1,0},{2,3},{3,2},{4,8},{5,9},{6,10},{7,11},{8,4},{9,5},{10,... | collective-permute-start | bytes 86024 | tf_op jit(solution)/shard_map/ppermute | solution.py:49
  12.9 1.9 %collective-permute-start.5 = (f32[56,128]{1,0:T(8,128)S(1)}, f32[56,128]{1,0:T(8,128)S(1)}, u32[]{:S(2)}, u32[]{:S(2)}) collective-permute-start(f32[56,128]{1,0:T(8,128)S(1)} %combine.1.halo), channel_id=1, source_target_pairs={{0,4},{1,5},{2,6},{3,7},{4,0},{5,1},{6,2},{7,3},{8,12},{9,13},{10,... | collective-permute-start | bytes 86024 | tf_op jit(solution)/shard_map/ppermute | solution.py:49
  14.8 1.2 %collective-permute-start.7 = (f32[8,128]{1,0:T(8,128)S(1)}, f32[8,128]{1,0:T(8,128)S(1)}, u32[]{:S(2)}, u32[]{:S(2)}) collective-permute-start(f32[8,128]{1,0:T(8,128)S(1)} %get-tuple-element.27), channel_id=1, source_target_pairs={{0,4},{1,5},{2,6},{3,7},{4,0},{5,1},{6,2},{7,3},{8,12},{9,13},{10,... | collective-permute-start | bytes 12296 | tf_op jit(solution)/shard_map/ppermute | solution.py:49

commit v4 on v3

--- a/solution.py
+++ b/solution.py
@@ -58,7 +58,9 @@
 
 
 def x_ring(i, j, nx, ny):
-    return odd_swap(i) % nx, j
+    if 0 < i < nx - 1:
+        return odd_swap(i), j
+    return (i, odd_swap(j)) if 0 < j < ny - 1 else (nx - 1 - i, j)
 
 
 def y_even(i, j, nx, ny):
@@ -265,7 +267,7 @@
         return self.of(row, at, TILE)
 
 
-def combine_kernel(depth, even, odd, halo):
+def combine_kernel(depth, odd, even, halo):
     plan = Edges(depth)
     sides = Sides("gy")
     for at, end, width in ((0, plan.window_at, FULL_K), (plan.window_at, plan.rows, WIN_K)):
@@ -279,7 +281,7 @@
         halo[at:end, :] = jnp.where(from_left, left, right)
 
 
-def columns_kernel(depth, den, reg, from_even, from_odd, halo, halo_even, halo_odd, columns, far):
+def columns_kernel(depth, den, reg, from_odd, from_even, halo, halo_even, halo_odd, columns, far):
     sent = Sent(depth)
     sides = Sides("gx")
     odd = as_float(lax.rem(lax.axis_index("gx"), 2))
@@ -637,8 +639,8 @@
         compiler_params=params,
         name="first",
     )(*own, mate_den)
+    edges_even = pair_permute(edges, y_even)
     edges_odd = pair_permute(edges, y_odd)
-    edges_even = pair_permute(edges, y_even)
     from_odd = pair_permute(to_odd, x_odd)
     from_even = pair_permute(to_even, x_even)
     halo = pl.pallas_call(
@@ -646,7 +648,7 @@
         out_shape=shape((plan.rows, LANES), f32),
         compiler_params=params,
         name="combine",
-    )(edges_even, edges_odd)
+    )(edges_odd, edges_even)
     halo_odd = pair_permute(halo, x_odd)
     halo_even = pair_permute(halo, x_even)
     wide = 2 * LANES
@@ -655,7 +657,7 @@
         out_shape=(shape((48, wide), f32), shape((TILE, LANES), f32)),
         compiler_params=params,
         name="columns",
-    )(own[0], own[5], from_even, from_odd, halo, halo_even, halo_odd)
+    )(own[0], own[5], from_odd, from_even, halo, halo_even, halo_odd)
     far = pair_permute(far, x_even)
     done = pl.pallas_call(
         functools.partial(full_kernel, depth),

time: 17.4 us -> 17 us (0.977)
  starting transfers between devices: 8.96 us -> 7.07 us
  waiting for transfers between devices: 3.82 us -> 5.28 us
    ppermute x8, starting transfers between devices: 8.96 us -> 7.07 us  [pair_permute(): return lax.ppermute(block, ('gx', 'gy'), route)]
    ppermute x8, waiting for transfers between devices: 3.82 us -> 5.28 us  [pair_permute(): return lax.ppermute(block, ('gx', 'gy'), route)]
where the time goes in v4:
time: 17 us; the launch traced here: 16.8 us
  starting transfers between devices  7.07 us (42%)
  waiting for transfers between devices  5.28 us (31%)
  Pallas kernels  3.77 us (22%)
  between operations  0.69 us (4%)
    ppermute x8, starting transfers between devices, pair_permute(): return lax.ppermute(block, ('gx', 'gy'), route)  7.07 us
    ppermute x8, waiting for transfers between devices, pair_permute(): return lax.ppermute(block, ('gx', 'gy'), route)  5.28 us
    pallas_call x1, Pallas kernels, per_device(): pl.pallas_call(functools.partial(near_kernel, depth), out_shape=(shape(de...  1.21 us
    pallas_call x1, Pallas kernels, per_device(): pl.pallas_call(functools.partial(load_kernel, depth), out_shape=(pltpu.VM...  1.19 us
    pallas_call x1, Pallas kernels, per_device(): pl.pallas_call(functools.partial(full_kernel, depth), out_shape=(pltpu.VM...  1.04 us
  transfers between devices with their start and end apart: 8, of which 3 were waited for; matrix products, arithmetic and copies ran while one was open for 0% of the time, Pallas kernels for 13%

profile of v4, /device:TPU:0, one launch (start us, length us, event | category | flops | bytes accessed | tf_op | source)
XLA Modules:
  0.0 16.8 jit_solution(1290021218978699718)
XLA Ops:
  0.6 0.5 %collective-permute-start = (f32[2,4,128]{2,1,0:T(4,128)}, f32[2,4,128]{2,1,0:T(4,128)S(1)}, u32[]{:S(2)}, u32[]{:S(2)}) collective-permute-start(f32[2,4,128]{2,1,0:T(4,128)} %den.1), channel_id=1, source_target_pairs={{0,4},{1,5},{2,6},{3,7},{4,0},{5,1},{6,2},{7,3},{8,12},{9,13},{10,... | collective-permute-start | bytes 12296 | tf_op jit(solution)/shard_map/ppermute | solution.py:49
  1.1 1.2 %load.1 = (f32[2,4,128]{2,1,0:T(4,128)S(1)}, f32[3,4,16,128]{3,2,1,0:T(8,128)S(1)}, f32[3,4,16,128]{3,2,1,0:T(8,128)S(1)}, f32[3,4,32,128]{3,2,1,0:T(8,128)S(1)}...) custom-call(f32[2,4,128]{2,1,0:T(4,128)} %den.1, f32[3,4,32,128]{3,2,1,0:T(8,128)} %e.1, f32[3,4,32,128]{3,2,1,0:T(8,128)} %h.1, ...), custom_call_target="tpu_custom_call" | custom-call | tf_op jit(solution)/shard_map/load/pallas_call | solution.py:616
  2.3 0.0 collective-permute-done.mate_den
  2.4 0.2 %first.1 = (f32[56,128]{1,0:T(8,128)S(1)}, f32[504,128]{1,0:T(8,128)S(1)}, f32[504,128]{1,0:T(8,128)S(1)}) custom-call(f32[2,4,128]{2,1,0:T(4,128)S(1)} %get-tuple-element.17.den, f32[3,4,16,128]{3,2,1,0:T(8,128)S(1)} %get-tuple-element.19.e, f32[3,4,16,128]{3,2,1,0:T(8,128)S(1)} %get-tuple-element.20.h, f32[3,4,32,128]{3,2,1,0:T(8,128)S(1)} %get-tuple-element.21.ae, ...), custom_call_target="tpu_custom_call" | custom-call | tf_op jit(solution)/shard_map/first/pallas_call | solution.py:632
  2.6 2.8 %collective-permute-start.1 = (f32[504,128]{1,0:T(8,128)S(1)}, f32[504,128]{1,0:T(8,128)S(1)}, u32[]{:S(2)}, u32[]{:S(2)}) collective-permute-start(f32[504,128]{1,0:T(8,128)S(1)} %get-tuple-element.23), channel_id=1, source_target_pairs={{0,1},{1,0},{2,3},{3,2},{4,8},{5,9},{6,10},{7,11},{8,4},{9,5},{10,... | collective-permute-start | bytes 774152 | tf_op jit(solution)/shard_map/ppermute | solution.py:49
  5.4 0.0 collective-permute-start.2
  5.4 1.6 %collective-permute-start.4 = (f32[56,128]{1,0:T(8,128)S(1)}, f32[56,128]{1,0:T(8,128)S(1)}, u32[]{:S(2)}, u32[]{:S(2)}) collective-permute-start(f32[56,128]{1,0:T(8,128)S(1)} %get-tuple-element.25), channel_id=1, source_target_pairs={{0,1},{1,0},{2,3},{3,2},{4,5},{5,4},{6,7},{7,6},{8,9},{9,8},{10,11... | collective-permute-start | bytes 86024 | tf_op jit(solution)/shard_map/ppermute | solution.py:49
  7.0 0.0 collective-permute-start.3
  7.0 3.3 %collective-permute-done.4.even = f32[56,128]{1,0:T(8,128)S(1)} collective-permute-done((f32[56,128]{1,0:T(8,128)S(1)}, f32[56,128]{1,0:T(8,128)S(1)}, u32[]{:S(2)}, u32[]{:S(2)}) %collective-permute-start.4) | collective-permute-done | bytes 28704 | tf_op jit(solution)/shard_map/ppermute | solution.py:49
  10.3 0.0 collective-permute-done.3.odd
  10.4 2.1 %collective-permute-start.6 = (f32[56,128]{1,0:T(8,128)S(1)}, f32[56,128]{1,0:T(8,128)S(1)}, u32[]{:S(2)}, u32[]{:S(2)}) collective-permute-start(f32[56,128]{1,0:T(8,128)S(1)} %combine.1.halo), channel_id=1, source_target_pairs={{0,1},{1,0},{2,3},{3,2},{4,8},{5,9},{6,10},{7,11},{8,4},{9,5},{10,... | collective-permute-start | bytes 86024 | tf_op jit(solution)/shard_map/ppermute | solution.py:49
  12.4 0.0 collective-permute-start.5
  12.4 1.8 %collective-permute-done.6.halo_odd = f32[56,128]{1,0:T(8,128)S(1)} collective-permute-done((f32[56,128]{1,0:T(8,128)S(1)}, f32[56,128]{1,0:T(8,128)S(1)}, u32[]{:S(2)}, u32[]{:S(2)}) %collective-permute-start.6) | collective-permute-done | bytes 28704 | tf_op jit(solution)/shard_map/ppermute | solution.py:49
  14.3 0.0 collective-permute-done.5.halo_even
  14.3 0.0 collective-permute-done.1.from_odd
  14.3 0.0 collective-permute-done.2.from_even
  14.3 0.1 columns.1
  14.4 0.0 collective-permute-start.7
  14.4 1.0 %full.1 = (f32[3,4,32,128]{3,2,1,0:T(8,128)S(1)}, f32[3,4,32,128]{3,2,1,0:T(8,128)S(1)}, f32[5,3,10,8,256]{4,3,2,1,0:T(8,128)S(1)}) custom-call(f32[3,4,16,128]{3,2,1,0:T(8,128)S(1)} %get-tuple-element.19.e, f32[3,4,16,128]{3,2,1,0:T(8,128)S(1)} %get-tuple-element.20.h, f32[3,4,32,128]{3,2,1,0:T(8,128)S(1)} %get-tuple-element.21.ae, ...), custom_call_target="tpu_custom_call" | custom-call | tf_op jit(solution)/shard_map/full/pallas_call | solution.py:662
  15.5 0.1 collective-permute-done.7.far
  15.6 1.2 %near.1 = (f32[2,4,128]{2,1,0:T(4,128)}, f32[3,4,32,128]{3,2,1,0:T(8,128)}, f32[3,4,32,128]{3,2,1,0:T(8,128)}) custom-call(f32[48,256]{1,0:T(8,128)S(1)} %get-tuple-element.26.columns, f32[8,128]{1,0:T(8,128)S(1)} %collective-permute-done.7.far, f32[3,4,32,128]{3,2,1,0:T(8,128)S(1)} %get-tuple-element.28.done_e, ...), custom_call_target="tpu_custom_call" | custom-call | tf_op jit(solution)/shard_map/near/pallas_call | solution.py:678
  (1 shorter events, 0.0 us)
Async XLA Ops:
  0.6 1.7 %collective-permute-start = (f32[2,4,128]{2,1,0:T(4,128)}, f32[2,4,128]{2,1,0:T(4,128)S(1)}, u32[]{:S(2)}, u32[]{:S(2)}) collective-permute-start(f32[2,4,128]{2,1,0:T(4,128)} %den.1), channel_id=1, source_target_pairs={{0,4},{1,5},{2,6},{3,7},{4,0},{5,1},{6,2},{7,3},{8,12},{9,13},{10,... | collective-permute-start | bytes 12296 | tf_op jit(solution)/shard_map/ppermute | solution.py:49
  2.6 11.7 %collective-permute-start.1 = (f32[504,128]{1,0:T(8,128)S(1)}, f32[504,128]{1,0:T(8,128)S(1)}, u32[]{:S(2)}, u32[]{:S(2)}) collective-permute-start(f32[504,128]{1,0:T(8,128)S(1)} %get-tuple-element.23), channel_id=1, source_target_pairs={{0,1},{1,0},{2,3},{3,2},{4,8},{5,9},{6,10},{7,11},{8,4},{9,5},{10,... | collective-permute-start | bytes 774152 | tf_op jit(solution)/shard_map/ppermute | solution.py:49
  5.4 8.9 %collective-permute-start.2 = (f32[504,128]{1,0:T(8,128)S(1)}, f32[504,128]{1,0:T(8,128)S(1)}, u32[]{:S(2)}, u32[]{:S(2)}) collective-permute-start(f32[504,128]{1,0:T(8,128)S(1)} %get-tuple-element.24), channel_id=1, source_target_pairs={{0,4},{1,5},{2,6},{3,7},{4,0},{5,1},{6,2},{7,3},{8,12},{9,13},{10,... | collective-permute-start | bytes 774152 | tf_op jit(solution)/shard_map/ppermute | solution.py:49
  5.4 4.9 %collective-permute-start.4 = (f32[56,128]{1,0:T(8,128)S(1)}, f32[56,128]{1,0:T(8,128)S(1)}, u32[]{:S(2)}, u32[]{:S(2)}) collective-permute-start(f32[56,128]{1,0:T(8,128)S(1)} %get-tuple-element.25), channel_id=1, source_target_pairs={{0,1},{1,0},{2,3},{3,2},{4,5},{5,4},{6,7},{7,6},{8,9},{9,8},{10,11... | collective-permute-start | bytes 86024 | tf_op jit(solution)/shard_map/ppermute | solution.py:49
  7.0 3.3 %collective-permute-start.3 = (f32[56,128]{1,0:T(8,128)S(1)}, f32[56,128]{1,0:T(8,128)S(1)}, u32[]{:S(2)}, u32[]{:S(2)}) collective-permute-start(f32[56,128]{1,0:T(8,128)S(1)} %get-tuple-element.25), channel_id=1, source_target_pairs={{0,4},{1,2},{2,1},{3,7},{4,0},{5,6},{6,5},{7,3},{8,12},{9,10},{10,... | collective-permute-start | bytes 86024 | tf_op jit(solution)/shard_map/ppermute | solution.py:49
  10.4 3.9 %collective-permute-start.6 = (f32[56,128]{1,0:T(8,128)S(1)}, f32[56,128]{1,0:T(8,128)S(1)}, u32[]{:S(2)}, u32[]{:S(2)}) collective-permute-start(f32[56,128]{1,0:T(8,128)S(1)} %combine.1.halo), channel_id=1, source_target_pairs={{0,1},{1,0},{2,3},{3,2},{4,8},{5,9},{6,10},{7,11},{8,4},{9,5},{10,... | collective-permute-start | bytes 86024 | tf_op jit(solution)/shard_map/ppermute | solution.py:49
  12.4 1.9 %collective-permute-start.5 = (f32[56,128]{1,0:T(8,128)S(1)}, f32[56,128]{1,0:T(8,128)S(1)}, u32[]{:S(2)}, u32[]{:S(2)}) collective-permute-start(f32[56,128]{1,0:T(8,128)S(1)} %combine.1.halo), channel_id=1, source_target_pairs={{0,4},{1,5},{2,6},{3,7},{4,0},{5,1},{6,2},{7,3},{8,12},{9,13},{10,... | collective-permute-start | bytes 86024 | tf_op jit(solution)/shard_map/ppermute | solution.py:49
  14.4 1.2 %collective-permute-start.7 = (f32[8,128]{1,0:T(8,128)S(1)}, f32[8,128]{1,0:T(8,128)S(1)}, u32[]{:S(2)}, u32[]{:S(2)}) collective-permute-start(f32[8,128]{1,0:T(8,128)S(1)} %get-tuple-element.27), channel_id=1, source_target_pairs={{0,4},{1,5},{2,6},{3,7},{4,0},{5,1},{6,2},{7,3},{8,12},{9,13},{10,... | collective-permute-start | bytes 12296 | tf_op jit(solution)/shard_map/ppermute | solution.py:49

commit v5 on v4

--- a/solution.py
+++ b/solution.py
@@ -60,7 +60,9 @@
 def x_ring(i, j, nx, ny):
     if 0 < i < nx - 1:
         return odd_swap(i), j
-    return (i, odd_swap(j)) if 0 < j < ny - 1 else (nx - 1 - i, j)
+    if i == 0:
+        return (0, j - 1) if j > 0 else (nx - 1, j)
+    return (i, j + 1) if j < ny - 1 else (0, j)
 
 
 def y_even(i, j, nx, ny):
@@ -147,7 +149,7 @@
     return low, low // TILE * TILE
 
 
-def load_kernel(depth, den, e, h, ae, ah, reg, own_den, own_e, own_h, own_ae, own_ah, own_reg, sems):
+def load_kernel(depth, den, e, h, ae, ah, reg, own_den, own_e, own_h, own_ae, own_ah, own_reg, packed, sems):
     near = pl.ds(near_layers(depth)[1], 2 * TILE)
     pairs = (
         (ae, own_ae),
@@ -160,7 +162,11 @@
     copies = [pltpu.make_async_copy(source, target, sems.at[n]) for n, (source, target) in enumerate(pairs)]
     for copy in copies:
         copy.start()
-    for copy in copies:
+    copies[0].wait()
+    copies[1].wait()
+    own = (own_ae, own_ah)
+    packed[...] = pack([field[c, row] for row in range(4) for field in own for c in range(3)], FULL_K)
+    for copy in copies[2:]:
         copy.wait()
 
 
@@ -174,7 +180,7 @@
     return windows
 
 
-def first_kernel(depth, den, e, h, ae, ah, reg, mate_den, edges, to_even, to_odd):
+def first_kernel(depth, den, e, h, ae, ah, reg, packed, mate_den, edges, to_even, to_odd):
     plan, sent = Edges(depth), Sent(depth)
     low = near_layers(depth)[0]
     odd = lax.rem(lax.axis_index("gx"), 2)
@@ -195,7 +201,6 @@
                 other = field[c, row, middle + from_right : middle + from_right + count, :]
                 value = jnp.where(jnp.full(value.shape, right, jnp.int32) == 1, value, other)
             ref[at : at + count, :] = value
-    planes = [own[name][c, row] for row in range(4) for name in ("ae", "ah") for c in range(3)]
     blank = jnp.zeros((4, LANES), jnp.float32)
     column = jnp.concatenate(
         [den[0], den[1], reg[...].astype(jnp.float32), blank, mate_den[0], mate_den[1]]
@@ -204,7 +209,7 @@
     )
     lane = lane_index(depth)
     mine = (lane >= COLUMN_LANE - COLUMN_K) & (lane < COLUMN_LANE + COLUMN_K)
-    edges[0:depth, :] = jnp.where(mine, pltpu.roll(column, COLUMN_LANE, 1), pack(planes, FULL_K))
+    edges[0:depth, :] = jnp.where(mine, pltpu.roll(column, COLUMN_LANE, 1), packed[...])
     for n in range(3):
         at = plan.window_at + n * TILE
         edges[at : at + TILE, :] = pack(windows[16 * n : 16 * n + 16], WIN_K)
@@ -622,6 +627,7 @@
             pltpu.VMEM(adj_e.shape, f32),
             pltpu.VMEM(adj_h.shape, f32),
             pltpu.VMEM(region.shape, region.dtype),
+            pltpu.VMEM((depth, LANES), f32),
         ),
         in_specs=[pl.BlockSpec(memory_space=pltpu.HBM)] * 6,
         scratch_shapes=[pltpu.SemaphoreType.DMA((6,))],
@@ -641,7 +647,7 @@
     )(*own, mate_den)
     edges_even = pair_permute(edges, y_even)
     edges_odd = pair_permute(edges, y_odd)
-    from_odd = pair_permute(to_odd, x_odd)
+    from_odd = pair_permute(to_odd, x_ring)
     from_even = pair_permute(to_even, x_even)
     halo = pl.pallas_call(
         functools.partial(combine_kernel, depth),
@@ -649,7 +655,7 @@
         compiler_params=params,
         name="combine",
     )(edges_odd, edges_even)
-    halo_odd = pair_permute(halo, x_odd)
+    halo_odd = pair_permute(halo, x_ring)
     halo_even = pair_permute(halo, x_even)
     wide = 2 * LANES
     columns, far = pl.pallas_call(

time: 17 us -> 16.8 us (0.988)
  starting transfers between devices: 7.07 us -> 6.12 us
  waiting for transfers between devices: 5.28 us -> 6.15 us
    ppermute x8, starting transfers between devices: 7.07 us -> 6.12 us  [pair_permute(): return lax.ppermute(block, ('gx', 'gy'), route)]
    ppermute x8, waiting for transfers between devices: 5.28 us -> 6.15 us  [pair_permute(): return lax.ppermute(block, ('gx', 'gy'), route)]
  transfers between devices with their start and end apart: 8 -> 8, of which waited for: 3 -> 3; matrix products, arithmetic and copies ran while one was open for 0% -> 0% of each run, Pallas kernels for 13% -> 14%
where the time goes in v5:
time: 16.8 us; the launch traced here: 16.7 us
  waiting for transfers between devices  6.15 us (37%)
  starting transfers between devices  6.12 us (36%)
  Pallas kernels  3.73 us (22%)
  between operations  0.69 us (4%)
    ppermute x8, waiting for transfers between devices, pair_permute(): return lax.ppermute(block, ('gx', 'gy'), route)  6.15 us
    ppermute x8, starting transfers between devices, pair_permute(): return lax.ppermute(block, ('gx', 'gy'), route)  6.12 us
    pallas_call x1, Pallas kernels, per_device(): pl.pallas_call(functools.partial(load_kernel, depth), out_shape=(pltpu.VM...  1.24 us
    pallas_call x1, Pallas kernels, per_device(): pl.pallas_call(functools.partial(near_kernel, depth), out_shape=(shape(de...  1.21 us
    pallas_call x1, Pallas kernels, per_device(): pl.pallas_call(functools.partial(full_kernel, depth), out_shape=(pltpu.VM...  1.04 us
  transfers between devices with their start and end apart: 8, of which 3 were waited for; matrix products, arithmetic and copies ran while one was open for 0% of the time, Pallas kernels for 14%

profile of v5, /device:TPU:0, one launch (start us, length us, event | category | flops | bytes accessed | tf_op | source)
XLA Modules:
  0.0 16.7 jit_solution(1054079225047040802)
XLA Ops:
  0.6 0.5 %collective-permute-start = (f32[2,4,128]{2,1,0:T(4,128)}, f32[2,4,128]{2,1,0:T(4,128)S(1)}, u32[]{:S(2)}, u32[]{:S(2)}) collective-permute-start(f32[2,4,128]{2,1,0:T(4,128)} %den.1), channel_id=1, source_target_pairs={{0,4},{1,5},{2,6},{3,7},{4,0},{5,1},{6,2},{7,3},{8,12},{9,13},{10,... | collective-permute-start | bytes 12296 | tf_op jit(solution)/shard_map/ppermute | solution.py:49
  1.1 1.2 %load.1 = (f32[2,4,128]{2,1,0:T(4,128)S(1)}, f32[3,4,16,128]{3,2,1,0:T(8,128)S(1)}, f32[3,4,16,128]{3,2,1,0:T(8,128)S(1)}, f32[3,4,32,128]{3,2,1,0:T(8,128)S(1)}...) custom-call(f32[2,4,128]{2,1,0:T(4,128)} %den.1, f32[3,4,32,128]{3,2,1,0:T(8,128)} %e.1, ...), custom_call_target="tpu_custom_call" | custom-call | tf_op jit(solution)/shard_map/load/pallas_call | solution.py:621
  2.4 0.0 collective-permute-done.mate_den
  2.4 0.1 first.1
  2.6 3.6 %collective-permute-start.1 = (f32[504,128]{1,0:T(8,128)S(1)}, f32[504,128]{1,0:T(8,128)S(1)}, u32[]{:S(2)}, u32[]{:S(2)}) collective-permute-start(f32[504,128]{1,0:T(8,128)S(1)} %get-tuple-element.25), channel_id=1, source_target_pairs={{0,28},{1,0},{2,1},{3,2},{4,8},{5,9},{6,10},{7,11},{8,4},{9,5},{10... | collective-permute-start | bytes 774152 | tf_op jit(solution)/shard_map/ppermute | solution.py:49
  6.2 0.0 collective-permute-start.2
  6.2 0.7 %collective-permute-start.4 = (f32[56,128]{1,0:T(8,128)S(1)}, f32[56,128]{1,0:T(8,128)S(1)}, u32[]{:S(2)}, u32[]{:S(2)}) collective-permute-start(f32[56,128]{1,0:T(8,128)S(1)} %get-tuple-element.27), channel_id=1, source_target_pairs={{0,1},{1,0},{2,3},{3,2},{4,5},{5,4},{6,7},{7,6},{8,9},{9,8},{10,11... | collective-permute-start | bytes 86024 | tf_op jit(solution)/shard_map/ppermute | solution.py:49
  6.9 0.0 collective-permute-start.3
  6.9 3.3 %collective-permute-done.4.even = f32[56,128]{1,0:T(8,128)S(1)} collective-permute-done((f32[56,128]{1,0:T(8,128)S(1)}, f32[56,128]{1,0:T(8,128)S(1)}, u32[]{:S(2)}, u32[]{:S(2)}) %collective-permute-start.4) | collective-permute-done | bytes 28704 | tf_op jit(solution)/shard_map/ppermute | solution.py:49
  10.2 0.0 collective-permute-done.3.odd
  10.2 1.2 %collective-permute-start.6 = (f32[56,128]{1,0:T(8,128)S(1)}, f32[56,128]{1,0:T(8,128)S(1)}, u32[]{:S(2)}, u32[]{:S(2)}) collective-permute-start(f32[56,128]{1,0:T(8,128)S(1)} %combine.1.halo), channel_id=1, source_target_pairs={{0,28},{1,0},{2,1},{3,2},{4,8},{5,9},{6,10},{7,11},{8,4},{9,5},{10... | collective-permute-start | bytes 86024 | tf_op jit(solution)/shard_map/ppermute | solution.py:49
  11.4 0.0 collective-permute-start.5
  11.5 2.7 %collective-permute-done.6.halo_odd = f32[56,128]{1,0:T(8,128)S(1)} collective-permute-done((f32[56,128]{1,0:T(8,128)S(1)}, f32[56,128]{1,0:T(8,128)S(1)}, u32[]{:S(2)}, u32[]{:S(2)}) %collective-permute-start.6) | collective-permute-done | bytes 28704 | tf_op jit(solution)/shard_map/ppermute | solution.py:49
  14.2 0.0 collective-permute-done.5.halo_even
  14.2 0.0 collective-permute-done.1.from_odd
  14.2 0.0 collective-permute-done.2.from_even
  14.2 0.1 columns.1
  14.3 0.0 collective-permute-start.7
  14.3 1.0 %full.1 = (f32[3,4,32,128]{3,2,1,0:T(8,128)S(1)}, f32[3,4,32,128]{3,2,1,0:T(8,128)S(1)}, f32[5,3,10,8,256]{4,3,2,1,0:T(8,128)S(1)}) custom-call(f32[3,4,16,128]{3,2,1,0:T(8,128)S(1)} %get-tuple-element.20.e, f32[3,4,16,128]{3,2,1,0:T(8,128)S(1)} %get-tuple-element.21.h, f32[3,4,32,128]{3,2,1,0:T(8,128)S(1)} %get-tuple-element.22.ae, ...), custom_call_target="tpu_custom_call" | custom-call | tf_op jit(solution)/shard_map/full/pallas_call | solution.py:668
  15.4 0.1 collective-permute-done.7.far
  15.5 1.2 %near.1 = (f32[2,4,128]{2,1,0:T(4,128)}, f32[3,4,32,128]{3,2,1,0:T(8,128)}, f32[3,4,32,128]{3,2,1,0:T(8,128)}) custom-call(f32[48,256]{1,0:T(8,128)S(1)} %get-tuple-element.28.columns, f32[8,128]{1,0:T(8,128)S(1)} %collective-permute-done.7.far, f32[3,4,32,128]{3,2,1,0:T(8,128)S(1)} %get-tuple-element.30.done_e, ...), custom_call_target="tpu_custom_call" | custom-call | tf_op jit(solution)/shard_map/near/pallas_call | solution.py:684
  (1 shorter events, 0.0 us)
Async XLA Ops:
  0.6 1.8 %collective-permute-start = (f32[2,4,128]{2,1,0:T(4,128)}, f32[2,4,128]{2,1,0:T(4,128)S(1)}, u32[]{:S(2)}, u32[]{:S(2)}) collective-permute-start(f32[2,4,128]{2,1,0:T(4,128)} %den.1), channel_id=1, source_target_pairs={{0,4},{1,5},{2,6},{3,7},{4,0},{5,1},{6,2},{7,3},{8,12},{9,13},{10,... | collective-permute-start | bytes 12296 | tf_op jit(solution)/shard_map/ppermute | solution.py:49
  2.6 11.6 %collective-permute-start.1 = (f32[504,128]{1,0:T(8,128)S(1)}, f32[504,128]{1,0:T(8,128)S(1)}, u32[]{:S(2)}, u32[]{:S(2)}) collective-permute-start(f32[504,128]{1,0:T(8,128)S(1)} %get-tuple-element.25), channel_id=1, source_target_pairs={{0,28},{1,0},{2,1},{3,2},{4,8},{5,9},{6,10},{7,11},{8,4},{9,5},{10... | collective-permute-start | bytes 774152 | tf_op jit(solution)/shard_map/ppermute | solution.py:49
  6.2 8.0 %collective-permute-start.2 = (f32[504,128]{1,0:T(8,128)S(1)}, f32[504,128]{1,0:T(8,128)S(1)}, u32[]{:S(2)}, u32[]{:S(2)}) collective-permute-start(f32[504,128]{1,0:T(8,128)S(1)} %get-tuple-element.26), channel_id=1, source_target_pairs={{0,4},{1,5},{2,6},{3,7},{4,0},{5,1},{6,2},{7,3},{8,12},{9,13},{10,... | collective-permute-start | bytes 774152 | tf_op jit(solution)/shard_map/ppermute | solution.py:49
  6.2 4.0 %collective-permute-start.4 = (f32[56,128]{1,0:T(8,128)S(1)}, f32[56,128]{1,0:T(8,128)S(1)}, u32[]{:S(2)}, u32[]{:S(2)}) collective-permute-start(f32[56,128]{1,0:T(8,128)S(1)} %get-tuple-element.27), channel_id=1, source_target_pairs={{0,1},{1,0},{2,3},{3,2},{4,5},{5,4},{6,7},{7,6},{8,9},{9,8},{10,11... | collective-permute-start | bytes 86024 | tf_op jit(solution)/shard_map/ppermute | solution.py:49
  6.9 3.3 %collective-permute-start.3 = (f32[56,128]{1,0:T(8,128)S(1)}, f32[56,128]{1,0:T(8,128)S(1)}, u32[]{:S(2)}, u32[]{:S(2)}) collective-permute-start(f32[56,128]{1,0:T(8,128)S(1)} %get-tuple-element.27), channel_id=1, source_target_pairs={{0,4},{1,2},{2,1},{3,7},{4,0},{5,6},{6,5},{7,3},{8,12},{9,10},{10,... | collective-permute-start | bytes 86024 | tf_op jit(solution)/shard_map/ppermute | solution.py:49
  10.2 3.9 %collective-permute-start.6 = (f32[56,128]{1,0:T(8,128)S(1)}, f32[56,128]{1,0:T(8,128)S(1)}, u32[]{:S(2)}, u32[]{:S(2)}) collective-permute-start(f32[56,128]{1,0:T(8,128)S(1)} %combine.1.halo), channel_id=1, source_target_pairs={{0,28},{1,0},{2,1},{3,2},{4,8},{5,9},{6,10},{7,11},{8,4},{9,5},{10... | collective-permute-start | bytes 86024 | tf_op jit(solution)/shard_map/ppermute | solution.py:49
  11.4 2.7 %collective-permute-start.5 = (f32[56,128]{1,0:T(8,128)S(1)}, f32[56,128]{1,0:T(8,128)S(1)}, u32[]{:S(2)}, u32[]{:S(2)}) collective-permute-start(f32[56,128]{1,0:T(8,128)S(1)} %combine.1.halo), channel_id=1, source_target_pairs={{0,4},{1,5},{2,6},{3,7},{4,0},{5,1},{6,2},{7,3},{8,12},{9,13},{10,... | collective-permute-start | bytes 86024 | tf_op jit(solution)/shard_map/ppermute | solution.py:49
  14.3 1.2 %collective-permute-start.7 = (f32[8,128]{1,0:T(8,128)S(1)}, f32[8,128]{1,0:T(8,128)S(1)}, u32[]{:S(2)}, u32[]{:S(2)}) collective-permute-start(f32[8,128]{1,0:T(8,128)S(1)} %get-tuple-element.29), channel_id=1, source_target_pairs={{0,4},{1,5},{2,6},{3,7},{4,0},{5,1},{6,2},{7,3},{8,12},{9,13},{10,... | collective-permute-start | bytes 12296 | tf_op jit(solution)/shard_map/ppermute | solution.py:49

commit v6 on v5

--- a/solution.py
+++ b/solution.py
@@ -151,22 +151,17 @@
 
 def load_kernel(depth, den, e, h, ae, ah, reg, own_den, own_e, own_h, own_ae, own_ah, own_reg, packed, sems):
     near = pl.ds(near_layers(depth)[1], 2 * TILE)
-    pairs = (
-        (ae, own_ae),
-        (ah, own_ah),
-        (e.at[:, :, near, :], own_e),
-        (h.at[:, :, near, :], own_h),
-        (den, own_den),
-        (reg, own_reg),
-    )
+    pairs = [(ae.at[c], own_ae.at[c]) for c in range(3)]
+    pairs += [(ah.at[c], own_ah.at[c]) for c in range(3)]
+    pairs += [(e.at[:, :, near, :], own_e), (h.at[:, :, near, :], own_h), (den, own_den), (reg, own_reg)]
     copies = [pltpu.make_async_copy(source, target, sems.at[n]) for n, (source, target) in enumerate(pairs)]
     for copy in copies:
         copy.start()
-    copies[0].wait()
-    copies[1].wait()
+    for copy in copies[:6]:
+        copy.wait()
     own = (own_ae, own_ah)
     packed[...] = pack([field[c, row] for row in range(4) for field in own for c in range(3)], FULL_K)
-    for copy in copies[2:]:
+    for copy in copies[6:]:
         copy.wait()
 
 
@@ -630,7 +625,7 @@
             pltpu.VMEM((depth, LANES), f32),
         ),
         in_specs=[pl.BlockSpec(memory_space=pltpu.HBM)] * 6,
-        scratch_shapes=[pltpu.SemaphoreType.DMA((6,))],
+        scratch_shapes=[pltpu.SemaphoreType.DMA((10,))],
         compiler_params=pltpu.CompilerParams(vmem_limit_bytes=LOAD_VMEM),
         name="load",
     )(density, e_field, h_field, adj_e, adj_h, region)
@@ -655,7 +650,7 @@
         compiler_params=params,
         name="combine",
     )(edges_odd, edges_even)
-    halo_odd = pair_permute(halo, x_ring)
+    halo_odd = pair_permute(halo, x_odd)
     halo_even = pair_permute(halo, x_even)
     wide = 2 * LANES
     columns, far = pl.pallas_call(

time: 16.8 us -> 16.8 us (level)
  starting transfers between devices: 6.12 us -> 6.98 us
  waiting for transfers between devices: 6.15 us -> 5.29 us
    ppermute x8, starting transfers between devices: 6.12 us -> 6.98 us  [pair_permute(): return lax.ppermute(block, ('gx', 'gy'), route)]
    ppermute x8, waiting for transfers between devices: 6.15 us -> 5.29 us  [pair_permute(): return lax.ppermute(block, ('gx', 'gy'), route)]
where the time goes in v6:
time: 16.8 us; the launch traced here: 16.7 us
  starting transfers between devices  6.98 us (42%)
  waiting for transfers between devices  5.29 us (31%)
  Pallas kernels  3.74 us (22%)
  between operations  0.69 us (4%)
    ppermute x8, starting transfers between devices, pair_permute(): return lax.ppermute(block, ('gx', 'gy'), route)  6.98 us
    ppermute x8, waiting for transfers between devices, pair_permute(): return lax.ppermute(block, ('gx', 'gy'), route)  5.29 us
    pallas_call x1, Pallas kernels, per_device(): pl.pallas_call(functools.partial(load_kernel, depth), out_shape=(pltpu.VM...  1.25 us
    pallas_call x1, Pallas kernels, per_device(): pl.pallas_call(functools.partial(near_kernel, depth), out_shape=(shape(de...  1.21 us
    pallas_call x1, Pallas kernels, per_device(): pl.pallas_call(functools.partial(full_kernel, depth), out_shape=(pltpu.VM...  1.04 us
  transfers between devices with their start and end apart: 8, of which 3 were waited for; matrix products, arithmetic and copies ran while one was open for 0% of the time, Pallas kernels for 14%

profile of v6, /device:TPU:0, one launch (start us, length us, event | category | flops | bytes accessed | tf_op | source)
XLA Modules:
  0.0 16.7 jit_solution(5189534573824787725)
XLA Ops:
  0.6 0.5 %collective-permute-start = (f32[2,4,128]{2,1,0:T(4,128)}, f32[2,4,128]{2,1,0:T(4,128)S(1)}, u32[]{:S(2)}, u32[]{:S(2)}) collective-permute-start(f32[2,4,128]{2,1,0:T(4,128)} %den.1), channel_id=1, source_target_pairs={{0,4},{1,5},{2,6},{3,7},{4,0},{5,1},{6,2},{7,3},{8,12},{9,13},{10,... | collective-permute-start | bytes 12296 | tf_op jit(solution)/shard_map/ppermute | solution.py:49
  1.1 1.3 %load.1 = (f32[2,4,128]{2,1,0:T(4,128)S(1)}, f32[3,4,16,128]{3,2,1,0:T(8,128)S(1)}, f32[3,4,16,128]{3,2,1,0:T(8,128)S(1)}, f32[3,4,32,128]{3,2,1,0:T(8,128)S(1)}...) custom-call(f32[2,4,128]{2,1,0:T(4,128)} %den.1, f32[3,4,32,128]{3,2,1,0:T(8,128)} %e.1, ...), custom_call_target="tpu_custom_call" | custom-call | tf_op jit(solution)/shard_map/load/pallas_call | solution.py:616
  2.4 0.0 collective-permute-done.mate_den
  2.4 0.1 first.1
  2.6 3.6 %collective-permute-start.1 = (f32[504,128]{1,0:T(8,128)S(1)}, f32[504,128]{1,0:T(8,128)S(1)}, u32[]{:S(2)}, u32[]{:S(2)}) collective-permute-start(f32[504,128]{1,0:T(8,128)S(1)} %get-tuple-element.25), channel_id=1, source_target_pairs={{0,28},{1,0},{2,1},{3,2},{4,8},{5,9},{6,10},{7,11},{8,4},{9,5},{10... | collective-permute-start | bytes 774152 | tf_op jit(solution)/shard_map/ppermute | solution.py:49
  6.2 0.0 collective-permute-start.2
  6.2 0.7 %collective-permute-start.4 = (f32[56,128]{1,0:T(8,128)S(1)}, f32[56,128]{1,0:T(8,128)S(1)}, u32[]{:S(2)}, u32[]{:S(2)}) collective-permute-start(f32[56,128]{1,0:T(8,128)S(1)} %get-tuple-element.27), channel_id=1, source_target_pairs={{0,1},{1,0},{2,3},{3,2},{4,5},{5,4},{6,7},{7,6},{8,9},{9,8},{10,11... | collective-permute-start | bytes 86024 | tf_op jit(solution)/shard_map/ppermute | solution.py:49
  6.9 0.0 collective-permute-start.3
  6.9 3.3 %collective-permute-done.4.even = f32[56,128]{1,0:T(8,128)S(1)} collective-permute-done((f32[56,128]{1,0:T(8,128)S(1)}, f32[56,128]{1,0:T(8,128)S(1)}, u32[]{:S(2)}, u32[]{:S(2)}) %collective-permute-start.4) | collective-permute-done | bytes 28704 | tf_op jit(solution)/shard_map/ppermute | solution.py:49
  10.2 0.0 collective-permute-done.3.odd
  10.2 2.1 %collective-permute-start.6 = (f32[56,128]{1,0:T(8,128)S(1)}, f32[56,128]{1,0:T(8,128)S(1)}, u32[]{:S(2)}, u32[]{:S(2)}) collective-permute-start(f32[56,128]{1,0:T(8,128)S(1)} %combine.1.halo), channel_id=1, source_target_pairs={{0,1},{1,0},{2,3},{3,2},{4,8},{5,9},{6,10},{7,11},{8,4},{9,5},{10,... | collective-permute-start | bytes 86024 | tf_op jit(solution)/shard_map/ppermute | solution.py:49
  12.3 0.0 collective-permute-start.5
  12.3 1.9 %collective-permute-done.6.halo_odd = f32[56,128]{1,0:T(8,128)S(1)} collective-permute-done((f32[56,128]{1,0:T(8,128)S(1)}, f32[56,128]{1,0:T(8,128)S(1)}, u32[]{:S(2)}, u32[]{:S(2)}) %collective-permute-start.6) | collective-permute-done | bytes 28704 | tf_op jit(solution)/shard_map/ppermute | solution.py:49
  14.2 0.0 collective-permute-done.5.halo_even
  14.2 0.0 collective-permute-done.1.from_odd
  14.2 0.0 collective-permute-done.2.from_even
  14.2 0.1 columns.1
  14.3 0.0 collective-permute-start.7
  14.3 1.0 %full.1 = (f32[3,4,32,128]{3,2,1,0:T(8,128)S(1)}, f32[3,4,32,128]{3,2,1,0:T(8,128)S(1)}, f32[5,3,10,8,256]{4,3,2,1,0:T(8,128)S(1)}) custom-call(f32[3,4,16,128]{3,2,1,0:T(8,128)S(1)} %get-tuple-element.20.e, f32[3,4,16,128]{3,2,1,0:T(8,128)S(1)} %get-tuple-element.21.h, f32[3,4,32,128]{3,2,1,0:T(8,128)S(1)} %get-tuple-element.22.ae, ...), custom_call_target="tpu_custom_call" | custom-call | tf_op jit(solution)/shard_map/full/pallas_call | solution.py:663
  15.4 0.1 collective-permute-done.7.far
  15.5 1.2 %near.1 = (f32[2,4,128]{2,1,0:T(4,128)}, f32[3,4,32,128]{3,2,1,0:T(8,128)}, f32[3,4,32,128]{3,2,1,0:T(8,128)}) custom-call(f32[48,256]{1,0:T(8,128)S(1)} %get-tuple-element.28.columns, f32[8,128]{1,0:T(8,128)S(1)} %collective-permute-done.7.far, f32[3,4,32,128]{3,2,1,0:T(8,128)S(1)} %get-tuple-element.30.done_e, ...), custom_call_target="tpu_custom_call" | custom-call | tf_op jit(solution)/shard_map/near/pallas_call | solution.py:679
  (1 shorter events, 0.0 us)
Async XLA Ops:
  0.6 1.8 %collective-permute-start = (f32[2,4,128]{2,1,0:T(4,128)}, f32[2,4,128]{2,1,0:T(4,128)S(1)}, u32[]{:S(2)}, u32[]{:S(2)}) collective-permute-start(f32[2,4,128]{2,1,0:T(4,128)} %den.1), channel_id=1, source_target_pairs={{0,4},{1,5},{2,6},{3,7},{4,0},{5,1},{6,2},{7,3},{8,12},{9,13},{10,... | collective-permute-start | bytes 12296 | tf_op jit(solution)/shard_map/ppermute | solution.py:49
  2.6 11.6 %collective-permute-start.1 = (f32[504,128]{1,0:T(8,128)S(1)}, f32[504,128]{1,0:T(8,128)S(1)}, u32[]{:S(2)}, u32[]{:S(2)}) collective-permute-start(f32[504,128]{1,0:T(8,128)S(1)} %get-tuple-element.25), channel_id=1, source_target_pairs={{0,28},{1,0},{2,1},{3,2},{4,8},{5,9},{6,10},{7,11},{8,4},{9,5},{10... | collective-permute-start | bytes 774152 | tf_op jit(solution)/shard_map/ppermute | solution.py:49
  6.2 8.0 %collective-permute-start.2 = (f32[504,128]{1,0:T(8,128)S(1)}, f32[504,128]{1,0:T(8,128)S(1)}, u32[]{:S(2)}, u32[]{:S(2)}) collective-permute-start(f32[504,128]{1,0:T(8,128)S(1)} %get-tuple-element.26), channel_id=1, source_target_pairs={{0,4},{1,5},{2,6},{3,7},{4,0},{5,1},{6,2},{7,3},{8,12},{9,13},{10,... | collective-permute-start | bytes 774152 | tf_op jit(solution)/shard_map/ppermute | solution.py:49
  6.2 4.0 %collective-permute-start.4 = (f32[56,128]{1,0:T(8,128)S(1)}, f32[56,128]{1,0:T(8,128)S(1)}, u32[]{:S(2)}, u32[]{:S(2)}) collective-permute-start(f32[56,128]{1,0:T(8,128)S(1)} %get-tuple-element.27), channel_id=1, source_target_pairs={{0,1},{1,0},{2,3},{3,2},{4,5},{5,4},{6,7},{7,6},{8,9},{9,8},{10,11... | collective-permute-start | bytes 86024 | tf_op jit(solution)/shard_map/ppermute | solution.py:49
  6.9 3.3 %collective-permute-start.3 = (f32[56,128]{1,0:T(8,128)S(1)}, f32[56,128]{1,0:T(8,128)S(1)}, u32[]{:S(2)}, u32[]{:S(2)}) collective-permute-start(f32[56,128]{1,0:T(8,128)S(1)} %get-tuple-element.27), channel_id=1, source_target_pairs={{0,4},{1,2},{2,1},{3,7},{4,0},{5,6},{6,5},{7,3},{8,12},{9,10},{10,... | collective-permute-start | bytes 86024 | tf_op jit(solution)/shard_map/ppermute | solution.py:49
  10.2 3.9 %collective-permute-start.6 = (f32[56,128]{1,0:T(8,128)S(1)}, f32[56,128]{1,0:T(8,128)S(1)}, u32[]{:S(2)}, u32[]{:S(2)}) collective-permute-start(f32[56,128]{1,0:T(8,128)S(1)} %combine.1.halo), channel_id=1, source_target_pairs={{0,1},{1,0},{2,3},{3,2},{4,8},{5,9},{6,10},{7,11},{8,4},{9,5},{10,... | collective-permute-start | bytes 86024 | tf_op jit(solution)/shard_map/ppermute | solution.py:49
  12.3 1.9 %collective-permute-start.5 = (f32[56,128]{1,0:T(8,128)S(1)}, f32[56,128]{1,0:T(8,128)S(1)}, u32[]{:S(2)}, u32[]{:S(2)}) collective-permute-start(f32[56,128]{1,0:T(8,128)S(1)} %combine.1.halo), channel_id=1, source_target_pairs={{0,4},{1,5},{2,6},{3,7},{4,0},{5,1},{6,2},{7,3},{8,12},{9,13},{10,... | collective-permute-start | bytes 86024 | tf_op jit(solution)/shard_map/ppermute | solution.py:49
  14.3 1.2 %collective-permute-start.7 = (f32[8,128]{1,0:T(8,128)S(1)}, f32[8,128]{1,0:T(8,128)S(1)}, u32[]{:S(2)}, u32[]{:S(2)}) collective-permute-start(f32[8,128]{1,0:T(8,128)S(1)} %get-tuple-element.29), channel_id=1, source_target_pairs={{0,4},{1,5},{2,6},{3,7},{4,0},{5,1},{6,2},{7,3},{8,12},{9,13},{10,... | collective-permute-start | bytes 12296 | tf_op jit(solution)/shard_map/ppermute | solution.py:49

commit v7 on v5

--- a/solution.py
+++ b/solution.py
@@ -286,7 +286,7 @@
         halo[at:end, :] = jnp.where(from_left, left, right)
 
 
-def columns_kernel(depth, den, reg, from_odd, from_even, halo, halo_even, halo_odd, columns, far):
+def columns_kernel(depth, den, reg, from_odd, from_even, halo, halo_odd, halo_even, columns, far):
     sent = Sent(depth)
     sides = Sides("gx")
     odd = as_float(lax.rem(lax.axis_index("gx"), 2))
@@ -663,7 +663,7 @@
         out_shape=(shape((48, wide), f32), shape((TILE, LANES), f32)),
         compiler_params=params,
         name="columns",
-    )(own[0], own[5], from_odd, from_even, halo, halo_even, halo_odd)
+    )(own[0], own[5], from_odd, from_even, halo, halo_odd, halo_even)
     far = pair_permute(far, x_even)
     done = pl.pallas_call(
         functools.partial(full_kernel, depth),

time: 16.8 us -> 16.9 us (level)
  starting transfers between devices: 6.12 us -> 6.7 us
  waiting for transfers between devices: 6.15 us -> 5.64 us
    ppermute x8, starting transfers between devices: 6.12 us -> 6.7 us  [pair_permute(): return lax.ppermute(block, ('gx', 'gy'), route)]
    ppermute x8, waiting for transfers between devices: 6.15 us -> 5.64 us  [pair_permute(): return lax.ppermute(block, ('gx', 'gy'), route)]
  transfers between devices with their start and end apart: 8 -> 8, of which waited for: 3 -> 2; matrix products, arithmetic and copies ran while one was open for 0% -> 0% of each run, Pallas kernels for 14% -> 14%
where the time goes in v7:
time: 16.9 us; the launch traced here: 16.8 us
  starting transfers between devices  6.7 us (40%)
  waiting for transfers between devices  5.64 us (33%)
  Pallas kernels  3.74 us (22%)
  between operations  0.68 us (4%)
    ppermute x8, starting transfers between devices, pair_permute(): return lax.ppermute(block, ('gx', 'gy'), route)  6.7 us
    ppermute x8, waiting for transfers between devices, pair_permute(): return lax.ppermute(block, ('gx', 'gy'), route)  5.64 us
    pallas_call x1, Pallas kernels, per_device(): pl.pallas_call(functools.partial(load_kernel, depth), out_shape=(pltpu.VM...  1.24 us
    pallas_call x1, Pallas kernels, per_device(): pl.pallas_call(functools.partial(near_kernel, depth), out_shape=(shape(de...  1.22 us
    pallas_call x1, Pallas kernels, per_device(): pl.pallas_call(functools.partial(full_kernel, depth), out_shape=(pltpu.VM...  1.03 us
  transfers between devices with their start and end apart: 8, of which 2 were waited for; matrix products, arithmetic and copies ran while one was open for 0% of the time, Pallas kernels for 14%

profile of v7, /device:TPU:0, one launch (start us, length us, event | category | flops | bytes accessed | tf_op | source)
XLA Modules:
  0.0 16.8 jit_solution(15890095362843202735)
XLA Ops:
  0.6 0.5 %collective-permute-start = (f32[2,4,128]{2,1,0:T(4,128)}, f32[2,4,128]{2,1,0:T(4,128)S(1)}, u32[]{:S(2)}, u32[]{:S(2)}) collective-permute-start(f32[2,4,128]{2,1,0:T(4,128)} %den.1), channel_id=1, source_target_pairs={{0,4},{1,5},{2,6},{3,7},{4,0},{5,1},{6,2},{7,3},{8,12},{9,13},{10,... | collective-permute-start | bytes 12296 | tf_op jit(solution)/shard_map/ppermute | solution.py:49
  1.1 1.2 %load.1 = (f32[2,4,128]{2,1,0:T(4,128)S(1)}, f32[3,4,16,128]{3,2,1,0:T(8,128)S(1)}, f32[3,4,16,128]{3,2,1,0:T(8,128)S(1)}, f32[3,4,32,128]{3,2,1,0:T(8,128)S(1)}...) custom-call(f32[2,4,128]{2,1,0:T(4,128)} %den.1, f32[3,4,32,128]{3,2,1,0:T(8,128)} %e.1, ...), custom_call_target="tpu_custom_call" | custom-call | tf_op jit(solution)/shard_map/load/pallas_call | solution.py:621
  2.4 0.0 collective-permute-done.mate_den
  2.4 0.1 first.1
  2.6 3.6 %collective-permute-start.1 = (f32[504,128]{1,0:T(8,128)S(1)}, f32[504,128]{1,0:T(8,128)S(1)}, u32[]{:S(2)}, u32[]{:S(2)}) collective-permute-start(f32[504,128]{1,0:T(8,128)S(1)} %get-tuple-element.25), channel_id=1, source_target_pairs={{0,28},{1,0},{2,1},{3,2},{4,8},{5,9},{6,10},{7,11},{8,4},{9,5},{10... | collective-permute-start | bytes 774152 | tf_op jit(solution)/shard_map/ppermute | solution.py:49
  6.2 0.0 collective-permute-start.2
  6.2 0.7 %collective-permute-start.4 = (f32[56,128]{1,0:T(8,128)S(1)}, f32[56,128]{1,0:T(8,128)S(1)}, u32[]{:S(2)}, u32[]{:S(2)}) collective-permute-start(f32[56,128]{1,0:T(8,128)S(1)} %get-tuple-element.27), channel_id=1, source_target_pairs={{0,1},{1,0},{2,3},{3,2},{4,5},{5,4},{6,7},{7,6},{8,9},{9,8},{10,11... | collective-permute-start | bytes 86024 | tf_op jit(solution)/shard_map/ppermute | solution.py:49
  6.9 0.0 collective-permute-start.3
  6.9 3.3 %collective-permute-done.4.even = f32[56,128]{1,0:T(8,128)S(1)} collective-permute-done((f32[56,128]{1,0:T(8,128)S(1)}, f32[56,128]{1,0:T(8,128)S(1)}, u32[]{:S(2)}, u32[]{:S(2)}) %collective-permute-start.4) | collective-permute-done | bytes 28704 | tf_op jit(solution)/shard_map/ppermute | solution.py:49
  10.2 0.0 collective-permute-done.3.odd
  10.2 0.1 collective-permute-start.6
  10.3 1.6 %collective-permute-start.5 = (f32[56,128]{1,0:T(8,128)S(1)}, f32[56,128]{1,0:T(8,128)S(1)}, u32[]{:S(2)}, u32[]{:S(2)}) collective-permute-start(f32[56,128]{1,0:T(8,128)S(1)} %combine.1.halo), channel_id=1, source_target_pairs={{0,28},{1,0},{2,1},{3,2},{4,8},{5,9},{6,10},{7,11},{8,4},{9,5},{10... | collective-permute-start | bytes 86024 | tf_op jit(solution)/shard_map/ppermute | solution.py:49
  11.9 0.0 collective-permute-done.6.halo_even
  11.9 2.3 %collective-permute-done.5.halo_odd = f32[56,128]{1,0:T(8,128)S(1)} collective-permute-done((f32[56,128]{1,0:T(8,128)S(1)}, f32[56,128]{1,0:T(8,128)S(1)}, u32[]{:S(2)}, u32[]{:S(2)}) %collective-permute-start.5) | collective-permute-done | bytes 28704 | tf_op jit(solution)/shard_map/ppermute | solution.py:49
  14.2 0.0 collective-permute-done.1.from_odd
  14.3 0.0 collective-permute-done.2.from_even
  14.3 0.1 columns.1
  14.3 0.2 collective-permute-start.7
  14.5 1.0 %full.1 = (f32[3,4,32,128]{3,2,1,0:T(8,128)S(1)}, f32[3,4,32,128]{3,2,1,0:T(8,128)S(1)}, f32[5,3,10,8,256]{4,3,2,1,0:T(8,128)S(1)}) custom-call(f32[3,4,16,128]{3,2,1,0:T(8,128)S(1)} %get-tuple-element.20.e, f32[3,4,16,128]{3,2,1,0:T(8,128)S(1)} %get-tuple-element.21.h, f32[3,4,32,128]{3,2,1,0:T(8,128)S(1)} %get-tuple-element.22.ae, ...), custom_call_target="tpu_custom_call" | custom-call | tf_op jit(solution)/shard_map/full/pallas_call | solution.py:668
  15.5 0.0 collective-permute-done.7.far
  15.5 1.2 %near.1 = (f32[2,4,128]{2,1,0:T(4,128)}, f32[3,4,32,128]{3,2,1,0:T(8,128)}, f32[3,4,32,128]{3,2,1,0:T(8,128)}) custom-call(f32[48,256]{1,0:T(8,128)S(1)} %get-tuple-element.28.columns, f32[8,128]{1,0:T(8,128)S(1)} %collective-permute-done.7.far, f32[3,4,32,128]{3,2,1,0:T(8,128)S(1)} %get-tuple-element.30.done_e, ...), custom_call_target="tpu_custom_call" | custom-call | tf_op jit(solution)/shard_map/near/pallas_call | solution.py:684
  (1 shorter events, 0.0 us)
Async XLA Ops:
  0.6 1.8 %collective-permute-start = (f32[2,4,128]{2,1,0:T(4,128)}, f32[2,4,128]{2,1,0:T(4,128)S(1)}, u32[]{:S(2)}, u32[]{:S(2)}) collective-permute-start(f32[2,4,128]{2,1,0:T(4,128)} %den.1), channel_id=1, source_target_pairs={{0,4},{1,5},{2,6},{3,7},{4,0},{5,1},{6,2},{7,3},{8,12},{9,13},{10,... | collective-permute-start | bytes 12296 | tf_op jit(solution)/shard_map/ppermute | solution.py:49
  2.6 11.7 %collective-permute-start.1 = (f32[504,128]{1,0:T(8,128)S(1)}, f32[504,128]{1,0:T(8,128)S(1)}, u32[]{:S(2)}, u32[]{:S(2)}) collective-permute-start(f32[504,128]{1,0:T(8,128)S(1)} %get-tuple-element.25), channel_id=1, source_target_pairs={{0,28},{1,0},{2,1},{3,2},{4,8},{5,9},{6,10},{7,11},{8,4},{9,5},{10... | collective-permute-start | bytes 774152 | tf_op jit(solution)/shard_map/ppermute | solution.py:49
  6.2 8.1 %collective-permute-start.2 = (f32[504,128]{1,0:T(8,128)S(1)}, f32[504,128]{1,0:T(8,128)S(1)}, u32[]{:S(2)}, u32[]{:S(2)}) collective-permute-start(f32[504,128]{1,0:T(8,128)S(1)} %get-tuple-element.26), channel_id=1, source_target_pairs={{0,4},{1,5},{2,6},{3,7},{4,0},{5,1},{6,2},{7,3},{8,12},{9,13},{10,... | collective-permute-start | bytes 774152 | tf_op jit(solution)/shard_map/ppermute | solution.py:49
  6.2 4.0 %collective-permute-start.4 = (f32[56,128]{1,0:T(8,128)S(1)}, f32[56,128]{1,0:T(8,128)S(1)}, u32[]{:S(2)}, u32[]{:S(2)}) collective-permute-start(f32[56,128]{1,0:T(8,128)S(1)} %get-tuple-element.27), channel_id=1, source_target_pairs={{0,1},{1,0},{2,3},{3,2},{4,5},{5,4},{6,7},{7,6},{8,9},{9,8},{10,11... | collective-permute-start | bytes 86024 | tf_op jit(solution)/shard_map/ppermute | solution.py:49
  6.9 3.3 %collective-permute-start.3 = (f32[56,128]{1,0:T(8,128)S(1)}, f32[56,128]{1,0:T(8,128)S(1)}, u32[]{:S(2)}, u32[]{:S(2)}) collective-permute-start(f32[56,128]{1,0:T(8,128)S(1)} %get-tuple-element.27), channel_id=1, source_target_pairs={{0,4},{1,2},{2,1},{3,7},{4,0},{5,6},{6,5},{7,3},{8,12},{9,10},{10,... | collective-permute-start | bytes 86024 | tf_op jit(solution)/shard_map/ppermute | solution.py:49
  10.2 1.7 %collective-permute-start.6 = (f32[56,128]{1,0:T(8,128)S(1)}, f32[56,128]{1,0:T(8,128)S(1)}, u32[]{:S(2)}, u32[]{:S(2)}) collective-permute-start(f32[56,128]{1,0:T(8,128)S(1)} %combine.1.halo), channel_id=1, source_target_pairs={{0,4},{1,5},{2,6},{3,7},{4,0},{5,1},{6,2},{7,3},{8,12},{9,13},{10,... | collective-permute-start | bytes 86024 | tf_op jit(solution)/shard_map/ppermute | solution.py:49
  10.3 3.9 %collective-permute-start.5 = (f32[56,128]{1,0:T(8,128)S(1)}, f32[56,128]{1,0:T(8,128)S(1)}, u32[]{:S(2)}, u32[]{:S(2)}) collective-permute-start(f32[56,128]{1,0:T(8,128)S(1)} %combine.1.halo), channel_id=1, source_target_pairs={{0,28},{1,0},{2,1},{3,2},{4,8},{5,9},{6,10},{7,11},{8,4},{9,5},{10... | collective-permute-start | bytes 86024 | tf_op jit(solution)/shard_map/ppermute | solution.py:49
  14.3 1.2 %collective-permute-start.7 = (f32[8,128]{1,0:T(8,128)S(1)}, f32[8,128]{1,0:T(8,128)S(1)}, u32[]{:S(2)}, u32[]{:S(2)}) collective-permute-start(f32[8,128]{1,0:T(8,128)S(1)} %get-tuple-element.29), channel_id=1, source_target_pairs={{0,4},{1,5},{2,6},{3,7},{4,0},{5,1},{6,2},{7,3},{8,12},{9,13},{10,... | collective-permute-start | bytes 12296 | tf_op jit(solution)/shard_map/ppermute | solution.py:49
